TPU v7x, 32 devices: a whole 2x2x4 slice. The times are simulated.
32 devices in a mesh: seq: 8 (over z, y), head: 4 (over x, core).
Axes of the slice: x: 2, y: 2, z: 4, core: 2. Of those that a mesh axis runs over, the one named last changes fastest.
Arguments:
- queries: bfloat16 [4096, 8192], P('seq', 'head'), may hold values from -6 to 6
- keys: bfloat16 [4096, 8192], P('seq', 'head'), may hold values from -0.52734375 to 0.52734375
- values: bfloat16 [4096, 8192], P('seq', 'head'), may hold values from -6 to 6
- suffix_keys: bfloat16 [32, 128, 8192], P('seq', None, 'head'), may hold values from -0.52734375 to 0.52734375
- suffix_values: bfloat16 [32, 128, 8192], P('seq', None, 'head'), may hold values from -6 to 6
- suffix_lengths: int32 [32], P('seq'), may hold values from 1 to 128
- step_queries: bfloat16 [2, 32, 8192], P(None, 'seq', 'head'), may hold values from -6 to 6
- step_keys: bfloat16 [2, 32, 8192], P(None, 'seq', 'head'), may hold values from -0.52734375 to 0.52734375
- step_values: bfloat16 [2, 32, 8192], P(None, 'seq', 'head'), may hold values from -6 to 6
- norm_gain: float32 [8192], P('head'), may hold values from 0.1 to 1.9
Outputs:
- prompt_out: bfloat16 [4096, 8192], P('seq', 'head')
- decoded: bfloat16 [2, 32, 8192], P(None, 'seq', 'head')
All inputs are finite; a program needn't handle non-finite values.
Results may differ from a plain program's by a relative error of at most 0.005.
Values sent between devices are 32-bit elements; how exact they have to be, the bound alone decides.
No kernel may reach another device: no remote copies, remote signals or barrier semaphores. Data moves between devices by JAX's collectives and lax.ppermute only.
A program may use at most 128 MiB of HBM per device.

v0:
```python
import jax
import jax.numpy as jnp
from jax import lax
from jax.sharding import PartitionSpec as P

HEAD_DIM = 128


HIGHEST_PREC = lax.Precision.HIGHEST


def entering(part, axis, combine, identity):
    place = lax.axis_index(axis)
    gathered = lax.all_gather(part, axis)
    state = jnp.zeros_like(part) + jnp.asarray(identity, part.dtype)

    def one(hop, state):
        return combine(state, lax.dynamic_index_in_dim(gathered, hop, 0, False))

    return lax.fori_loop(0, place, one, state)


def add_states(earlier, later):
    return earlier + later


def on_device(
    queries,
    keys,
    values,
    suffix_keys,
    suffix_values,
    suffix_lengths,
    step_queries,
    step_keys,
    step_values,
    norm_gain,
):
    rows_here = queries.shape[0]
    heads_here = queries.shape[1] // HEAD_DIM
    block_queries = queries.reshape(rows_here, heads_here, HEAD_DIM)
    block_keys = keys.reshape(rows_here, heads_here, HEAD_DIM)
    block_values = values.reshape(rows_here, heads_here, HEAD_DIM)
    own_state = jnp.einsum(
        "chd,che->hde", block_keys, block_values, preferred_element_type=jnp.float32
    )
    prior = entering(own_state, "seq", add_states, jnp.zeros_like(own_state))
    final = lax.psum(own_state, "seq")
    positions = lax.iota(jnp.int32, rows_here)
    causal = positions[None, :] <= positions[:, None]
    scores = jnp.einsum(
        "chd,shd->hcs", block_queries, block_keys, preferred_element_type=jnp.float32
    )
    scores = jnp.where(causal[None], scores, 0.0).astype(jnp.bfloat16)
    intra = jnp.einsum("hcs,she->che", scores, block_values, preferred_element_type=jnp.float32)
    inter = jnp.einsum(
        "chd,hde->che",
        block_queries,
        prior.astype(jnp.bfloat16),
        preferred_element_type=jnp.float32,
    )
    attended = (intra + inter).reshape(rows_here, heads_here * HEAD_DIM)
    total_sq = lax.psum(jnp.sum(attended * attended, axis=1), "head")
    width_all = heads_here * HEAD_DIM * lax.axis_size("head")
    scale_rows = lax.rsqrt(total_sq / width_all + 1e-06)
    prompt_out = (attended * scale_rows[:, None] * norm_gain).astype(jnp.bfloat16)
    samples_here = suffix_keys.shape[0]
    suffix_len = suffix_keys.shape[1]
    live = (lax.iota(jnp.int32, suffix_len)[None, :] < suffix_lengths[:, None]).astype(jnp.bfloat16)
    masked_keys = (suffix_keys * live[:, :, None]).reshape(
        samples_here, suffix_len, heads_here, HEAD_DIM
    )
    suffix_vals = suffix_values.reshape(samples_here, suffix_len, heads_here, HEAD_DIM)
    state = final[None] + jnp.einsum(
        "bjhd,bjhe->bhde", masked_keys, suffix_vals, preferred_element_type=jnp.float32
    )
    outputs = []
    for step in range(step_queries.shape[0]):
        new_keys = step_keys[step].reshape(samples_here, heads_here, HEAD_DIM)
        new_vals = step_values[step].reshape(samples_here, heads_here, HEAD_DIM)
        new_query = (
            step_queries[step].reshape(samples_here, heads_here, HEAD_DIM).astype(jnp.float32)
        )
        state = state + jnp.einsum(
            "bhd,bhe->bhde", new_keys, new_vals, preferred_element_type=jnp.float32
        )
        raw = jnp.einsum("bhd,bhde->bhe", new_query, state, precision=HIGHEST_PREC)
        outputs.append(raw.reshape(samples_here, heads_here * HEAD_DIM))
    stacked = jnp.stack(outputs)
    step_sq = lax.psum(jnp.sum(stacked * stacked, axis=2), "head")
    scale_steps = lax.rsqrt(step_sq / width_all + 1e-06)
    decoded = (stacked * scale_steps[:, :, None] * norm_gain).astype(jnp.bfloat16)
    return (prompt_out, decoded)


def solution(mesh):
    return jax.shard_map(
        on_device,
        mesh=mesh,
        in_specs=(
            P("seq", "head"),
            P("seq", "head"),
            P("seq", "head"),
            P("seq", None, "head"),
            P("seq", None, "head"),
            P("seq"),
            P(None, "seq", "head"),
            P(None, "seq", "head"),
            P(None, "seq", "head"),
            P("head"),
        ),
        out_specs=(P("seq", "head"), P(None, "seq", "head")),
        check_vma=False,
    )
```

profile of v0, /device:TPU:0, one launch (start us, length us, event | category | flops | bytes accessed | tf_op | source)
XLA Modules:
  0.0 251.3 jit_solution(12130280192778950017)
XLA Ops:
  7.2 0.0 copy-start
  7.2 0.0 all-gather.3.cloned.1.call-start
  7.2 4.1 %copy.33 = bf16[512,2048]{0,1:T(8,128)(2,1)} copy(bf16[512,2048]{1,0:T(8,128)(2,1)} %param.13) | data formatting | bytes 4194304 | tf_op jit(solution)/shard_map/reshape | solution.py:42
  11.3 3.9 %fusion.9 = f32[16,128,128]{2,1,0:T(8,128)} fusion(bf16[512,16,128]{0,2,1:T(8,128)(2,1)} %bitcast.77, bf16[512,2048]{1,0:T(8,128)(2,1)} %param.14), kind=kOutput, calls=%fused_computation.15 | convolution fusion | flops 268435456 | bytes 5242880 | tf_op jit(solution)/shard_map/chd,che->hde/dot_general | solution.py:44
  15.2 0.0 all-gather.3.cloned.1.call-update
  15.3 0.0 copy-done.5
  15.3 0.0 copy-done.6
  15.3 0.1 fusion.28
  15.4 3.2 %broadcast_multiply_fusion = bf16[4,128,2048]{2,1,0:T(8,128)(2,1)} fusion(bf16[4,128,2048]{2,1,0:T(8,128)(2,1)} %param.15, bf16[4,128]{1,0:T(4,128)(2,1)S(1)} %fusion.28), kind=kLoop, calls=%fused_computation.31 | loop fusion | flops 1048576 | bytes 4195328 | tf_op jit(solution)/shard_map/mul | solution.py:70
  18.6 4.0 %copy.34 = bf16[4,128,2048]{1,2,0:T(8,128)(2,1)} copy(bf16[4,128,2048]{2,1,0:T(8,128)(2,1)} %broadcast_multiply_fusion) | data formatting | bytes 4194304 | tf_op jit(solution)/shard_map/reshape | solution.py:70
  22.6 0.1 iota_compare_fusion
  22.6 0.0 copy-done.3
  22.7 0.0 copy-done.4
  22.7 4.9 %fusion.5 = f32[4,16,128,128]{3,2,1,0:T(8,128)} fusion(bf16[4,128,16,128]{1,3,2,0:T(8,128)(2,1)} %bitcast.79, bf16[4,128,2048]{2,1,0:T(8,128)(2,1)} %param.16), kind=kOutput, calls=%fused_computation.11 | convolution fusion | flops 268435456 | bytes 8388608 | tf_op jit(solution)/shard_map/bjhd,bjhe->bhde/dot_general | solution.py:74
  27.6 0.0 copy-done
  27.6 9.4 %fusion.4 = f32[16,512,128]{1,2,0:T(8,128)} fusion(bf16[512,16,128]{0,2,1:T(8,128)(2,1)} %bitcast.78, pred[512,512]{1,0:T(8,128)(4,1)S(1)} %iota_compare_fusion, bf16[512,2048]{1,0:T(8,128)(2,1)} %param.14, bf16[512,2048]{1,0:T(8,128)(2,1)S(1)} %copy-done), kind=kOutput, calls=%fused_computation.10 | convolution fusion | flops 2155872256 | bytes 10747904 | tf_op jit(solution)/shard_map/hcs,she->che/dot_general | solution.py:55
  37.0 106.1 %all-gather.3.cloned.1.call-done = f32[128,128,128]{2,1,0:T(8,128)} async-done(((f32[16,128,128]{2,1,0:T(8,128)}), f32[128,128,128]{2,1,0:T(8,128)}) %all-gather.3.cloned.1.call-update) | async-done | bytes 8388624 | tf_op jit(solution)/shard_map/all_gather | solution.py:14
  143.0 0.0 all-reduce.3.cloned.1.call-start
  143.0 0.7 all-reduce.3.cloned.1.call-update
  143.8 0.1 broadcast_in_dim.16
  143.9 5.0 %multiply_reduce_fusion = (f32[512]{0:T(512)S(1)}, f32[512,16,128]{0,2,1:T(8,128)}) fusion(f32[16,128,128]{2,1,0:T(8,128)S(1)} %get-tuple-element.25, f32[16,512,128]{1,2,0:T(8,128)} %fusion.4, bf16[512,2048]{1,0:T(8,128)(2,1)S(1)} %copy-done), kind=kOutput, calls=%fused_computation.8 | convolution fusion | flops 271842816 | bytes 11536384 | tf_op jit(solution)/shard_map/chd,hde->che/dot_general | solution.py:56
  148.9 5.5 %copy.25 = f32[512,2048]{1,0:T(8,128)} copy(f32[512,2048]{0,1:T(8,128)} %bitcast.76) | data formatting | bytes 8388608 | tf_op jit(solution)/shard_map/reshape | solution.py:62
  154.4 69.3 %all-reduce.3.cloned.1.call-done = f32[16,128,128]{2,1,0:T(8,128)} async-done(((f32[16,128,128]{2,1,0:T(8,128)}), f32[16,128,128]{2,1,0:T(8,128)}) %all-reduce.3.cloned.1.call-update) | async-done | bytes 1048592 | tf_op jit(solution)/shard_map/psum | solution.py:48
  223.7 4.8 %fusion.3 = f32[4,16,1,128]{3,2,1,0:T(1,128)S(1)} fusion(bf16[4,16,128,1]{2,3,1,0:T(2,128)(2,1)S(1)} %reshape.97, f32[4,16,128,128]{3,2,1,0:T(8,128)} %fusion.5, f32[4,16,128]{2,1,0:T(8,128)S(1)} %get-tuple-element.45, f32[4,16,128]{2,1,0:T(8,128)S(1)} %get-tuple-element.47, f32[16,128,128]{2,1,0:T(8,128)} %all-reduce.3.cloned.1.call-done), kind=kOutput, calls=%fused_computation.9 | convolution fusion | flops 15728640 | bytes 5357568 | tf_op jit(solution)/shard_map/bhd,bhde->bhe/dot_general | solution.py:87
  228.6 0.0 copy-done.1
  228.6 0.0 copy-start.2
  228.6 5.2 %fusion = f32[4,16,1,128]{3,2,1,0:T(1,128)S(1)} fusion(bf16[4,16,128,1]{2,3,1,0:T(2,128)(2,1)S(1)} %reshape.99, f32[4,16,128,128]{3,2,1,0:T(8,128)} %fusion.5, f32[4,16,128]{2,1,0:T(8,128)S(1)} %get-tuple-element.44, f32[4,16,128]{2,1,0:T(8,128)S(1)} %get-tuple-element.46, f32[4,16,128]{2,1,0:T(8,128)S(1)} %get-tuple-element.45, ...), kind=kOutput, calls=%fused_computation.3 | convolution fusion | flops 17825792 | bytes 5423104 | tf_op jit(solution)/shard_map/bhd,bhde->bhe/dot_general | solution.py:87
  233.9 0.1 multiply_reduce_fusion.1
  234.0 5.8 %all-reduce = (f32[512]{0:T(512)S(1)}, f32[2,4]{1,0:T(2,128)S(1)}) all-reduce(f32[512]{0:T(512)S(1)} %get-tuple-element.42, f32[2,4]{1,0:T(2,128)S(1)} %multiply_reduce_fusion.1), channel_id=1, replica_groups=mesh['seq'=8,'head'=4] {'head'}, use_global_device_ids=true, to_apply=%region_3.4 | all-reduce | flops 520 | bytes 4160 | tf_op jit(solution)/shard_map/psum | solution.py:63
  239.8 0.0 copy-done.2
  239.8 0.7 multiply_convert_fusion.1
  240.5 3.9 %multiply_convert_fusion = bf16[512,2048]{1,0:T(8,128)(2,1)} fusion(f32[512,2048]{1,0:T(8,128)} %copy.25, f32[2048]{0:T(1024)S(1)} %copy-done.2, f32[512]{0:T(512)S(1)} %add_rsqrt_fusion), kind=kLoop, calls=%fused_computation.7 | loop fusion | flops 3145728 | bytes 6301696 | tf_op jit(solution)/shard_map/convert_element_type | solution.py:66
  (19 shorter events, 0.2 us)
Async XLA Ops:
  7.2 20.5 %copy-start = (bf16[512,2048]{1,0:T(8,128)(2,1)S(1)}, bf16[512,2048]{1,0:T(8,128)(2,1)}, u32[]{:S(2)}) copy-start(bf16[512,2048]{1,0:T(8,128)(2,1)} %param.12) | copy-start | bytes 6291460
  7.2 135.9 %all-gather.3.cloned.1.call-start = ((), (), s32[]{:S(2)}) async-start(), calls=%async_computation.1 | async-start | bytes 9437184 | tf_op jit(solution)/shard_map/all_gather | solution.py:14
  11.3 4.0 %copy-start.5 = (bf16[2,4,2048]{2,1,0:T(4,128)(2,1)S(1)}, bf16[2,4,2048]{2,1,0:T(4,128)(2,1)}, u32[]{:S(2)}) copy-start(bf16[2,4,2048]{2,1,0:T(4,128)(2,1)} %param.18) | copy-start | bytes 98308
  11.3 4.0 %copy-start.6 = (s32[4]{0:T(128)S(1)}, s32[4]{0:T(128)}, u32[]{:S(2)}) copy-start(s32[4]{0:T(128)} %param.17) | copy-start | bytes 52
  18.6 4.1 %copy-start.3 = (bf16[2,4,2048]{2,1,0:T(4,128)(2,1)S(1)}, bf16[2,4,2048]{2,1,0:T(4,128)(2,1)}, u32[]{:S(2)}) copy-start(bf16[2,4,2048]{2,1,0:T(4,128)(2,1)} %param.20) | copy-start | bytes 98308
  18.6 4.1 %copy-start.4 = (bf16[2,4,2048]{2,1,0:T(4,128)(2,1)S(1)}, bf16[2,4,2048]{2,1,0:T(4,128)(2,1)}, u32[]{:S(2)}) copy-start(bf16[2,4,2048]{2,1,0:T(4,128)(2,1)} %param.19) | copy-start | bytes 98308
  143.0 80.7 %all-reduce.3.cloned.1.call-start = ((), (), s32[]{:S(2)}) async-start(), calls=%async_computation | async-start | bytes 2097152 | tf_op jit(solution)/shard_map/psum | solution.py:48
  223.7 4.9 %copy-start.1 = (f32[16,128,128]{2,1,0:T(8,128)S(1)}, f32[16,128,128]{2,1,0:T(8,128)}, u32[]{:S(2)}) copy-start(f32[16,128,128]{2,1,0:T(8,128)} %all-reduce.3.cloned.1.call-done) | copy-start | bytes 3145732
  228.6 11.3 %copy-start.2 = (f32[2048]{0:T(1024)S(1)}, f32[2048]{0:T(1024)}, u32[]{:S(2)}) copy-start(f32[2048]{0:T(1024)} %param.21) | copy-start | bytes 24580
Sparse Core Ops, SparseCore 0:
  15.4 127.6 all-gather.2
  147.4 76.2 all-reduce.2
where the time goes:
time: 252 us; the launch traced here: 251 us
  waiting for transfers between devices  176 us (70%)
  matrix products  33.2 us (13%)
  between operations  14.2 us (6%)
  local copies, waits for them, and re-layouts  13.8 us (5%)
  other arithmetic  8.06 us (3%)
  blocking collectives  5.85 us (2%)
    all_gather x1, waiting for transfers between devices, entering(): gathered = lax.all_gather(part, axis)  106 us
    psum x1, waiting for transfers between devices, on_device(): final = lax.psum(own_state, 'seq')  69.3 us
    dot_general x2, matrix products, on_device(): raw = jnp.einsum('bhd,bhde->bhe', new_query, state, precision=HIGHEST_PREC)  10 us
    dot_general x1, matrix products, on_device(): jnp.einsum('hcs,she->che', scores, block_values, preferred_element_type=j...  9.35 us
    psum x1, blocking collectives, on_device(): total_sq = lax.psum(jnp.sum(attended * attended, axis=1), 'head')  5.85 us
    reshape x1, local copies, waits for them, and re-layouts, on_device(): attended = (intra + inter).reshape(rows_here, heads_here * HEAD_DIM)  5.48 us
  transfers between devices with their start and end apart: 2, of which 2 were waited for; matrix products, arithmetic and copies ran while one was open for 13% of the time, Pallas kernels for 0%

commit v1 on v0

v1 whole, which is shorter than its diff:
```python
import functools

import jax
import jax.numpy as jnp
from jax import lax
from jax.experimental import pallas as pl
from jax.experimental.pallas import tpu as pltpu
from jax.sharding import PartitionSpec as P

HEAD_DIM = 128
LANES = 128
CHUNKS = 2
F32 = jnp.float32
BF16 = jnp.bfloat16
VMEM_LIMIT = 48 * 1024 * 1024


def dot(a, b, contract=((1,), (0,))):
    return lax.dot_general(a, b, (contract, ((), ())), preferred_element_type=F32)


def params(semantics=None):
    return pltpu.CompilerParams(vmem_limit_bytes=VMEM_LIMIT, dimension_semantics=semantics)


def cost(flops, moved):
    return pl.CostEstimate(flops=int(flops), bytes_accessed=int(moved), transcendentals=0)


def head_cols(head):
    return slice(head * HEAD_DIM, (head + 1) * HEAD_DIM)


def flat_rows(ref):
    return jnp.concatenate([ref[i].astype(F32) for i in range(ref.shape[0])], axis=0)


def state_kernel(group, place_ref, k_ref, v_ref, q_ref, *out_refs):
    heads = out_refs[0].shape[0]
    turn = pl.program_id(0)
    for m in range(group):

        @pl.when(turn == m)
        def _():
            rows = flat_rows(q_ref)
            for h in range(heads):
                cols = head_cols(h)
                out_refs[m][h, :HEAD_DIM, :] = dot(k_ref[:, cols], v_ref[:, cols], ((0,), (0,)))
                out_refs[m][h, HEAD_DIM:, :] = rows[:, cols]


def block_states(chunk, group, heads, place, keys, values, step_queries):
    rows = keys.shape[0]
    steps, samples, _ = step_queries.shape
    wide = heads * HEAD_DIM
    taken = lambda m, place: (0, chunk * group + (place[0] ^ m))
    message = (heads, HEAD_DIM + steps * samples, HEAD_DIM)
    return pl.pallas_call(
        functools.partial(state_kernel, group),
        grid_spec=pltpu.PrefetchScalarGridSpec(
            num_scalar_prefetch=1,
            grid=(group,),
            in_specs=[
                pl.BlockSpec((rows, wide), taken),
                pl.BlockSpec((rows, wide), taken),
                pl.BlockSpec(
                    (steps, samples, wide), lambda m, place: (0, 0, chunk * group + (place[0] ^ m))
                ),
            ],
            out_specs=[pl.BlockSpec(message, lambda m, place: (0, 0, 0))] * group,
        ),
        out_shape=[jax.ShapeDtypeStruct(message, F32)] * group,
        compiler_params=params(("arbitrary",)),
        cost_estimate=cost(2 * rows * wide * HEAD_DIM * group, 4 * rows * wide * group),
        name="block_states",
    )(place, keys, values, step_queries)


def total_kernel(*refs):
    *parts, out_ref = refs
    total = parts[0][:, :HEAD_DIM, :]
    for part in parts[1:]:
        total = total + part[:, :HEAD_DIM, :]
    out_ref[...] = total


def group_total(parts):
    heads = parts[0].shape[0]
    shape = (heads, HEAD_DIM, HEAD_DIM)
    return pl.pallas_call(
        total_kernel,
        out_shape=jax.ShapeDtypeStruct(shape, F32),
        compiler_params=params(),
        cost_estimate=cost(0, 4 * heads * HEAD_DIM * HEAD_DIM * (len(parts) + 1)),
        name="group_total",
    )(*parts)


def prior_kernel(group, others, place_ref, *refs):
    parts, total_ref = refs[:group], refs[group]
    other_refs, out_refs = refs[group + 1 : group + 1 + others], refs[group + 1 + others :]
    place, block = place_ref[0], place_ref[1]
    heads = parts[0].shape[0]
    for h in range(heads):
        entering = jnp.zeros((HEAD_DIM, HEAD_DIM), F32)
        final = total_ref[h]
        for k in range(others):
            other = other_refs[k][h]
            entering = entering + jnp.where(block > k, other, 0.0)
            final = final + other
        high = final.astype(BF16)
        low = (final - high.astype(F32)).astype(BF16)
        for m in range(group):
            prior = entering
            for k in range(group):
                if k != m:
                    prior = prior + jnp.where(
                        (place ^ k) < (place ^ m), parts[k][h, :HEAD_DIM, :], 0.0
                    )
            out_refs[m][h, :HEAD_DIM, :] = prior
            query = parts[m][h, HEAD_DIM:, :].astype(BF16)
            out_refs[m][h, HEAD_DIM:, :] = dot(query, high) + dot(query, low)


def priors(place, parts, total, others):
    group = len(parts)
    smem = pl.BlockSpec(memory_space=pltpu.SMEM)
    vmem = pl.BlockSpec(memory_space=pltpu.VMEM)
    return pl.pallas_call(
        functools.partial(prior_kernel, group, len(others)),
        in_specs=[smem] + [vmem] * (group + 1 + len(others)),
        out_specs=[vmem] * group,
        out_shape=[jax.ShapeDtypeStruct(parts[0].shape, F32)] * group,
        compiler_params=params(),
        cost_estimate=cost(0, 4 * parts[0].size * (2 * group + 1 + len(others))),
        name="priors",
    )(place, *parts, total, *others)


def intra_kernel(tile, q_ref, k_ref, v_ref, out_ref):
    rows, wide = q_ref.shape
    keep = lax.broadcasted_iota(jnp.int32, (tile, tile), 0) >= lax.broadcasted_iota(
        jnp.int32, (tile, tile), 1
    )
    for h in range(wide // HEAD_DIM):
        cols = head_cols(h)
        for i in range(rows // tile):
            here = slice(i * tile, (i + 1) * tile)
            query = q_ref[here, cols]
            scores = dot(query, k_ref[here, cols], ((1,), (1,)))
            scores = jnp.where(keep, scores, 0.0).astype(BF16)
            total = dot(scores, v_ref[here, cols])
            if i:
                before = slice(0, i * tile)
                scores = dot(query, k_ref[before, cols], ((1,), (1,))).astype(BF16)
                total = total + dot(scores, v_ref[before, cols])
            out_ref[here, cols] = total


def intra_block(chunk, wide, queries, keys, values):
    rows = queries.shape[0]
    tile = 256 if rows % 256 == 0 else rows
    step = 2 * HEAD_DIM if wide % (2 * HEAD_DIM) == 0 else HEAD_DIM
    turns = wide // step
    spec = pl.BlockSpec((rows, step), lambda t: (0, chunk * turns + t))
    return pl.pallas_call(
        functools.partial(intra_kernel, tile),
        grid=(turns,),
        in_specs=[spec] * 3,
        out_specs=pl.BlockSpec((rows, step), lambda t: (0, t)),
        out_shape=jax.ShapeDtypeStruct((rows, wide), F32),
        compiler_params=params(("arbitrary",)),
        cost_estimate=cost(4 * rows * rows * wide, 10 * rows * wide),
        name="intra_block",
    )(queries, keys, values)


def suffix_kernel(lengths_ref, q_ref, k_ref, v_ref, sk_ref, sv_ref, out_ref):
    samples, suffix, wide = k_ref.shape
    steps = q_ref.shape[0]
    rows = steps * samples
    queries = flat_rows(q_ref).astype(BF16)
    step_keys = flat_rows(sk_ref).astype(BF16)
    step_values = flat_rows(sv_ref).astype(BF16)
    row = lax.broadcasted_iota(jnp.int32, (rows, samples * suffix), 0)
    col = lax.broadcasted_iota(jnp.int32, (rows, samples * suffix), 1)
    live = jnp.zeros((rows, samples * suffix), jnp.bool_)
    for n in range(samples):
        mine = (col >= n * suffix) & (col < n * suffix + lengths_ref[n]) & (row % samples == n)
        live = live | mine
    row = lax.broadcasted_iota(jnp.int32, (rows, rows), 0)
    col = lax.broadcasted_iota(jnp.int32, (rows, rows), 1)
    near = (row % samples == col % samples) & (row // samples >= col // samples)

    def weighted(scores, mask, values):
        scores = jnp.where(mask, scores, 0.0)
        high = scores.astype(BF16)
        low = (scores - high.astype(F32)).astype(BF16)
        return dot(high, values) + dot(low, values)

    for h in range(wide // HEAD_DIM):
        cols = head_cols(h)
        query = queries[:, cols]
        keys = k_ref[:, :, cols].reshape(samples * suffix, HEAD_DIM)
        values = v_ref[:, :, cols].reshape(samples * suffix, HEAD_DIM)
        out_ref[:, cols] = weighted(dot(query, keys, ((1,), (1,))), live, values) + weighted(
            dot(query, step_keys[:, cols], ((1,), (1,))), near, step_values[:, cols]
        )


def suffix_part(lengths, step_queries, suffix_keys, suffix_values, step_keys, step_values):
    samples, suffix, width = suffix_keys.shape
    steps = step_queries.shape[0]
    step = 2 * HEAD_DIM if width % (2 * HEAD_DIM) == 0 else HEAD_DIM
    small = pl.BlockSpec((steps, samples, step), lambda t: (0, 0, t))
    large = pl.BlockSpec((samples, suffix, step), lambda t: (0, 0, t))
    return pl.pallas_call(
        suffix_kernel,
        grid=(width // step,),
        in_specs=[pl.BlockSpec(memory_space=pltpu.SMEM), small, large, large, small, small],
        out_specs=pl.BlockSpec((steps * samples, step), lambda t: (0, t)),
        out_shape=jax.ShapeDtypeStruct((steps * samples, width), F32),
        compiler_params=params(("arbitrary",)),
        cost_estimate=cost(64 * samples * suffix * width, 4 * samples * suffix * width),
        name="suffix_part",
    )(lengths, step_queries, suffix_keys, suffix_values, step_keys, step_values)


def attended_kernel(group, first, last, place_ref, q_ref, intra_ref, extra_ref, *refs):
    parts = refs[:group]
    if first:
        before_ref, (att_ref, raw_ref, sum_ref, acc_ref) = None, refs[group:]
    else:
        before_ref, att_ref, raw_ref, sum_ref, acc_ref = refs[group:]
    rows = q_ref.shape[0]
    heads = parts[0].shape[0]
    dec = extra_ref.shape[0]
    turn = pl.program_id(0)

    @pl.when(turn == 0)
    def _():
        if first:
            acc_ref[...] = jnp.zeros_like(acc_ref)
        else:
            acc_ref[...] = before_ref[...]

    for m in range(group):

        @pl.when(turn == m)
        def _():
            squares = acc_ref[:rows, :]
            raw_squares = acc_ref[rows : rows + dec, :]
            for h in range(heads):
                cols = head_cols(h)
                prior = parts[m][h, :HEAD_DIM, :].astype(BF16)
                att = intra_ref[:, cols] + dot(q_ref[:, cols], prior)
                att_ref[:, cols] = att
                squares = squares + att * att
                raw = parts[m][h, HEAD_DIM:, :] + extra_ref[:, cols]
                raw_ref[:, cols] = raw
                raw_squares = raw_squares + raw * raw
            acc_ref[:rows, :] = squares
            acc_ref[rows : rows + dec, :] = raw_squares

    @pl.when(turn == group - 1)
    def _():
        if last:
            sum_ref[...] = jnp.sum(acc_ref[...].T, axis=0, keepdims=True)
        else:
            sum_ref[...] = acc_ref[...]


def padded_rows(rows, dec):
    return -(-(rows + dec) // LANES) * LANES


def attend(chunk, last, place, queries, intra, extra, parts, before):
    group = len(parts)
    heads = parts[0].shape[0]
    wide = heads * HEAD_DIM
    rows, dec = queries.shape[0], extra.shape[0]
    padded = padded_rows(rows, dec)
    whole = lambda m, place: (0, chunk * group + (place[0] ^ m))
    own = lambda m, place: (0, place[0] ^ m)
    fixed = lambda m, place: (0, 0)
    sums = (1, padded) if last else (padded, LANES)
    first = before is None
    return pl.pallas_call(
        functools.partial(attended_kernel, group, first, last),
        grid_spec=pltpu.PrefetchScalarGridSpec(
            num_scalar_prefetch=1,
            grid=(group,),
            in_specs=[
                pl.BlockSpec((rows, wide), whole),
                pl.BlockSpec((rows, wide), own),
                pl.BlockSpec((dec, wide), whole),
            ]
            + [pl.BlockSpec(parts[0].shape, lambda m, place: (0, 0, 0))] * group
            + ([] if first else [pl.BlockSpec((padded, LANES), fixed)]),
            out_specs=[
                pl.BlockSpec((rows, wide), own),
                pl.BlockSpec((dec, wide), own),
                pl.BlockSpec(sums, fixed),
            ],
            scratch_shapes=[pltpu.VMEM((padded, LANES), F32)],
        ),
        out_shape=[
            jax.ShapeDtypeStruct((rows, wide * group), F32),
            jax.ShapeDtypeStruct((dec, wide * group), F32),
            jax.ShapeDtypeStruct(sums, F32),
        ],
        compiler_params=params(("arbitrary",)),
        cost_estimate=cost(2 * rows * wide * group * HEAD_DIM, 10 * rows * wide * group),
        name="attend",
    )(place, queries, intra, extra, *parts, *([] if first else [before]))


def norm_kernel(chunks, sums, width, gain_ref, *refs):
    sum_refs = refs[:sums]
    att_refs = refs[sums : sums + chunks]
    raw_refs = refs[sums + chunks : sums + 2 * chunks]
    out_ref, dec_ref, scale_ref = refs[sums + 2 * chunks :]
    tile = out_ref.shape[0]
    dec = raw_refs[0].shape[0]
    rows = tile * pl.num_programs(0)
    turn = pl.program_id(0)
    wide = att_refs[0].shape[1]

    @pl.when(turn == 0)
    def _():
        total = sum_refs[0][...]
        for ref in sum_refs[1:]:
            total = total + ref[...]
        scale = lax.rsqrt(total / width + 1e-06)
        scale_ref[...] = jnp.broadcast_to(scale, (LANES, scale.shape[1])).T
        samples = dec_ref.shape[1]
        here = scale_ref[pl.ds(tile * pl.num_programs(0), dec), :]
        for c in range(chunks):
            for h in range(wide // HEAD_DIM):
                cols = head_cols(h)
                at = slice(c * wide + h * HEAD_DIM, c * wide + (h + 1) * HEAD_DIM)
                out = raw_refs[c][:, cols] * here * gain_ref[:, at]
                for i in range(dec_ref.shape[0]):
                    dec_ref[i, :, at] = out[i * samples : (i + 1) * samples].astype(BF16)

    here = scale_ref[pl.ds(pl.multiple_of(turn * tile, tile), tile), :]
    for c in range(chunks):
        for h in range(wide // HEAD_DIM):
            cols = head_cols(h)
            at = slice(c * wide + h * HEAD_DIM, c * wide + (h + 1) * HEAD_DIM)
            out_ref[:, at] = (att_refs[c][:, cols] * here * gain_ref[:, at]).astype(BF16)


def normalize(atts, raws, sums, gain, steps, width_all):
    rows, wide = atts[0].shape
    width = wide * len(atts)
    dec = raws[0].shape[0]
    tile = 128 if rows % 128 == 0 else rows
    fixed = lambda t: (0, 0)
    return pl.pallas_call(
        functools.partial(norm_kernel, len(atts), len(sums), width_all),
        grid=(rows // tile,),
        in_specs=[pl.BlockSpec((1, width), fixed)]
        + [pl.BlockSpec(sums[0].shape, fixed)] * len(sums)
        + [pl.BlockSpec((tile, wide), lambda t: (t, 0))] * len(atts)
        + [pl.BlockSpec((dec, wide), fixed)] * len(raws),
        out_specs=[
            pl.BlockSpec((tile, width), lambda t: (t, 0)),
            pl.BlockSpec((steps, dec // steps, width), lambda t: (0, 0, 0)),
        ],
        out_shape=[
            jax.ShapeDtypeStruct((rows, width), BF16),
            jax.ShapeDtypeStruct((steps, dec // steps, width), BF16),
        ],
        scratch_shapes=[pltpu.VMEM((sums[0].shape[1], LANES), F32)],
        compiler_params=params(("arbitrary",)),
        cost_estimate=cost(0, 6 * rows * width),
        name="normalize",
    )(gain[None, :], *sums, *atts, *raws)


def group_size(devices, heads):
    size = 1
    while (
        devices % (2 * size) == 0
        and size * size < devices
        and heads % (2 * size * CHUNKS) == 0
    ):
        size *= 2
    return size


def on_device(
    queries,
    keys,
    values,
    suffix_keys,
    suffix_values,
    suffix_lengths,
    step_queries,
    step_keys,
    step_values,
    norm_gain,
):
    width = queries.shape[1]
    heads_here = width // HEAD_DIM
    devices = lax.axis_size("seq")
    group = group_size(devices, heads_here)
    blocks = devices // group
    heads = heads_here // (group * CHUNKS)
    rank = lax.axis_index("seq")
    place = jnp.stack([rank % group, rank // group]).astype(jnp.int32)

    def swap(m):
        return [(i, i // group * group + (i % group ^ m)) for i in range(devices)]

    def exchange(messages):
        return [messages[0]] + [
            lax.ppermute(messages[m], "seq", swap(m)) for m in range(1, group)
        ]

    chunks = range(CHUNKS)
    parts = [
        exchange(block_states(c, group, heads, place, keys, values, step_queries)) for c in chunks
    ]
    totals = [group_total(parts[c]) for c in chunks]
    others = [
        [
            lax.ppermute(
                totals[c], "seq", [(i, (i + k * group) % devices) for i in range(devices)]
            )
            for k in range(1, blocks)
        ]
        for c in chunks
    ]
    entering = [exchange(priors(place, parts[c], totals[c], others[c])) for c in chunks]
    intra = [intra_block(c, width // CHUNKS, queries, keys, values) for c in chunks]
    extra = suffix_part(
        suffix_lengths, step_queries, suffix_keys, suffix_values, step_keys, step_values
    )
    atts, raws, sums = [], [], None
    for c in chunks:
        att, raw, sums = attend(
            c, c == CHUNKS - 1, place, queries, intra[c], extra, entering[c], sums
        )
        atts.append(att)
        raws.append(raw)
    others_of_row = lax.axis_size("head")
    all_sums = [sums] + [
        lax.ppermute(
            sums, "head", [(i, (i + k) % others_of_row) for i in range(others_of_row)]
        )
        for k in range(1, others_of_row)
    ]
    return tuple(
        normalize(
            atts, raws, all_sums, norm_gain, step_queries.shape[0], width * others_of_row
        )
    )


def solution(mesh):
    return jax.shard_map(
        on_device,
        mesh=mesh,
        in_specs=(
            P("seq", "head"),
            P("seq", "head"),
            P("seq", "head"),
            P("seq", None, "head"),
            P("seq", None, "head"),
            P("seq"),
            P(None, "seq", "head"),
            P(None, "seq", "head"),
            P(None, "seq", "head"),
            P("head"),
        ),
        out_specs=(P("seq", "head"), P(None, "seq", "head")),
        check_vma=False,
    )
```

time: 252 us -> 73.8 us (0.29)
  waiting for transfers between devices: 176 us -> 10.7 us
  matrix products: 33.2 us -> 0 us
  Pallas kernels: 0 us -> 32.6 us
  starting transfers between devices: 0.04 us -> 23.8 us
  between operations: 14.2 us -> 0.86 us
  local copies, waits for them, and re-layouts: 13.8 us -> 5.33 us
  other arithmetic: 8.06 us -> 0.08 us
  blocking collectives: 5.85 us -> 0 us
    all_gather x1 -> x0, waiting for transfers between devices: 106 us -> none  [entering(): gathered = lax.all_gather(part, axis)]
    psum x1 -> x0, waiting for transfers between devices: 69.3 us -> none  [on_device(): final = lax.psum(own_state, 'seq')]
    dot_general x6 -> x0, matrix products: 33.2 us -> none  [the longest x2 10 us: on_device(): raw = jnp.einsum('bhd,bhde->bhe', new_query, state, precision=HIGHEST_PREC)]
    pallas_call x0 -> x12, Pallas kernels: none -> 32.6 us  [the longest x2 10 us: intra_block(): pl.pallas_call(functools.partial(intra_kernel, tile), grid=(turns,), in_s...]
    ppermute x0 -> x17, starting transfers between devices: none -> 23.8 us  [the longest x12 16.9 us: exchange(): lax.ppermute(messages[m], 'seq', swap(m))]
    reshape x3 -> x0, local copies, waits for them, and re-layouts: 13.5 us -> none  [the longest x1 5.48 us: on_device(): attended = (intra + inter).reshape(rows_here, heads_here * HEAD_DIM)]
    ppermute x0 -> x17, waiting for transfers between devices: none -> 10.7 us  [the longest x2 6.08 us: on_device(): lax.ppermute(totals[c], 'seq', [(i, (i + k * group) % devices) for i in r...]
    psum x1 -> x0, blocking collectives: 5.85 us -> none  [on_device(): total_sq = lax.psum(jnp.sum(attended * attended, axis=1), 'head')]
  transfers between devices with their start and end apart: 2 -> 17, of which waited for: 2 -> 5; matrix products, arithmetic and copies ran while one was open for 13% -> 0% of each run, Pallas kernels for 0% -> 33%
where the time goes in v1:
time: 73.8 us; the launch traced here: 73.4 us
  Pallas kernels  32.6 us (44%)
  starting transfers between devices  23.8 us (32%)
  waiting for transfers between devices  10.7 us (14%)
  local copies, waits for them, and re-layouts  5.33 us (7%)
  between operations  0.86 us (1%)
    ppermute x12, starting transfers between devices, exchange(): lax.ppermute(messages[m], 'seq', swap(m))  16.9 us
    pallas_call x2, Pallas kernels, intra_block(): pl.pallas_call(functools.partial(intra_kernel, tile), grid=(turns,), in_s...  10 us
    pallas_call x2, Pallas kernels, attend(): pl.pallas_call(functools.partial(attended_kernel, group, first, last), gr...  7.55 us
    pallas_call x1, Pallas kernels, suffix_part(): pl.pallas_call(suffix_kernel, grid=(width // step,), in_specs=[pl.BlockSp...  6.8 us
    ppermute x2, waiting for transfers between devices, on_device(): lax.ppermute(totals[c], 'seq', [(i, (i + k * group) % devices) for i in r...  6.08 us
    unnamed x24, local copies, waits for them, and re-layouts  5.33 us
    ppermute x2, starting transfers between devices, on_device(): lax.ppermute(totals[c], 'seq', [(i, (i + k * group) % devices) for i in r...  5.12 us
    pallas_call x2, Pallas kernels, block_states(): pl.pallas_call(functools.partial(state_kernel, group), grid_spec=pltpu.Pr...  4.25 us
  transfers between devices with their start and end apart: 17, of which 5 were waited for; matrix products, arithmetic and copies ran while one was open for 0% of the time, Pallas kernels for 33%

profile of v1, /device:TPU:0, one launch (start us, length us, event | category | flops | bytes accessed | tf_op | source)
XLA Modules:
  0.0 73.4 jit_solution(17354038129210478858)
XLA Ops:
  0.7 1.6 %copy-done = bf16[512,2048]{1,0:T(8,128)(2,1)S(1)} copy-done((bf16[512,2048]{1,0:T(8,128)(2,1)S(1)}, bf16[512,2048]{1,0:T(8,128)(2,1)}, u32[]{:S(2)}) %copy-start) | copy-done | bytes 2097176
  2.3 1.6 %copy-done.1 = bf16[512,2048]{1,0:T(8,128)(2,1)S(1)} copy-done((bf16[512,2048]{1,0:T(8,128)(2,1)S(1)}, bf16[512,2048]{1,0:T(8,128)(2,1)}, u32[]{:S(2)}) %copy-start.1) | copy-done | bytes 2097176
  3.9 0.8 %copy-done.7 = bf16[2,4,2048]{2,1,0:T(4,128)(2,1)S(1)} copy-done((bf16[2,4,2048]{2,1,0:T(4,128)(2,1)S(1)}, bf16[2,4,2048]{2,1,0:T(4,128)(2,1)}, u32[]{:S(2)}) %copy-start.7) | copy-done | bytes 32792
  4.7 2.1 %block_states.3 = (f32[2,136,128]{2,1,0:T(8,128)S(1)}, f32[2,136,128]{2,1,0:T(8,128)S(1)}, f32[2,136,128]{2,1,0:T(8,128)S(1)}, f32[2,136,128]{2,1,0:T(8,128)S(1)}) custom-call(s32[2]{0:T(128)S(1)} %pad_add_fusion.place_ref, bf16[512,2048]{1,0:T(8,128)(2,1)S(1)} %copy-done, bf16[512,2048]{1,0:T(8,128)(2,1)S(1)} %copy-done.1, bf16[2,4,2048]{2,1,0:T(4,128)(2,1)S(1)} %copy-done.7), custom_call_target="tpu_custom_call" | custom-call | flops 134217728 | bytes 2097152 | tf_op jit(solution)/shard_map/block_states/pallas_call | solution.py:58
  6.8 3.0 %collective-permute-start.7 = (f32[2,136,128]{2,1,0:T(8,128)S(1)}, f32[2,136,128]{2,1,0:T(8,128)S(1)}, u32[]{:S(2)}, u32[]{:S(2)}) collective-permute-start(f32[2,136,128]{2,1,0:T(8,128)S(1)} %get-tuple-element.33), channel_id=1, source_target_pairs={{0,4},{4,0},{8,12},{12,8},{16,20},{20,16},{24,28},{28,24},{1,5},{5... | collective-permute-start | bytes 417800 | tf_op jit(solution)/shard_map/ppermute | solution.py:419
  9.8 1.6 %collective-permute-start.8 = (f32[2,136,128]{2,1,0:T(8,128)S(1)}, f32[2,136,128]{2,1,0:T(8,128)S(1)}, u32[]{:S(2)}, u32[]{:S(2)}) collective-permute-start(f32[2,136,128]{2,1,0:T(8,128)S(1)} %get-tuple-element.34), channel_id=1, source_target_pairs={{0,8},{4,12},{8,0},{12,4},{16,24},{20,28},{24,16},{28,20},{1,9},{5... | collective-permute-start | bytes 417800 | tf_op jit(solution)/shard_map/ppermute | solution.py:419
  11.4 2.1 %block_states.2 = (f32[2,136,128]{2,1,0:T(8,128)S(1)}, f32[2,136,128]{2,1,0:T(8,128)S(1)}, f32[2,136,128]{2,1,0:T(8,128)S(1)}, f32[2,136,128]{2,1,0:T(8,128)S(1)}) custom-call(s32[2]{0:T(128)S(1)} %pad_add_fusion.place_ref, bf16[512,2048]{1,0:T(8,128)(2,1)S(1)} %copy-done, bf16[512,2048]{1,0:T(8,128)(2,1)S(1)} %copy-done.1, bf16[2,4,2048]{2,1,0:T(4,128)(2,1)S(1)} %copy-done.7), custom_call_target="tpu_custom_call" | custom-call | flops 134217728 | bytes 2097152 | tf_op jit(solution)/shard_map/block_states/pallas_call | solution.py:58
  13.6 2.0 %collective-permute-start = (f32[2,136,128]{2,1,0:T(8,128)S(1)}, f32[2,136,128]{2,1,0:T(8,128)S(1)}, u32[]{:S(2)}, u32[]{:S(2)}) collective-permute-start(f32[2,136,128]{2,1,0:T(8,128)S(1)} %get-tuple-element.25), channel_id=1, source_target_pairs={{0,4},{4,0},{8,12},{12,8},{16,20},{20,16},{24,28},{28,24},{1,5},{5... | collective-permute-start | bytes 417800 | tf_op jit(solution)/shard_map/ppermute | solution.py:419
  15.5 1.6 %collective-permute-start.1 = (f32[2,136,128]{2,1,0:T(8,128)S(1)}, f32[2,136,128]{2,1,0:T(8,128)S(1)}, u32[]{:S(2)}, u32[]{:S(2)}) collective-permute-start(f32[2,136,128]{2,1,0:T(8,128)S(1)} %get-tuple-element.26), channel_id=1, source_target_pairs={{0,8},{4,12},{8,0},{12,4},{16,24},{20,28},{24,16},{28,20},{1,9},{5... | collective-permute-start | bytes 417800 | tf_op jit(solution)/shard_map/ppermute | solution.py:419
  17.1 1.7 %collective-permute-done.9.refs_3_ = f32[2,136,128]{2,1,0:T(8,128)S(1)} collective-permute-done((f32[2,136,128]{2,1,0:T(8,128)S(1)}, f32[2,136,128]{2,1,0:T(8,128)S(1)}, u32[]{:S(2)}, u32[]{:S(2)}) %collective-permute-start.9) | collective-permute-done | bytes 139296 | tf_op jit(solution)/shard_map/ppermute | solution.py:419
  18.9 2.8 %collective-permute-start.10 = (f32[2,128,128]{2,1,0:T(8,128)S(1)}, f32[2,128,128]{2,1,0:T(8,128)S(1)}, u32[]{:S(2)}, u32[]{:S(2)}) collective-permute-start(f32[2,128,128]{2,1,0:T(8,128)S(1)} %group_total.3.refs_4_), channel_id=1, source_target_pairs={{0,16},{4,20},{8,24},{12,28},{16,0},{20,4},{24,8},{28,12},{1,17},{... | collective-permute-start | bytes 393224 | tf_op jit(solution)/shard_map/ppermute | solution.py:429
  21.7 4.2 %collective-permute-done.10.refs_5_ = f32[2,128,128]{2,1,0:T(8,128)S(1)} collective-permute-done((f32[2,128,128]{2,1,0:T(8,128)S(1)}, f32[2,128,128]{2,1,0:T(8,128)S(1)}, u32[]{:S(2)}, u32[]{:S(2)}) %collective-permute-start.10) | collective-permute-done | bytes 131104 | tf_op jit(solution)/shard_map/ppermute | solution.py:429
  25.9 0.8 %priors.3 = (f32[2,136,128]{2,1,0:T(8,128)S(1)}, f32[2,136,128]{2,1,0:T(8,128)S(1)}, f32[2,136,128]{2,1,0:T(8,128)S(1)}, f32[2,136,128]{2,1,0:T(8,128)S(1)}) custom-call(s32[2]{0:T(128)S(1)} %pad_add_fusion.place_ref, f32[2,136,128]{2,1,0:T(8,128)S(1)} %get-tuple-element.32.refs_0_, f32[2,136,128]{2,1,0:T(8,128)S(1)} %collective-permute-done.7.refs_1_, ...), custom_call_target="tpu_custom_call" | custom-call | bytes 1392640 | tf_op jit(solution)/shard_map/priors/pallas_call | solution.py:129
  26.7 1.7 %collective-permute-start.11 = (f32[2,136,128]{2,1,0:T(8,128)S(1)}, f32[2,136,128]{2,1,0:T(8,128)S(1)}, u32[]{:S(2)}, u32[]{:S(2)}) collective-permute-start(f32[2,136,128]{2,1,0:T(8,128)S(1)} %get-tuple-element.37), channel_id=1, source_target_pairs={{0,4},{4,0},{8,12},{12,8},{16,20},{20,16},{24,28},{28,24},{1,5},{5... | collective-permute-start | bytes 417800 | tf_op jit(solution)/shard_map/ppermute | solution.py:419
  28.4 2.3 %collective-permute-start.3 = (f32[2,128,128]{2,1,0:T(8,128)S(1)}, f32[2,128,128]{2,1,0:T(8,128)S(1)}, u32[]{:S(2)}, u32[]{:S(2)}) collective-permute-start(f32[2,128,128]{2,1,0:T(8,128)S(1)} %group_total.2.refs_4_), channel_id=1, source_target_pairs={{0,16},{4,20},{8,24},{12,28},{16,0},{20,4},{24,8},{28,12},{1,17},{... | collective-permute-start | bytes 393224 | tf_op jit(solution)/shard_map/ppermute | solution.py:429
  30.8 2.6 %collective-permute-start.12 = (f32[2,136,128]{2,1,0:T(8,128)S(1)}, f32[2,136,128]{2,1,0:T(8,128)S(1)}, u32[]{:S(2)}, u32[]{:S(2)}) collective-permute-start(f32[2,136,128]{2,1,0:T(8,128)S(1)} %get-tuple-element.38), channel_id=1, source_target_pairs={{0,8},{4,12},{8,0},{12,4},{16,24},{20,28},{24,16},{28,20},{1,9},{5... | collective-permute-start | bytes 417800 | tf_op jit(solution)/shard_map/ppermute | solution.py:419
  33.3 0.4 collective-permute-start.13
  33.8 1.9 %collective-permute-done.3.refs_5_ = f32[2,128,128]{2,1,0:T(8,128)S(1)} collective-permute-done((f32[2,128,128]{2,1,0:T(8,128)S(1)}, f32[2,128,128]{2,1,0:T(8,128)S(1)}, u32[]{:S(2)}, u32[]{:S(2)}) %collective-permute-start.3) | collective-permute-done | bytes 131104 | tf_op jit(solution)/shard_map/ppermute | solution.py:429
  35.7 0.8 %priors.2 = (f32[2,136,128]{2,1,0:T(8,128)S(1)}, f32[2,136,128]{2,1,0:T(8,128)S(1)}, f32[2,136,128]{2,1,0:T(8,128)S(1)}, f32[2,136,128]{2,1,0:T(8,128)S(1)}) custom-call(s32[2]{0:T(128)S(1)} %pad_add_fusion.place_ref, f32[2,136,128]{2,1,0:T(8,128)S(1)} %get-tuple-element.24.refs_0_, f32[2,136,128]{2,1,0:T(8,128)S(1)} %collective-permute-done.refs_1_, ...), custom_call_target="tpu_custom_call" | custom-call | bytes 1392640 | tf_op jit(solution)/shard_map/priors/pallas_call | solution.py:129
  36.5 1.4 %collective-permute-start.4 = (f32[2,136,128]{2,1,0:T(8,128)S(1)}, f32[2,136,128]{2,1,0:T(8,128)S(1)}, u32[]{:S(2)}, u32[]{:S(2)}) collective-permute-start(f32[2,136,128]{2,1,0:T(8,128)S(1)} %get-tuple-element.29), channel_id=1, source_target_pairs={{0,4},{4,0},{8,12},{12,8},{16,20},{20,16},{24,28},{28,24},{1,5},{5... | collective-permute-start | bytes 417800 | tf_op jit(solution)/shard_map/ppermute | solution.py:419
  37.9 2.6 %collective-permute-start.5 = (f32[2,136,128]{2,1,0:T(8,128)S(1)}, f32[2,136,128]{2,1,0:T(8,128)S(1)}, u32[]{:S(2)}, u32[]{:S(2)}) collective-permute-start(f32[2,136,128]{2,1,0:T(8,128)S(1)} %get-tuple-element.30), channel_id=1, source_target_pairs={{0,8},{4,12},{8,0},{12,4},{16,24},{20,28},{24,16},{28,20},{1,9},{5... | collective-permute-start | bytes 417800 | tf_op jit(solution)/shard_map/ppermute | solution.py:419
  40.6 5.1 %intra_block.3.intra_ref = f32[512,1024]{1,0:T(8,128)S(1)} custom-call(bf16[512,2048]{1,0:T(8,128)(2,1)S(1)} %copy-done.2, bf16[512,2048]{1,0:T(8,128)(2,1)} %k_ref.9, bf16[512,2048]{1,0:T(8,128)(2,1)} %v_ref.9), custom_call_target="tpu_custom_call" | custom-call | flops 1073741824 | bytes 5242880 | tf_op jit(solution)/shard_map/intra_block/pallas_call | solution.py:166
  45.7 1.3 %copy-done.3 = f32[512,1024]{1,0:T(8,128)} copy-done((f32[512,1024]{1,0:T(8,128)}, f32[512,1024]{1,0:T(8,128)S(1)}, u32[]{:S(2)}) %copy-start.3) | copy-done | bytes 2097176
  47.1 6.8 %suffix_part.1.extra_ref = f32[8,2048]{1,0:T(8,128)S(1)} custom-call(s32[4]{0:T(128)S(1)} %copy-done.11, bf16[2,4,2048]{2,1,0:T(4,128)(2,1)S(1)} %copy-done.7, bf16[4,128,2048]{2,1,0:T(8,128)(2,1)S(1)} %copy-done.5, bf16[4,128,2048]{2,1,0:T(8,128)(2,1)S(1)} %copy-done.6, bf16[2,4,2048]{2,1,0:T(4,128)(2,1)S(1)} %copy-done.8, bf16[2,4,2048]{2,1,0:T(4,128)(2,1)S(1)} %copy-done.9), custom_call_target="tpu_custom_call" | custom-call | flops 67108864 | bytes 4194304 | tf_op jit(solution)/shard_map/suffix_part/pallas_call | solution.py:217
  53.9 4.9 %intra_block.2.intra_ref = f32[512,1024]{1,0:T(8,128)S(1)} custom-call(bf16[512,2048]{1,0:T(8,128)(2,1)S(1)} %copy-done.2, bf16[512,2048]{1,0:T(8,128)(2,1)} %k_ref.9, bf16[512,2048]{1,0:T(8,128)(2,1)} %v_ref.9), custom_call_target="tpu_custom_call" | custom-call | flops 1073741824 | bytes 5242880 | tf_op jit(solution)/shard_map/intra_block/pallas_call | solution.py:166
  58.8 3.7 %attend.2 = (f32[512,1024]{1,0:T(8,128)S(1)}, f32[8,1024]{1,0:T(8,128)S(1)}, f32[640,128]{1,0:T(8,128)S(1)}) custom-call(s32[2]{0:T(128)S(1)} %pad_add_fusion.place_ref, bf16[512,2048]{1,0:T(8,128)(2,1)S(1)} %copy-done.2, f32[512,1024]{1,0:T(8,128)} %copy-done.3, f32[8,2048]{1,0:T(8,128)S(1)} %suffix_part.1.extra_ref, ...), custom_call_target="tpu_custom_call" | custom-call | flops 134217728 | bytes 5242880 | tf_op jit(solution)/shard_map/attend/pallas_call | solution.py:288
  62.7 3.8 %attend.3 = (f32[512,1024]{1,0:T(8,128)S(1)}, f32[8,1024]{1,0:T(8,128)S(1)}, f32[1,640]{1,0:T(1,128)S(1)}) custom-call(s32[2]{0:T(128)S(1)} %pad_add_fusion.place_ref, bf16[512,2048]{1,0:T(8,128)(2,1)S(1)} %copy-done.2, f32[512,1024]{1,0:T(8,128)} %copy-done.4, f32[8,2048]{1,0:T(8,128)S(1)} %suffix_part.1.extra_ref, ...), custom_call_target="tpu_custom_call" | custom-call | flops 134217728 | bytes 5242880 | tf_op jit(solution)/shard_map/attend/pallas_call | solution.py:288
  66.5 1.6 %collective-permute-start.15 = (f32[1,640]{1,0:T(1,128)S(1)}, f32[1,640]{1,0:T(1,128)S(1)}, u32[]{:S(2)}, u32[]{:S(2)}) collective-permute-start(f32[1,640]{1,0:T(1,128)S(1)} %get-tuple-element.41.refs_0_), channel_id=1, source_target_pairs={{0,2},{1,3},{2,0},{3,1},{4,6},{5,7},{6,4},{7,5},{8,10},{9,11},{10,... | collective-permute-start | bytes 7688 | tf_op jit(solution)/shard_map/ppermute | solution.py:450
  68.1 0.2 collective-permute-start.14
  68.3 1.9 %collective-permute-done.15.refs_2_ = f32[1,640]{1,0:T(1,128)S(1)} collective-permute-done((f32[1,640]{1,0:T(1,128)S(1)}, f32[1,640]{1,0:T(1,128)S(1)}, u32[]{:S(2)}, u32[]{:S(2)}) %collective-permute-start.15) | collective-permute-done | bytes 2592 | tf_op jit(solution)/shard_map/ppermute | solution.py:450
  70.2 0.9 %collective-permute-done.14.refs_1_ = f32[1,640]{1,0:T(1,128)S(1)} collective-permute-done((f32[1,640]{1,0:T(1,128)S(1)}, f32[1,640]{1,0:T(1,128)S(1)}, u32[]{:S(2)}, u32[]{:S(2)}) %collective-permute-start.14) | collective-permute-done | bytes 2592 | tf_op jit(solution)/shard_map/ppermute | solution.py:450
  71.1 2.3 %normalize.1 = (bf16[512,2048]{1,0:T(8,128)(2,1)}, bf16[2,4,2048]{2,1,0:T(4,128)(2,1)}) custom-call(f32[1,2048]{1,0:T(1,128)S(1)} %bitcast.3, f32[1,640]{1,0:T(1,128)S(1)} %get-tuple-element.41.refs_0_, f32[1,640]{1,0:T(1,128)S(1)} %collective-permute-done.14.refs_1_, f32[1,640]{1,0:T(1,128)S(1)} %collective-permute-done.15.refs_2_, ...), custom_call_target="tpu_custom_call" | custom-call | bytes 6291456 | tf_op jit(solution)/shard_map/normalize/pallas_call | solution.py:360
  (39 shorter events, 0.4 us)
Async XLA Ops:
  0.7 1.6 %copy-start = (bf16[512,2048]{1,0:T(8,128)(2,1)S(1)}, bf16[512,2048]{1,0:T(8,128)(2,1)}, u32[]{:S(2)}) copy-start(bf16[512,2048]{1,0:T(8,128)(2,1)} %k_ref.9) | copy-start | bytes 6291460
  2.3 1.6 %copy-start.1 = (bf16[512,2048]{1,0:T(8,128)(2,1)S(1)}, bf16[512,2048]{1,0:T(8,128)(2,1)}, u32[]{:S(2)}) copy-start(bf16[512,2048]{1,0:T(8,128)(2,1)} %v_ref.9) | copy-start | bytes 6291460
  3.9 0.8 %copy-start.7 = (bf16[2,4,2048]{2,1,0:T(4,128)(2,1)S(1)}, bf16[2,4,2048]{2,1,0:T(4,128)(2,1)}, u32[]{:S(2)}) copy-start(bf16[2,4,2048]{2,1,0:T(4,128)(2,1)} %q_ref.11) | copy-start | bytes 98308
  6.8 10.3 %collective-permute-start.7 = (f32[2,136,128]{2,1,0:T(8,128)S(1)}, f32[2,136,128]{2,1,0:T(8,128)S(1)}, u32[]{:S(2)}, u32[]{:S(2)}) collective-permute-start(f32[2,136,128]{2,1,0:T(8,128)S(1)} %get-tuple-element.33), channel_id=1, source_target_pairs={{0,4},{4,0},{8,12},{12,8},{16,20},{20,16},{24,28},{28,24},{1,5},{5... | collective-permute-start | bytes 417800 | tf_op jit(solution)/shard_map/ppermute | solution.py:419
  9.8 7.3 %collective-permute-start.8 = (f32[2,136,128]{2,1,0:T(8,128)S(1)}, f32[2,136,128]{2,1,0:T(8,128)S(1)}, u32[]{:S(2)}, u32[]{:S(2)}) collective-permute-start(f32[2,136,128]{2,1,0:T(8,128)S(1)} %get-tuple-element.34), channel_id=1, source_target_pairs={{0,8},{4,12},{8,0},{12,4},{16,24},{20,28},{24,16},{28,20},{1,9},{5... | collective-permute-start | bytes 417800 | tf_op jit(solution)/shard_map/ppermute | solution.py:419
  11.4 7.4 %collective-permute-start.9 = (f32[2,136,128]{2,1,0:T(8,128)S(1)}, f32[2,136,128]{2,1,0:T(8,128)S(1)}, u32[]{:S(2)}, u32[]{:S(2)}) collective-permute-start(f32[2,136,128]{2,1,0:T(8,128)S(1)} %get-tuple-element.35), channel_id=1, source_target_pairs={{0,12},{4,8},{8,4},{12,0},{16,28},{20,24},{24,20},{28,16},{1,13},{... | collective-permute-start | bytes 417800 | tf_op jit(solution)/shard_map/ppermute | solution.py:419
  13.5 27.1 %copy-start.2 = (bf16[512,2048]{1,0:T(8,128)(2,1)S(1)}, bf16[512,2048]{1,0:T(8,128)(2,1)}, u32[]{:S(2)}) copy-start(bf16[512,2048]{1,0:T(8,128)(2,1)} %q_ref.13) | copy-start | bytes 6291460
  13.6 14.8 %collective-permute-start = (f32[2,136,128]{2,1,0:T(8,128)S(1)}, f32[2,136,128]{2,1,0:T(8,128)S(1)}, u32[]{:S(2)}, u32[]{:S(2)}) collective-permute-start(f32[2,136,128]{2,1,0:T(8,128)S(1)} %get-tuple-element.25), channel_id=1, source_target_pairs={{0,4},{4,0},{8,12},{12,8},{16,20},{20,16},{24,28},{28,24},{1,5},{5... | collective-permute-start | bytes 417800 | tf_op jit(solution)/shard_map/ppermute | solution.py:419
  15.5 12.8 %collective-permute-start.1 = (f32[2,136,128]{2,1,0:T(8,128)S(1)}, f32[2,136,128]{2,1,0:T(8,128)S(1)}, u32[]{:S(2)}, u32[]{:S(2)}) collective-permute-start(f32[2,136,128]{2,1,0:T(8,128)S(1)} %get-tuple-element.26), channel_id=1, source_target_pairs={{0,8},{4,12},{8,0},{12,4},{16,24},{20,28},{24,16},{28,20},{1,9},{5... | collective-permute-start | bytes 417800 | tf_op jit(solution)/shard_map/ppermute | solution.py:419
  17.1 11.3 %collective-permute-start.2 = (f32[2,136,128]{2,1,0:T(8,128)S(1)}, f32[2,136,128]{2,1,0:T(8,128)S(1)}, u32[]{:S(2)}, u32[]{:S(2)}) collective-permute-start(f32[2,136,128]{2,1,0:T(8,128)S(1)} %get-tuple-element.27), channel_id=1, source_target_pairs={{0,12},{4,8},{8,4},{12,0},{16,28},{20,24},{24,20},{28,16},{1,13},{... | collective-permute-start | bytes 417800 | tf_op jit(solution)/shard_map/ppermute | solution.py:419
  18.9 7.0 %collective-permute-start.10 = (f32[2,128,128]{2,1,0:T(8,128)S(1)}, f32[2,128,128]{2,1,0:T(8,128)S(1)}, u32[]{:S(2)}, u32[]{:S(2)}) collective-permute-start(f32[2,128,128]{2,1,0:T(8,128)S(1)} %group_total.3.refs_4_), channel_id=1, source_target_pairs={{0,16},{4,20},{8,24},{12,28},{16,0},{20,4},{24,8},{28,12},{1,17},{... | collective-permute-start | bytes 393224 | tf_op jit(solution)/shard_map/ppermute | solution.py:429
  26.7 13.8 %collective-permute-start.11 = (f32[2,136,128]{2,1,0:T(8,128)S(1)}, f32[2,136,128]{2,1,0:T(8,128)S(1)}, u32[]{:S(2)}, u32[]{:S(2)}) collective-permute-start(f32[2,136,128]{2,1,0:T(8,128)S(1)} %get-tuple-element.37), channel_id=1, source_target_pairs={{0,4},{4,0},{8,12},{12,8},{16,20},{20,16},{24,28},{28,24},{1,5},{5... | collective-permute-start | bytes 417800 | tf_op jit(solution)/shard_map/ppermute | solution.py:419
  28.4 7.2 %collective-permute-start.3 = (f32[2,128,128]{2,1,0:T(8,128)S(1)}, f32[2,128,128]{2,1,0:T(8,128)S(1)}, u32[]{:S(2)}, u32[]{:S(2)}) collective-permute-start(f32[2,128,128]{2,1,0:T(8,128)S(1)} %group_total.2.refs_4_), channel_id=1, source_target_pairs={{0,16},{4,20},{8,24},{12,28},{16,0},{20,4},{24,8},{28,12},{1,17},{... | collective-permute-start | bytes 393224 | tf_op jit(solution)/shard_map/ppermute | solution.py:429
  30.8 28.1 %collective-permute-start.12 = (f32[2,136,128]{2,1,0:T(8,128)S(1)}, f32[2,136,128]{2,1,0:T(8,128)S(1)}, u32[]{:S(2)}, u32[]{:S(2)}) collective-permute-start(f32[2,136,128]{2,1,0:T(8,128)S(1)} %get-tuple-element.38), channel_id=1, source_target_pairs={{0,8},{4,12},{8,0},{12,4},{16,24},{20,28},{24,16},{28,20},{1,9},{5... | collective-permute-start | bytes 417800 | tf_op jit(solution)/shard_map/ppermute | solution.py:419
  33.3 25.5 %collective-permute-start.13 = (f32[2,136,128]{2,1,0:T(8,128)S(1)}, f32[2,136,128]{2,1,0:T(8,128)S(1)}, u32[]{:S(2)}, u32[]{:S(2)}) collective-permute-start(f32[2,136,128]{2,1,0:T(8,128)S(1)} %get-tuple-element.39), channel_id=1, source_target_pairs={{0,12},{4,8},{8,4},{12,0},{16,28},{20,24},{24,20},{28,16},{1,13},{... | collective-permute-start | bytes 417800 | tf_op jit(solution)/shard_map/ppermute | solution.py:419
  36.5 26.1 %collective-permute-start.4 = (f32[2,136,128]{2,1,0:T(8,128)S(1)}, f32[2,136,128]{2,1,0:T(8,128)S(1)}, u32[]{:S(2)}, u32[]{:S(2)}) collective-permute-start(f32[2,136,128]{2,1,0:T(8,128)S(1)} %get-tuple-element.29), channel_id=1, source_target_pairs={{0,4},{4,0},{8,12},{12,8},{16,20},{20,16},{24,28},{28,24},{1,5},{5... | collective-permute-start | bytes 417800 | tf_op jit(solution)/shard_map/ppermute | solution.py:419
  37.9 24.8 %collective-permute-start.5 = (f32[2,136,128]{2,1,0:T(8,128)S(1)}, f32[2,136,128]{2,1,0:T(8,128)S(1)}, u32[]{:S(2)}, u32[]{:S(2)}) collective-permute-start(f32[2,136,128]{2,1,0:T(8,128)S(1)} %get-tuple-element.30), channel_id=1, source_target_pairs={{0,8},{4,12},{8,0},{12,4},{16,24},{20,28},{24,16},{28,20},{1,9},{5... | collective-permute-start | bytes 417800 | tf_op jit(solution)/shard_map/ppermute | solution.py:419
  40.5 6.6 %copy-start.5 = (bf16[4,128,2048]{2,1,0:T(8,128)(2,1)S(1)}, bf16[4,128,2048]{2,1,0:T(8,128)(2,1)}, u32[]{:S(2)}) copy-start(bf16[4,128,2048]{2,1,0:T(8,128)(2,1)} %k_ref.6) | copy-start | bytes 6291460
  40.5 6.6 %copy-start.6 = (bf16[4,128,2048]{2,1,0:T(8,128)(2,1)S(1)}, bf16[4,128,2048]{2,1,0:T(8,128)(2,1)}, u32[]{:S(2)}) copy-start(bf16[4,128,2048]{2,1,0:T(8,128)(2,1)} %v_ref.6) | copy-start | bytes 6291460
  40.5 6.6 %copy-start.8 = (bf16[2,4,2048]{2,1,0:T(4,128)(2,1)S(1)}, bf16[2,4,2048]{2,1,0:T(4,128)(2,1)}, u32[]{:S(2)}) copy-start(bf16[2,4,2048]{2,1,0:T(4,128)(2,1)} %sk_ref.1) | copy-start | bytes 98308
  40.5 6.5 %copy-start.9 = (bf16[2,4,2048]{2,1,0:T(4,128)(2,1)S(1)}, bf16[2,4,2048]{2,1,0:T(4,128)(2,1)}, u32[]{:S(2)}) copy-start(bf16[2,4,2048]{2,1,0:T(4,128)(2,1)} %sv_ref.1) | copy-start | bytes 98308
  40.5 6.5 %copy-start.11 = (s32[4]{0:T(128)S(1)}, s32[4]{0:T(128)}, u32[]{:S(2)}) copy-start(s32[4]{0:T(128)} %lengths_ref.1) | copy-start | bytes 52
  40.5 22.1 %collective-permute-start.6 = (f32[2,136,128]{2,1,0:T(8,128)S(1)}, f32[2,136,128]{2,1,0:T(8,128)S(1)}, u32[]{:S(2)}, u32[]{:S(2)}) collective-permute-start(f32[2,136,128]{2,1,0:T(8,128)S(1)} %get-tuple-element.31), channel_id=1, source_target_pairs={{0,12},{4,8},{8,4},{12,0},{16,28},{20,24},{24,20},{28,16},{1,13},{... | collective-permute-start | bytes 417800 | tf_op jit(solution)/shard_map/ppermute | solution.py:419
  45.7 1.4 %copy-start.3 = (f32[512,1024]{1,0:T(8,128)}, f32[512,1024]{1,0:T(8,128)S(1)}, u32[]{:S(2)}) copy-start(f32[512,1024]{1,0:T(8,128)S(1)} %intra_block.3.intra_ref) | copy-start | bytes 6291460
  58.8 3.8 %copy-start.4 = (f32[512,1024]{1,0:T(8,128)}, f32[512,1024]{1,0:T(8,128)S(1)}, u32[]{:S(2)}) copy-start(f32[512,1024]{1,0:T(8,128)S(1)} %intra_block.2.intra_ref) | copy-start | bytes 6291460
  62.6 8.5 %copy-start.10 = (f32[2048]{0:T(1024)S(1)}, f32[2048]{0:T(1024)}, u32[]{:S(2)}) copy-start(f32[2048]{0:T(1024)} %param.19) | copy-start | bytes 24580
  66.5 1.8 %collective-permute-start.16 = (f32[1,640]{1,0:T(1,128)S(1)}, f32[1,640]{1,0:T(1,128)S(1)}, u32[]{:S(2)}, u32[]{:S(2)}) collective-permute-start(f32[1,640]{1,0:T(1,128)S(1)} %get-tuple-element.41.refs_0_), channel_id=1, source_target_pairs={{0,3},{1,0},{2,1},{3,2},{4,7},{5,4},{6,5},{7,6},{8,11},{9,8},{10,9... | collective-permute-start | bytes 7688 | tf_op jit(solution)/shard_map/ppermute | solution.py:450
  66.5 3.7 %collective-permute-start.15 = (f32[1,640]{1,0:T(1,128)S(1)}, f32[1,640]{1,0:T(1,128)S(1)}, u32[]{:S(2)}, u32[]{:S(2)}) collective-permute-start(f32[1,640]{1,0:T(1,128)S(1)} %get-tuple-element.41.refs_0_), channel_id=1, source_target_pairs={{0,2},{1,3},{2,0},{3,1},{4,6},{5,7},{6,4},{7,5},{8,10},{9,11},{10,... | collective-permute-start | bytes 7688 | tf_op jit(solution)/shard_map/ppermute | solution.py:450
  68.1 3.0 %collective-permute-start.14 = (f32[1,640]{1,0:T(1,128)S(1)}, f32[1,640]{1,0:T(1,128)S(1)}, u32[]{:S(2)}, u32[]{:S(2)}) collective-permute-start(f32[1,640]{1,0:T(1,128)S(1)} %get-tuple-element.41.refs_0_), channel_id=1, source_target_pairs={{0,1},{1,2},{2,3},{3,0},{4,5},{5,6},{6,7},{7,4},{8,9},{9,10},{10,1... | collective-permute-start | bytes 7688 | tf_op jit(solution)/shard_map/ppermute | solution.py:450

commit v2 on v0

v2 whole, which is shorter than its diff:
```python
import functools

import jax
import jax.numpy as jnp
from jax import lax
from jax.experimental import pallas as pl
from jax.experimental.pallas import tpu as pltpu
from jax.sharding import PartitionSpec as P

HEAD_DIM = 128
LANES = 128
CHUNKS = 2
F32 = jnp.float32
BF16 = jnp.bfloat16
VMEM_LIMIT = 24 * 1024 * 1024
SMEM = pl.BlockSpec(memory_space=pltpu.SMEM)
VMEM = pl.BlockSpec(memory_space=pltpu.VMEM)
ANY = pl.BlockSpec(memory_space=pl.ANY)


def dot(a, b, contract=((1,), (0,))):
    return lax.dot_general(a, b, (contract, ((), ())), preferred_element_type=F32)


def params():
    return pltpu.CompilerParams(vmem_limit_bytes=VMEM_LIMIT)


def cost(flops, moved):
    return pl.CostEstimate(flops=int(flops), bytes_accessed=int(moved), transcendentals=0)


def head_cols(head):
    return slice(head * HEAD_DIM, (head + 1) * HEAD_DIM)


def flat_rows(ref):
    return jnp.concatenate([ref[i].astype(F32) for i in range(ref.shape[0])], axis=0)


def owned_cols(place_ref, m, first, heads):
    wide = heads * HEAD_DIM
    return pl.ds(pl.multiple_of(first + (place_ref[0] ^ m) * wide, wide), wide)


def split(x):
    high = x.astype(BF16)
    return high, (x - high.astype(F32)).astype(BF16)


def state_kernel(group, first, place_ref, q_ref, k_hbm, v_hbm, *refs):
    out_refs, (k_buf, v_buf, sems) = refs[:group], refs[group:]
    heads = out_refs[0].shape[0]
    order = [*range(1, group), 0]
    copies = {}
    for m in order:
        cols = owned_cols(place_ref, m, first, heads)
        copies[m] = [
            pltpu.make_async_copy(k_hbm.at[:, cols], k_buf.at[m], sems.at[m, 0]),
            pltpu.make_async_copy(v_hbm.at[:, cols], v_buf.at[m], sems.at[m, 1]),
        ]
        for copy in copies[m]:
            copy.start()
    for m in order:
        rows = jnp.concatenate(
            [
                q_ref[i, :, owned_cols(place_ref, m, first, heads)].astype(F32)
                for i in range(q_ref.shape[0])
            ],
            axis=0,
        )
        for copy in copies[m]:
            copy.wait()
        for h in range(heads):
            cols = head_cols(h)
            out_refs[m][h, :HEAD_DIM, :] = dot(k_buf[m, :, cols], v_buf[m, :, cols], ((0,), (0,)))
            out_refs[m][h, HEAD_DIM:, :] = rows[:, cols]


def block_states(chunk, group, heads, place, keys, values, step_queries):
    rows = keys.shape[0]
    steps, samples, _ = step_queries.shape
    wide = heads * HEAD_DIM
    message = (heads, HEAD_DIM + steps * samples, HEAD_DIM)
    hbm = pl.BlockSpec(memory_space=pltpu.HBM)
    return pl.pallas_call(
        functools.partial(state_kernel, group, chunk * group * wide),
        in_specs=[SMEM, VMEM, hbm, hbm],
        out_specs=[VMEM] * group,
        out_shape=[jax.ShapeDtypeStruct(message, F32)] * group,
        scratch_shapes=[
            pltpu.VMEM((group, rows, wide), keys.dtype),
            pltpu.VMEM((group, rows, wide), values.dtype),
            pltpu.SemaphoreType.DMA((group, 2)),
        ],
        compiler_params=params(),
        cost_estimate=cost(2 * rows * wide * HEAD_DIM * group, 4 * rows * wide * group),
        name="block_states",
    )(
        place,
        step_queries,
        pltpu.with_memory_space_constraint(keys, pltpu.HBM),
        pltpu.with_memory_space_constraint(values, pltpu.HBM),
    )


def total_kernel(group, *refs):
    total = refs[0][:, :HEAD_DIM, :]
    for part in refs[1:group]:
        total = total + part[:, :HEAD_DIM, :]
    refs[-1][...] = total


def group_total(parts, after):
    heads = parts[0].shape[0]
    shape = (heads, HEAD_DIM, HEAD_DIM)
    return pl.pallas_call(
        functools.partial(total_kernel, len(parts)),
        in_specs=[VMEM] * len(parts) + [ANY] * len(after),
        out_specs=VMEM,
        out_shape=jax.ShapeDtypeStruct(shape, F32),
        compiler_params=params(),
        cost_estimate=cost(0, 4 * heads * HEAD_DIM * HEAD_DIM * (len(parts) + 1)),
        name="group_total",
    )(*parts, *after)


def prior_kernel(group, others, place_ref, *refs):
    parts, total_ref = refs[:group], refs[group]
    other_refs, out_refs = refs[group + 1 : group + 1 + others], refs[-group:]
    place, block = place_ref[0], place_ref[1]
    heads = parts[0].shape[0]
    for h in range(heads):
        entering = jnp.zeros((HEAD_DIM, HEAD_DIM), F32)
        final = total_ref[h]
        for k in range(others):
            other = other_refs[k][h]
            entering = entering + jnp.where(block > k, other, 0.0)
            final = final + other
        high, low = split(final)
        query = jnp.concatenate([part[h, HEAD_DIM:, :] for part in parts], axis=0).astype(BF16)
        raw = dot(query, high) + dot(query, low)
        dec = raw.shape[0] // group
        for m in range(group):
            prior = entering
            for k in range(group):
                if k != m:
                    prior = prior + jnp.where(
                        (place ^ k) < (place ^ m), parts[k][h, :HEAD_DIM, :], 0.0
                    )
            out_refs[m][h, :HEAD_DIM, :] = prior
            out_refs[m][h, HEAD_DIM:, :] = raw[m * dec : (m + 1) * dec]


def priors(place, parts, total, others, after):
    group = len(parts)
    return pl.pallas_call(
        functools.partial(prior_kernel, group, len(others)),
        in_specs=[SMEM] + [VMEM] * (group + 1 + len(others)) + [ANY] * len(after),
        out_specs=[VMEM] * group,
        out_shape=[jax.ShapeDtypeStruct(parts[0].shape, F32)] * group,
        compiler_params=params(),
        cost_estimate=cost(0, 4 * parts[0].size * (2 * group + 1 + len(others))),
        name="priors",
    )(place, *parts, total, *others, *after)


def intra_kernel(tile, first, q_ref, k_ref, v_ref, *refs):
    out_ref = refs[-1]
    rows, wide = out_ref.shape
    keep = lax.broadcasted_iota(jnp.int32, (tile, tile), 0) >= lax.broadcasted_iota(
        jnp.int32, (tile, tile), 1
    )
    for h in range(wide // HEAD_DIM):
        cols = slice(first + h * HEAD_DIM, first + (h + 1) * HEAD_DIM)
        for i in range(rows // tile):
            here = slice(i * tile, (i + 1) * tile)
            query = q_ref[here, cols]
            scores = dot(query, k_ref[here, cols], ((1,), (1,)))
            scores = jnp.where(keep, scores, 0.0).astype(BF16)
            total = dot(scores, v_ref[here, cols])
            if i:
                before = slice(0, i * tile)
                scores = dot(query, k_ref[before, cols], ((1,), (1,))).astype(BF16)
                total = total + dot(scores, v_ref[before, cols])
            out_ref[here, head_cols(h)] = total


def intra_block(first, wide, queries, keys, values, after):
    rows = queries.shape[0]
    tile = 256 if rows % 256 == 0 else rows
    return pl.pallas_call(
        functools.partial(intra_kernel, tile, first),
        in_specs=[VMEM] * 3 + [ANY] * len(after),
        out_specs=VMEM,
        out_shape=jax.ShapeDtypeStruct((rows, wide), F32),
        compiler_params=params(),
        cost_estimate=cost(4 * rows * rows * wide, 10 * rows * wide),
        name="intra_block",
    )(queries, keys, values, *after)


def suffix_kernel(lengths_ref, q_ref, k_ref, v_ref, sk_ref, sv_ref, *refs):
    out_ref = refs[-1]
    samples, suffix, width = k_ref.shape
    steps = q_ref.shape[0]
    rows = steps * samples
    tokens = samples * suffix
    heads = max(1, min(LANES // rows, width // HEAD_DIM))
    queries = flat_rows(q_ref)
    step_keys = flat_rows(sk_ref).astype(BF16)
    step_values = flat_rows(sv_ref).astype(BF16)

    at = lax.broadcasted_iota(jnp.int32, (heads * rows, tokens), 0) % samples
    token = lax.broadcasted_iota(jnp.int32, (heads * rows, tokens), 1)
    ends = jnp.zeros((heads * rows, tokens), jnp.int32)
    for n in range(samples):
        ends = jnp.where(at == n, n * suffix + lengths_ref[n], ends)
    live = (token >= at * suffix) & (token < ends)
    row = lax.broadcasted_iota(jnp.int32, (heads * rows, rows), 0) % rows
    col = lax.broadcasted_iota(jnp.int32, (heads * rows, rows), 1)
    near = (row % samples == col % samples) & (row // samples >= col // samples)

    for top in range(0, width // HEAD_DIM, heads):
        scores = jnp.zeros((tokens, heads * rows), F32)
        step_scores = jnp.zeros((rows, heads * rows), F32)
        for h in range(heads):
            cols = head_cols(top + h)
            query = queries[:, cols]
            pieces = [jnp.zeros((h * rows, HEAD_DIM), F32)] if h else []
            pieces.append(query)
            if h < heads - 1:
                pieces.append(jnp.zeros(((heads - 1 - h) * rows, HEAD_DIM), F32))
            placed = jnp.concatenate(pieces, axis=0).astype(BF16)
            keys = k_ref[:, :, cols].reshape(tokens, HEAD_DIM)
            scores = scores + dot(keys, placed, ((1,), (1,)))
            step_scores = step_scores + dot(step_keys[:, cols], placed, ((1,), (1,)))
        high, low = split(jnp.where(live, scores.T, 0.0))
        step_high, step_low = split(jnp.where(near, step_scores.T, 0.0))
        for h in range(heads):
            cols = head_cols(top + h)
            own = slice(h * rows, (h + 1) * rows)
            values = v_ref[:, :, cols].reshape(tokens, HEAD_DIM)
            out_ref[:, cols] = (
                dot(high[own], values)
                + dot(low[own], values)
                + dot(step_high[own], step_values[:, cols])
                + dot(step_low[own], step_values[:, cols])
            )


def suffix_part(lengths, step_queries, suffix_keys, suffix_values, step_keys, step_values, after):
    samples, suffix, width = suffix_keys.shape
    steps = step_queries.shape[0]
    return pl.pallas_call(
        suffix_kernel,
        in_specs=[SMEM] + [VMEM] * 5 + [ANY] * len(after),
        out_specs=VMEM,
        out_shape=jax.ShapeDtypeStruct((steps * samples, width), F32),
        compiler_params=params(),
        cost_estimate=cost(64 * samples * suffix * width, 4 * samples * suffix * width),
        name="suffix_part",
    )(lengths, step_queries, suffix_keys, suffix_values, step_keys, step_values, *after)


def attended_kernel(group, top, first, last, place_ref, q_ref, intra_ref, extra_ref, *refs):
    parts = refs[:group]
    att_ref, raw_ref, sum_ref, acc_ref = refs[-4:]
    rows = q_ref.shape[0]
    heads = parts[0].shape[0]
    dec = extra_ref.shape[0]
    if first:
        acc_ref[...] = jnp.zeros_like(acc_ref)
    else:
        acc_ref[...] = refs[group][...]
    for m in range(group):
        all_cols = owned_cols(place_ref, m, top, heads)
        own_cols = owned_cols(place_ref, m, 0, heads)
        query = q_ref[:, all_cols]
        intra = intra_ref[:, own_cols]
        extra = extra_ref[:, all_cols]
        squares = acc_ref[:rows, :]
        raw_squares = acc_ref[rows : rows + dec, :]
        atts, raws = [], []
        for h in range(heads):
            cols = head_cols(h)
            att = intra[:, cols] + dot(query[:, cols], parts[m][h, :HEAD_DIM, :].astype(BF16))
            raw = extra[:, cols] + parts[m][h, HEAD_DIM:, :]
            squares = squares + att * att
            raw_squares = raw_squares + raw * raw
            atts.append(att)
            raws.append(raw)
        att_ref[:, own_cols] = jnp.concatenate(atts, axis=1)
        raw_ref[:, own_cols] = jnp.concatenate(raws, axis=1)
        acc_ref[:rows, :] = squares
        acc_ref[rows : rows + dec, :] = raw_squares
    if last:
        sum_ref[...] = jnp.sum(acc_ref[...].T, axis=0, keepdims=True)
    else:
        sum_ref[...] = acc_ref[...]


def attend(chunk, last, place, queries, intra, extra, parts, before, after):
    group = len(parts)
    heads = parts[0].shape[0]
    wide = group * heads * HEAD_DIM
    rows, dec = queries.shape[0], extra.shape[0]
    padded = -(-(rows + dec) // LANES) * LANES
    sums = (1, padded) if last else (padded, LANES)
    return pl.pallas_call(
        functools.partial(attended_kernel, group, chunk * wide, not before, last),
        in_specs=[SMEM] + [VMEM] * (3 + group + len(before)) + [ANY] * len(after),
        out_specs=[VMEM] * 3,
        out_shape=[
            jax.ShapeDtypeStruct((rows, wide), F32),
            jax.ShapeDtypeStruct((dec, wide), F32),
            jax.ShapeDtypeStruct(sums, F32),
        ],
        scratch_shapes=[pltpu.VMEM((padded, LANES), F32)],
        compiler_params=params(),
        cost_estimate=cost(2 * rows * wide * HEAD_DIM, 10 * rows * wide),
        name="attend",
    )(place, queries, intra, extra, *parts, *before, *after)


def norm_kernel(chunks, sums, width, tile, gain_ref, *refs):
    sum_refs = refs[:sums]
    att_refs = refs[sums : sums + chunks]
    raw_refs = refs[sums + chunks : sums + 2 * chunks]
    out_hbm, dec_ref, scale_ref, buf_ref, sems = refs[sums + 2 * chunks :]
    rows, wide = att_refs[0].shape
    dec = raw_refs[0].shape[0]
    samples = dec_ref.shape[1]
    total = sum_refs[0][...]
    for ref in sum_refs[1:]:
        total = total + ref[...]
    scale = lax.rsqrt(total / width + 1e-06)
    scale_ref[...] = jnp.broadcast_to(scale, (LANES, scale.shape[1])).T
    copies = []
    for i in range(rows // tile):
        here = slice(i * tile, (i + 1) * tile)
        row_scale = scale_ref[here, :]
        for c in range(chunks):
            for h in range(wide // HEAD_DIM):
                at = slice(c * wide + h * HEAD_DIM, c * wide + (h + 1) * HEAD_DIM)
                buf_ref[here, at] = (
                    att_refs[c][here, head_cols(h)] * row_scale * gain_ref[:, at]
                ).astype(BF16)
        copies.append(pltpu.make_async_copy(buf_ref.at[here], out_hbm.at[here], sems.at[i]))
        copies[-1].start()
    row_scale = scale_ref[rows : rows + dec, :]
    for c in range(chunks):
        for h in range(wide // HEAD_DIM):
            at = slice(c * wide + h * HEAD_DIM, c * wide + (h + 1) * HEAD_DIM)
            out = raw_refs[c][:, head_cols(h)] * row_scale * gain_ref[:, at]
            for i in range(dec_ref.shape[0]):
                dec_ref[i, :, at] = out[i * samples : (i + 1) * samples].astype(BF16)
    for copy in copies:
        copy.wait()


def normalize(atts, raws, sums, gain, steps, width_all):
    rows, wide = atts[0].shape
    width = wide * len(atts)
    dec = raws[0].shape[0]
    tile = 128 if rows % 128 == 0 else rows
    return pl.pallas_call(
        functools.partial(norm_kernel, len(atts), len(sums), width_all, tile),
        in_specs=[VMEM] * (1 + len(sums) + 2 * len(atts)),
        out_specs=[pl.BlockSpec(memory_space=pltpu.HBM), VMEM],
        out_shape=[
            jax.ShapeDtypeStruct((rows, width), BF16),
            jax.ShapeDtypeStruct((steps, dec // steps, width), BF16),
        ],
        scratch_shapes=[
            pltpu.VMEM((sums[0].shape[1], LANES), F32),
            pltpu.VMEM((rows, width), BF16),
            pltpu.SemaphoreType.DMA((rows // tile,)),
        ],
        compiler_params=params(),
        cost_estimate=cost(0, 6 * rows * width),
        name="normalize",
    )(gain[None, :], *sums, *atts, *raws)


def group_size(devices, heads):
    size = 1
    while (
        devices % (2 * size) == 0
        and size * size < devices
        and heads % (2 * size * CHUNKS) == 0
    ):
        size *= 2
    return size


def on_device(
    queries,
    keys,
    values,
    suffix_keys,
    suffix_values,
    suffix_lengths,
    step_queries,
    step_keys,
    step_values,
    norm_gain,
):
    width = queries.shape[1]
    heads_here = width // HEAD_DIM
    devices = lax.axis_size("seq")
    group = group_size(devices, heads_here)
    blocks = devices // group
    heads = heads_here // (group * CHUNKS)
    rank = lax.axis_index("seq")
    place = jnp.stack([rank % group, rank // group]).astype(jnp.int32)

    def swap(m):
        return [(i, i // group * group + (i % group ^ m)) for i in range(devices)]

    def exchange(messages):
        return [messages[0]] + [
            lax.ppermute(messages[m], "seq", swap(m)) for m in range(1, group)
        ]

    def across(total):
        return [
            lax.ppermute(total, "seq", [(i, (i + k * group) % devices) for i in range(devices)])
            for k in range(1, blocks)
        ]

    wide = width // CHUNKS
    parts, totals, others, entering, intra = [], [], [], [], []
    for c in range(CHUNKS):
        parts.append(exchange(block_states(c, group, heads, place, keys, values, step_queries)))
    last = [parts[-1][0]]
    for c in range(CHUNKS):
        if c == 0 or CHUNKS == 1:
            last = [intra_block(c * wide, wide, queries, keys, values, last)]
            intra += last
        totals.append(group_total(parts[c], last))
        others.append(across(totals[c]))
        if c == 0 and CHUNKS > 1:
            last = [intra_block(wide, width - wide, queries, keys, values, [totals[c]])]
            intra += last
        else:
            extra = suffix_part(
                suffix_lengths,
                step_queries,
                suffix_keys,
                suffix_values,
                step_keys,
                step_values,
                [totals[c]],
            )
            last = [extra]
        sent = priors(place, parts[c], totals[c], others[c], last)
        entering.append(exchange(sent))
        last = [sent[0]]
    atts, raws, sums = [], [], []
    for c in range(CHUNKS):
        att, raw, total = attend(
            c, c == CHUNKS - 1, place, queries, intra[c], extra, entering[c], sums, last
        )
        sums = [total]
        atts.append(att)
        raws.append(raw)
    sums = sums[0]
    others_of_row = lax.axis_size("head")
    all_sums = [sums] + [
        lax.ppermute(
            sums, "head", [(i, (i + k) % others_of_row) for i in range(others_of_row)]
        )
        for k in range(1, others_of_row)
    ]
    return tuple(
        normalize(
            atts, raws, all_sums, norm_gain, step_queries.shape[0], width * others_of_row
        )
    )


def solution(mesh):
    return jax.shard_map(
        on_device,
        mesh=mesh,
        in_specs=(
            P("seq", "head"),
            P("seq", "head"),
            P("seq", "head"),
            P("seq", None, "head"),
            P("seq", None, "head"),
            P("seq"),
            P(None, "seq", "head"),
            P(None, "seq", "head"),
            P(None, "seq", "head"),
            P("head"),
        ),
        out_specs=(P("seq", "head"), P(None, "seq", "head")),
        check_vma=False,
    )
```

time: 252 us -> 54.3 us (0.22)
  waiting for transfers between devices: 176 us -> 9.3 us
  matrix products: 33.2 us -> 0 us
  starting transfers between devices: 0.04 us -> 21.7 us
  Pallas kernels: 0 us -> 21.4 us
  between operations: 14.2 us -> 0.78 us
  local copies, waits for them, and re-layouts: 13.8 us -> 0.8 us
  other arithmetic: 8.06 us -> 0.08 us
  blocking collectives: 5.85 us -> 0 us
    all_gather x1 -> x0, waiting for transfers between devices: 106 us -> none  [entering(): gathered = lax.all_gather(part, axis)]
    psum x1 -> x0, waiting for transfers between devices: 69.3 us -> none  [on_device(): final = lax.psum(own_state, 'seq')]
    dot_general x6 -> x0, matrix products: 33.2 us -> none  [the longest x2 10 us: on_device(): raw = jnp.einsum('bhd,bhde->bhe', new_query, state, precision=HIGHEST_PREC)]
    ppermute x0 -> x17, starting transfers between devices: none -> 21.7 us  [the longest x12 16 us: exchange(): lax.ppermute(messages[m], 'seq', swap(m))]
    pallas_call x0 -> x12, Pallas kernels: none -> 21.4 us  [the longest x2 6.56 us: intra_block(): pl.pallas_call(functools.partial(intra_kernel, tile, first), in_specs=[VM...]
    reshape x3 -> x0, local copies, waits for them, and re-layouts: 13.5 us -> none  [the longest x1 5.48 us: on_device(): attended = (intra + inter).reshape(rows_here, heads_here * HEAD_DIM)]
    ppermute x0 -> x17, waiting for transfers between devices: none -> 9.3 us  [the longest x12 4.05 us: exchange(): lax.ppermute(messages[m], 'seq', swap(m))]
    psum x1 -> x0, blocking collectives: 5.85 us -> none  [on_device(): total_sq = lax.psum(jnp.sum(attended * attended, axis=1), 'head')]
  transfers between devices with their start and end apart: 2 -> 17, of which waited for: 2 -> 7; matrix products, arithmetic and copies ran while one was open for 13% -> 0% of each run, Pallas kernels for 0% -> 28%
where the time goes in v2:
time: 54.3 us; the launch traced here: 54.1 us
  starting transfers between devices  21.7 us (40%)
  Pallas kernels  21.4 us (39%)
  waiting for transfers between devices  9.3 us (17%)
  local copies, waits for them, and re-layouts  0.8 us (1%)
  between operations  0.78 us (1%)
    ppermute x12, starting transfers between devices, exchange(): lax.ppermute(messages[m], 'seq', swap(m))  16 us
    pallas_call x2, Pallas kernels, intra_block(): pl.pallas_call(functools.partial(intra_kernel, tile, first), in_specs=[VM...  6.56 us
    pallas_call x2, Pallas kernels, block_states(): pl.pallas_call(functools.partial(state_kernel, group, chunk * group * wid...  5.86 us
    ppermute x12, waiting for transfers between devices, exchange(): lax.ppermute(messages[m], 'seq', swap(m))  4.05 us
    ppermute x2, starting transfers between devices, across(): lax.ppermute(total, 'seq', [(i, (i + k * group) % devices) for i in range...  3.91 us
    pallas_call x1, Pallas kernels, suffix_part(): pl.pallas_call(suffix_kernel, in_specs=[SMEM] + [VMEM] * 5 + [ANY] * len(...  2.93 us
    ppermute x3, waiting for transfers between devices, on_device(): lax.ppermute(sums, 'head', [(i, (i + k) % others_of_row) for i in range(o...  2.85 us
    ppermute x2, waiting for transfers between devices, across(): lax.ppermute(total, 'seq', [(i, (i + k * group) % devices) for i in range...  2.4 us
  transfers between devices with their start and end apart: 17, of which 7 were waited for; matrix products, arithmetic and copies ran while one was open for 0% of the time, Pallas kernels for 28%

profile of v2, /device:TPU:0, one launch (start us, length us, event | category | flops | bytes accessed | tf_op | source)
XLA Modules:
  0.0 54.1 jit_solution(8447353466918898545)
XLA Ops:
  0.7 0.8 %copy-done.5 = bf16[2,4,2048]{2,1,0:T(4,128)(2,1)S(1)} copy-done((bf16[2,4,2048]{2,1,0:T(4,128)(2,1)S(1)}, bf16[2,4,2048]{2,1,0:T(4,128)(2,1)}, u32[]{:S(2)}) %copy-start.5) | copy-done | bytes 32792
  1.5 2.8 %block_states.2 = (f32[2,136,128]{2,1,0:T(8,128)S(1)}, f32[2,136,128]{2,1,0:T(8,128)S(1)}, f32[2,136,128]{2,1,0:T(8,128)S(1)}, f32[2,136,128]{2,1,0:T(8,128)S(1)}) custom-call(s32[2]{0:T(128)S(1)} %pad_add_fusion.place_ref, bf16[2,4,2048]{2,1,0:T(4,128)(2,1)S(1)} %copy-done.5, bf16[512,2048]{1,0:T(8,128)(2,1)} %k_ref.4, bf16[512,2048]{1,0:T(8,128)(2,1)} %v_ref.4), custom_call_target="tpu_custom_call" | custom-call | flops 134217728 | bytes 2097152 | tf_op jit(solution)/shard_map/block_states/pallas_call | solution.py:86
  4.3 3.0 %collective-permute-start = (f32[2,136,128]{2,1,0:T(8,128)S(1)}, f32[2,136,128]{2,1,0:T(8,128)S(1)}, u32[]{:S(2)}, u32[]{:S(2)}) collective-permute-start(f32[2,136,128]{2,1,0:T(8,128)S(1)} %get-tuple-element.25), channel_id=1, source_target_pairs={{0,4},{4,0},{8,12},{12,8},{16,20},{20,16},{24,28},{28,24},{1,5},{5... | collective-permute-start | bytes 417800 | tf_op jit(solution)/shard_map/ppermute | solution.py:423
  7.4 1.6 %collective-permute-start.1 = (f32[2,136,128]{2,1,0:T(8,128)S(1)}, f32[2,136,128]{2,1,0:T(8,128)S(1)}, u32[]{:S(2)}, u32[]{:S(2)}) collective-permute-start(f32[2,136,128]{2,1,0:T(8,128)S(1)} %get-tuple-element.26), channel_id=1, source_target_pairs={{0,8},{4,12},{8,0},{12,4},{16,24},{20,28},{24,16},{28,20},{1,9},{5... | collective-permute-start | bytes 417800 | tf_op jit(solution)/shard_map/ppermute | solution.py:423
  9.0 3.0 %block_states.3 = (f32[2,136,128]{2,1,0:T(8,128)S(1)}, f32[2,136,128]{2,1,0:T(8,128)S(1)}, f32[2,136,128]{2,1,0:T(8,128)S(1)}, f32[2,136,128]{2,1,0:T(8,128)S(1)}) custom-call(s32[2]{0:T(128)S(1)} %pad_add_fusion.place_ref, bf16[2,4,2048]{2,1,0:T(4,128)(2,1)S(1)} %copy-done.5, bf16[512,2048]{1,0:T(8,128)(2,1)} %k_ref.4, bf16[512,2048]{1,0:T(8,128)(2,1)} %v_ref.4), custom_call_target="tpu_custom_call" | custom-call | flops 134217728 | bytes 2097152 | tf_op jit(solution)/shard_map/block_states/pallas_call | solution.py:86
  12.0 1.7 %collective-permute-start.3 = (f32[2,136,128]{2,1,0:T(8,128)S(1)}, f32[2,136,128]{2,1,0:T(8,128)S(1)}, u32[]{:S(2)}, u32[]{:S(2)}) collective-permute-start(f32[2,136,128]{2,1,0:T(8,128)S(1)} %get-tuple-element.29), channel_id=1, source_target_pairs={{0,4},{4,0},{8,12},{12,8},{16,20},{20,16},{24,28},{28,24},{1,5},{5... | collective-permute-start | bytes 417800 | tf_op jit(solution)/shard_map/ppermute | solution.py:423
  13.7 1.6 %collective-permute-start.4 = (f32[2,136,128]{2,1,0:T(8,128)S(1)}, f32[2,136,128]{2,1,0:T(8,128)S(1)}, u32[]{:S(2)}, u32[]{:S(2)}) collective-permute-start(f32[2,136,128]{2,1,0:T(8,128)S(1)} %get-tuple-element.30), channel_id=1, source_target_pairs={{0,8},{4,12},{8,0},{12,4},{16,24},{20,28},{24,16},{28,20},{1,9},{5... | collective-permute-start | bytes 417800 | tf_op jit(solution)/shard_map/ppermute | solution.py:423
  15.3 0.3 collective-permute-start.5
  15.5 3.3 %intra_block.2.refs_4_.intra_ref = f32[512,1024]{1,0:T(8,128)S(1)} custom-call(bf16[512,2048]{1,0:T(8,128)(2,1)S(1)} %copy-done.2, bf16[512,2048]{1,0:T(8,128)(2,1)S(1)} %copy-done, bf16[512,2048]{1,0:T(8,128)(2,1)S(1)} %copy-done.1, f32[2,136,128]{2,1,0:T(8,128)S(1)} %get-tuple-element.28.refs_0_), custom_call_target="tpu_custom_call" | custom-call | flops 1073741824 | bytes 5242880 | tf_op jit(solution)/shard_map/intra_block/pallas_call | solution.py:192
  18.9 3.1 %collective-permute-start.6 = (f32[2,128,128]{2,1,0:T(8,128)S(1)}, f32[2,128,128]{2,1,0:T(8,128)S(1)}, u32[]{:S(2)}, u32[]{:S(2)}) collective-permute-start(f32[2,128,128]{2,1,0:T(8,128)S(1)} %group_total.2.refs_0_.refs_4_), channel_id=1, source_target_pairs={{0,16},{4,20},{8,24},{12,28},{16,0},{20,4},{24,8},{28,12},{1,17},{... | collective-permute-start | bytes 393224 | tf_op jit(solution)/shard_map/ppermute | solution.py:428
  22.0 3.3 %intra_block.3.refs_6_.intra_ref = f32[512,1024]{1,0:T(8,128)S(1)} custom-call(bf16[512,2048]{1,0:T(8,128)(2,1)S(1)} %copy-done.2, bf16[512,2048]{1,0:T(8,128)(2,1)S(1)} %copy-done, bf16[512,2048]{1,0:T(8,128)(2,1)S(1)} %copy-done.1, f32[2,128,128]{2,1,0:T(8,128)S(1)} %group_total.2.refs_0_.refs_4_), custom_call_target="tpu_custom_call" | custom-call | flops 1073741824 | bytes 5242880 | tf_op jit(solution)/shard_map/intra_block/pallas_call | solution.py:192
  25.3 1.6 %collective-permute-done.6.refs_5_ = f32[2,128,128]{2,1,0:T(8,128)S(1)} collective-permute-done((f32[2,128,128]{2,1,0:T(8,128)S(1)}, f32[2,128,128]{2,1,0:T(8,128)S(1)}, u32[]{:S(2)}, u32[]{:S(2)}) %collective-permute-start.6) | collective-permute-done | bytes 131104 | tf_op jit(solution)/shard_map/ppermute | solution.py:428
  26.9 0.8 %priors.2 = (f32[2,136,128]{2,1,0:T(8,128)S(1)}, f32[2,136,128]{2,1,0:T(8,128)S(1)}, f32[2,136,128]{2,1,0:T(8,128)S(1)}, f32[2,136,128]{2,1,0:T(8,128)S(1)}) custom-call(s32[2]{0:T(128)S(1)} %pad_add_fusion.place_ref, f32[2,136,128]{2,1,0:T(8,128)S(1)} %get-tuple-element.24.refs_0_, f32[2,136,128]{2,1,0:T(8,128)S(1)} %collective-permute-done.refs_1_, ...), custom_call_target="tpu_custom_call" | custom-call | bytes 1392640 | tf_op jit(solution)/shard_map/priors/pallas_call | solution.py:157
  27.7 1.5 %collective-permute-start.11 = (f32[2,136,128]{2,1,0:T(8,128)S(1)}, f32[2,136,128]{2,1,0:T(8,128)S(1)}, u32[]{:S(2)}, u32[]{:S(2)}) collective-permute-start(f32[2,136,128]{2,1,0:T(8,128)S(1)} %get-tuple-element.37), channel_id=1, source_target_pairs={{0,4},{4,0},{8,12},{12,8},{16,20},{20,16},{24,28},{28,24},{1,5},{5... | collective-permute-start | bytes 417800 | tf_op jit(solution)/shard_map/ppermute | solution.py:423
  29.3 0.8 %collective-permute-start.7 = (f32[2,128,128]{2,1,0:T(8,128)S(1)}, f32[2,128,128]{2,1,0:T(8,128)S(1)}, u32[]{:S(2)}, u32[]{:S(2)}) collective-permute-start(f32[2,128,128]{2,1,0:T(8,128)S(1)} %group_total.3.refs_0_.refs_4_), channel_id=1, source_target_pairs={{0,16},{4,20},{8,24},{12,28},{16,0},{20,4},{24,8},{28,12},{1,17},{... | collective-permute-start | bytes 393224 | tf_op jit(solution)/shard_map/ppermute | solution.py:428
  30.1 2.8 %collective-permute-start.12 = (f32[2,136,128]{2,1,0:T(8,128)S(1)}, f32[2,136,128]{2,1,0:T(8,128)S(1)}, u32[]{:S(2)}, u32[]{:S(2)}) collective-permute-start(f32[2,136,128]{2,1,0:T(8,128)S(1)} %get-tuple-element.38), channel_id=1, source_target_pairs={{0,8},{4,12},{8,0},{12,4},{16,24},{20,28},{24,16},{28,20},{1,9},{5... | collective-permute-start | bytes 417800 | tf_op jit(solution)/shard_map/ppermute | solution.py:423
  32.9 2.9 %suffix_part.1.refs_6_.extra_ref = f32[8,2048]{1,0:T(8,128)S(1)} custom-call(s32[4]{0:T(128)S(1)} %copy-done.9, bf16[2,4,2048]{2,1,0:T(4,128)(2,1)S(1)} %copy-done.5, bf16[4,128,2048]{2,1,0:T(8,128)(2,1)S(1)} %copy-done.3, bf16[4,128,2048]{2,1,0:T(8,128)(2,1)S(1)} %copy-done.4, bf16[2,4,2048]{2,1,0:T(4,128)(2,1)S(1)} %copy-done.6, ...), custom_call_target="tpu_custom_call" | custom-call | flops 67108864 | bytes 4194304 | tf_op jit(solution)/shard_map/suffix_part/pallas_call | solution.py:255
  35.9 0.8 %collective-permute-done.7.refs_5_ = f32[2,128,128]{2,1,0:T(8,128)S(1)} collective-permute-done((f32[2,128,128]{2,1,0:T(8,128)S(1)}, f32[2,128,128]{2,1,0:T(8,128)S(1)}, u32[]{:S(2)}, u32[]{:S(2)}) %collective-permute-start.7) | collective-permute-done | bytes 131104 | tf_op jit(solution)/shard_map/ppermute | solution.py:428
  36.7 0.8 %priors.3 = (f32[2,136,128]{2,1,0:T(8,128)S(1)}, f32[2,136,128]{2,1,0:T(8,128)S(1)}, f32[2,136,128]{2,1,0:T(8,128)S(1)}, f32[2,136,128]{2,1,0:T(8,128)S(1)}) custom-call(s32[2]{0:T(128)S(1)} %pad_add_fusion.place_ref, f32[2,136,128]{2,1,0:T(8,128)S(1)} %get-tuple-element.28.refs_0_, f32[2,136,128]{2,1,0:T(8,128)S(1)} %collective-permute-done.3.refs_1_, ...), custom_call_target="tpu_custom_call" | custom-call | bytes 1392640 | tf_op jit(solution)/shard_map/priors/pallas_call | solution.py:157
  37.5 0.6 %collective-permute-start.8 = (f32[2,136,128]{2,1,0:T(8,128)S(1)}, f32[2,136,128]{2,1,0:T(8,128)S(1)}, u32[]{:S(2)}, u32[]{:S(2)}) collective-permute-start(f32[2,136,128]{2,1,0:T(8,128)S(1)} %get-tuple-element.34), channel_id=1, source_target_pairs={{0,4},{4,0},{8,12},{12,8},{16,20},{20,16},{24,28},{28,24},{1,5},{5... | collective-permute-start | bytes 417800 | tf_op jit(solution)/shard_map/ppermute | solution.py:423
  38.1 2.0 %collective-permute-start.9 = (f32[2,136,128]{2,1,0:T(8,128)S(1)}, f32[2,136,128]{2,1,0:T(8,128)S(1)}, u32[]{:S(2)}, u32[]{:S(2)}) collective-permute-start(f32[2,136,128]{2,1,0:T(8,128)S(1)} %get-tuple-element.35), channel_id=1, source_target_pairs={{0,8},{4,12},{8,0},{12,4},{16,24},{20,28},{24,16},{28,20},{1,9},{5... | collective-permute-start | bytes 417800 | tf_op jit(solution)/shard_map/ppermute | solution.py:423
  40.1 0.9 %collective-permute-start.10 = (f32[2,136,128]{2,1,0:T(8,128)S(1)}, f32[2,136,128]{2,1,0:T(8,128)S(1)}, u32[]{:S(2)}, u32[]{:S(2)}) collective-permute-start(f32[2,136,128]{2,1,0:T(8,128)S(1)} %get-tuple-element.36), channel_id=1, source_target_pairs={{0,12},{4,8},{8,4},{12,0},{16,28},{20,24},{24,20},{28,16},{1,13},{... | collective-permute-start | bytes 417800 | tf_op jit(solution)/shard_map/ppermute | solution.py:423
  41.0 1.0 %attend.2 = (f32[512,1024]{1,0:T(8,128)S(1)}, f32[8,1024]{1,0:T(8,128)S(1)}, f32[640,128]{1,0:T(8,128)S(1)}) custom-call(s32[2]{0:T(128)S(1)} %pad_add_fusion.place_ref, bf16[512,2048]{1,0:T(8,128)(2,1)S(1)} %copy-done.2, f32[512,1024]{1,0:T(8,128)S(1)} %intra_block.2.refs_4_.intra_ref, f32[8,2048]{1,0:T(8,128)S(1)} %suffix_part.1.refs_6_.extra_ref, ...), custom_call_target="tpu_custom_call" | custom-call | flops 134217728 | bytes 5242880 | tf_op jit(solution)/shard_map/attend/pallas_call | solution.py:310
  42.0 0.9 %collective-permute-done.8.refs_1_ = f32[2,136,128]{2,1,0:T(8,128)S(1)} collective-permute-done((f32[2,136,128]{2,1,0:T(8,128)S(1)}, f32[2,136,128]{2,1,0:T(8,128)S(1)}, u32[]{:S(2)}, u32[]{:S(2)}) %collective-permute-start.8) | collective-permute-done | bytes 139296 | tf_op jit(solution)/shard_map/ppermute | solution.py:423
  42.9 0.2 collective-permute-done.9.refs_2_
  43.2 2.9 %collective-permute-done.10.refs_3_ = f32[2,136,128]{2,1,0:T(8,128)S(1)} collective-permute-done((f32[2,136,128]{2,1,0:T(8,128)S(1)}, f32[2,136,128]{2,1,0:T(8,128)S(1)}, u32[]{:S(2)}, u32[]{:S(2)}) %collective-permute-start.10) | collective-permute-done | bytes 139296 | tf_op jit(solution)/shard_map/ppermute | solution.py:423
  46.1 1.1 %attend.3 = (f32[512,1024]{1,0:T(8,128)S(1)}, f32[8,1024]{1,0:T(8,128)S(1)}, f32[1,640]{1,0:T(1,128)S(1)}) custom-call(s32[2]{0:T(128)S(1)} %pad_add_fusion.place_ref, bf16[512,2048]{1,0:T(8,128)(2,1)S(1)} %copy-done.2, f32[512,1024]{1,0:T(8,128)S(1)} %intra_block.3.refs_6_.intra_ref, f32[8,2048]{1,0:T(8,128)S(1)} %suffix_part.1.refs_6_.extra_ref, ...), custom_call_target="tpu_custom_call" | custom-call | flops 134217728 | bytes 5242880 | tf_op jit(solution)/shard_map/attend/pallas_call | solution.py:310
  47.3 1.6 %collective-permute-start.15 = (f32[1,640]{1,0:T(1,128)S(1)}, f32[1,640]{1,0:T(1,128)S(1)}, u32[]{:S(2)}, u32[]{:S(2)}) collective-permute-start(f32[1,640]{1,0:T(1,128)S(1)} %get-tuple-element.41.refs_0_), channel_id=1, source_target_pairs={{0,2},{1,3},{2,0},{3,1},{4,6},{5,7},{6,4},{7,5},{8,10},{9,11},{10,... | collective-permute-start | bytes 7688 | tf_op jit(solution)/shard_map/ppermute | solution.py:471
  48.8 0.2 collective-permute-start.14
  49.0 1.9 %collective-permute-done.15.refs_2_ = f32[1,640]{1,0:T(1,128)S(1)} collective-permute-done((f32[1,640]{1,0:T(1,128)S(1)}, f32[1,640]{1,0:T(1,128)S(1)}, u32[]{:S(2)}, u32[]{:S(2)}) %collective-permute-start.15) | collective-permute-done | bytes 2592 | tf_op jit(solution)/shard_map/ppermute | solution.py:471
  50.9 0.9 %collective-permute-done.14.refs_1_ = f32[1,640]{1,0:T(1,128)S(1)} collective-permute-done((f32[1,640]{1,0:T(1,128)S(1)}, f32[1,640]{1,0:T(1,128)S(1)}, u32[]{:S(2)}, u32[]{:S(2)}) %collective-permute-start.14) | collective-permute-done | bytes 2592 | tf_op jit(solution)/shard_map/ppermute | solution.py:471
  51.9 2.2 %normalize.1 = (bf16[512,2048]{1,0:T(8,128)(2,1)}, bf16[2,4,2048]{2,1,0:T(4,128)(2,1)}) custom-call(f32[1,2048]{1,0:T(1,128)S(1)} %bitcast.3, f32[1,640]{1,0:T(1,128)S(1)} %get-tuple-element.41.refs_0_, f32[1,640]{1,0:T(1,128)S(1)} %collective-permute-done.14.refs_1_, f32[1,640]{1,0:T(1,128)S(1)} %collective-permute-done.15.refs_2_, ...), custom_call_target="tpu_custom_call" | custom-call | bytes 6291456 | tf_op jit(solution)/shard_map/normalize/pallas_call | solution.py:367
  (35 shorter events, 0.3 us)
Async XLA Ops:
  0.7 0.8 %copy-start.5 = (bf16[2,4,2048]{2,1,0:T(4,128)(2,1)S(1)}, bf16[2,4,2048]{2,1,0:T(4,128)(2,1)}, u32[]{:S(2)}) copy-start(bf16[2,4,2048]{2,1,0:T(4,128)(2,1)} %q_ref.11) | copy-start | bytes 98308
  1.5 14.1 %copy-start.2 = (bf16[512,2048]{1,0:T(8,128)(2,1)S(1)}, bf16[512,2048]{1,0:T(8,128)(2,1)}, u32[]{:S(2)}) copy-start(bf16[512,2048]{1,0:T(8,128)(2,1)} %q_ref.13) | copy-start | bytes 6291460
  4.3 10.9 %collective-permute-start = (f32[2,136,128]{2,1,0:T(8,128)S(1)}, f32[2,136,128]{2,1,0:T(8,128)S(1)}, u32[]{:S(2)}, u32[]{:S(2)}) collective-permute-start(f32[2,136,128]{2,1,0:T(8,128)S(1)} %get-tuple-element.25), channel_id=1, source_target_pairs={{0,4},{4,0},{8,12},{12,8},{16,20},{20,16},{24,28},{28,24},{1,5},{5... | collective-permute-start | bytes 417800 | tf_op jit(solution)/shard_map/ppermute | solution.py:423
  7.4 11.5 %collective-permute-start.1 = (f32[2,136,128]{2,1,0:T(8,128)S(1)}, f32[2,136,128]{2,1,0:T(8,128)S(1)}, u32[]{:S(2)}, u32[]{:S(2)}) collective-permute-start(f32[2,136,128]{2,1,0:T(8,128)S(1)} %get-tuple-element.26), channel_id=1, source_target_pairs={{0,8},{4,12},{8,0},{12,4},{16,24},{20,28},{24,16},{28,20},{1,9},{5... | collective-permute-start | bytes 417800 | tf_op jit(solution)/shard_map/ppermute | solution.py:423
  8.9 6.6 %copy-start = (bf16[512,2048]{1,0:T(8,128)(2,1)S(1)}, bf16[512,2048]{1,0:T(8,128)(2,1)}, u32[]{:S(2)}) copy-start(bf16[512,2048]{1,0:T(8,128)(2,1)} %k_ref.4) | copy-start | bytes 6291460
  8.9 6.6 %copy-start.1 = (bf16[512,2048]{1,0:T(8,128)(2,1)S(1)}, bf16[512,2048]{1,0:T(8,128)(2,1)}, u32[]{:S(2)}) copy-start(bf16[512,2048]{1,0:T(8,128)(2,1)} %v_ref.4) | copy-start | bytes 6291460
  8.9 9.9 %collective-permute-start.2 = (f32[2,136,128]{2,1,0:T(8,128)S(1)}, f32[2,136,128]{2,1,0:T(8,128)S(1)}, u32[]{:S(2)}, u32[]{:S(2)}) collective-permute-start(f32[2,136,128]{2,1,0:T(8,128)S(1)} %get-tuple-element.27), channel_id=1, source_target_pairs={{0,12},{4,8},{8,4},{12,0},{16,28},{20,24},{24,20},{28,16},{1,13},{... | collective-permute-start | bytes 417800 | tf_op jit(solution)/shard_map/ppermute | solution.py:423
  12.0 17.2 %collective-permute-start.3 = (f32[2,136,128]{2,1,0:T(8,128)S(1)}, f32[2,136,128]{2,1,0:T(8,128)S(1)}, u32[]{:S(2)}, u32[]{:S(2)}) collective-permute-start(f32[2,136,128]{2,1,0:T(8,128)S(1)} %get-tuple-element.29), channel_id=1, source_target_pairs={{0,4},{4,0},{8,12},{12,8},{16,20},{20,16},{24,28},{28,24},{1,5},{5... | collective-permute-start | bytes 417800 | tf_op jit(solution)/shard_map/ppermute | solution.py:423
  13.7 15.5 %collective-permute-start.4 = (f32[2,136,128]{2,1,0:T(8,128)S(1)}, f32[2,136,128]{2,1,0:T(8,128)S(1)}, u32[]{:S(2)}, u32[]{:S(2)}) collective-permute-start(f32[2,136,128]{2,1,0:T(8,128)S(1)} %get-tuple-element.30), channel_id=1, source_target_pairs={{0,8},{4,12},{8,0},{12,4},{16,24},{20,28},{24,16},{28,20},{1,9},{5... | collective-permute-start | bytes 417800 | tf_op jit(solution)/shard_map/ppermute | solution.py:423
  15.3 14.0 %collective-permute-start.5 = (f32[2,136,128]{2,1,0:T(8,128)S(1)}, f32[2,136,128]{2,1,0:T(8,128)S(1)}, u32[]{:S(2)}, u32[]{:S(2)}) collective-permute-start(f32[2,136,128]{2,1,0:T(8,128)S(1)} %get-tuple-element.31), channel_id=1, source_target_pairs={{0,12},{4,8},{8,4},{12,0},{16,28},{20,24},{24,20},{28,16},{1,13},{... | collective-permute-start | bytes 417800 | tf_op jit(solution)/shard_map/ppermute | solution.py:423
  18.9 8.0 %collective-permute-start.6 = (f32[2,128,128]{2,1,0:T(8,128)S(1)}, f32[2,128,128]{2,1,0:T(8,128)S(1)}, u32[]{:S(2)}, u32[]{:S(2)}) collective-permute-start(f32[2,128,128]{2,1,0:T(8,128)S(1)} %group_total.2.refs_0_.refs_4_), channel_id=1, source_target_pairs={{0,16},{4,20},{8,24},{12,28},{16,0},{20,4},{24,8},{28,12},{1,17},{... | collective-permute-start | bytes 393224 | tf_op jit(solution)/shard_map/ppermute | solution.py:428
  22.0 10.9 %copy-start.4 = (bf16[4,128,2048]{2,1,0:T(8,128)(2,1)S(1)}, bf16[4,128,2048]{2,1,0:T(8,128)(2,1)}, u32[]{:S(2)}) copy-start(bf16[4,128,2048]{2,1,0:T(8,128)(2,1)} %v_ref.5) | copy-start | bytes 6291460
  25.3 7.6 %copy-start.3 = (bf16[4,128,2048]{2,1,0:T(8,128)(2,1)S(1)}, bf16[4,128,2048]{2,1,0:T(8,128)(2,1)}, u32[]{:S(2)}) copy-start(bf16[4,128,2048]{2,1,0:T(8,128)(2,1)} %k_ref.5) | copy-start | bytes 6291460
  25.3 7.6 %copy-start.6 = (bf16[2,4,2048]{2,1,0:T(4,128)(2,1)S(1)}, bf16[2,4,2048]{2,1,0:T(4,128)(2,1)}, u32[]{:S(2)}) copy-start(bf16[2,4,2048]{2,1,0:T(4,128)(2,1)} %sk_ref.1) | copy-start | bytes 98308
  25.3 7.6 %copy-start.7 = (bf16[2,4,2048]{2,1,0:T(4,128)(2,1)S(1)}, bf16[2,4,2048]{2,1,0:T(4,128)(2,1)}, u32[]{:S(2)}) copy-start(bf16[2,4,2048]{2,1,0:T(4,128)(2,1)} %sv_ref.1) | copy-start | bytes 98308
  25.3 7.6 %copy-start.9 = (s32[4]{0:T(128)S(1)}, s32[4]{0:T(128)}, u32[]{:S(2)}) copy-start(s32[4]{0:T(128)} %lengths_ref.1) | copy-start | bytes 52
  27.7 12.4 %collective-permute-start.11 = (f32[2,136,128]{2,1,0:T(8,128)S(1)}, f32[2,136,128]{2,1,0:T(8,128)S(1)}, u32[]{:S(2)}, u32[]{:S(2)}) collective-permute-start(f32[2,136,128]{2,1,0:T(8,128)S(1)} %get-tuple-element.37), channel_id=1, source_target_pairs={{0,4},{4,0},{8,12},{12,8},{16,20},{20,16},{24,28},{28,24},{1,5},{5... | collective-permute-start | bytes 417800 | tf_op jit(solution)/shard_map/ppermute | solution.py:423
  29.3 7.4 %collective-permute-start.7 = (f32[2,128,128]{2,1,0:T(8,128)S(1)}, f32[2,128,128]{2,1,0:T(8,128)S(1)}, u32[]{:S(2)}, u32[]{:S(2)}) collective-permute-start(f32[2,128,128]{2,1,0:T(8,128)S(1)} %group_total.3.refs_0_.refs_4_), channel_id=1, source_target_pairs={{0,16},{4,20},{8,24},{12,28},{16,0},{20,4},{24,8},{28,12},{1,17},{... | collective-permute-start | bytes 393224 | tf_op jit(solution)/shard_map/ppermute | solution.py:428
  30.1 10.9 %collective-permute-start.12 = (f32[2,136,128]{2,1,0:T(8,128)S(1)}, f32[2,136,128]{2,1,0:T(8,128)S(1)}, u32[]{:S(2)}, u32[]{:S(2)}) collective-permute-start(f32[2,136,128]{2,1,0:T(8,128)S(1)} %get-tuple-element.38), channel_id=1, source_target_pairs={{0,8},{4,12},{8,0},{12,4},{16,24},{20,28},{24,16},{28,20},{1,9},{5... | collective-permute-start | bytes 417800 | tf_op jit(solution)/shard_map/ppermute | solution.py:423
  32.8 8.2 %collective-permute-start.13 = (f32[2,136,128]{2,1,0:T(8,128)S(1)}, f32[2,136,128]{2,1,0:T(8,128)S(1)}, u32[]{:S(2)}, u32[]{:S(2)}) collective-permute-start(f32[2,136,128]{2,1,0:T(8,128)S(1)} %get-tuple-element.39), channel_id=1, source_target_pairs={{0,12},{4,8},{8,4},{12,0},{16,28},{20,24},{24,20},{28,16},{1,13},{... | collective-permute-start | bytes 417800 | tf_op jit(solution)/shard_map/ppermute | solution.py:423
  37.5 5.4 %collective-permute-start.8 = (f32[2,136,128]{2,1,0:T(8,128)S(1)}, f32[2,136,128]{2,1,0:T(8,128)S(1)}, u32[]{:S(2)}, u32[]{:S(2)}) collective-permute-start(f32[2,136,128]{2,1,0:T(8,128)S(1)} %get-tuple-element.34), channel_id=1, source_target_pairs={{0,4},{4,0},{8,12},{12,8},{16,20},{20,16},{24,28},{28,24},{1,5},{5... | collective-permute-start | bytes 417800 | tf_op jit(solution)/shard_map/ppermute | solution.py:423
  38.1 5.1 %collective-permute-start.9 = (f32[2,136,128]{2,1,0:T(8,128)S(1)}, f32[2,136,128]{2,1,0:T(8,128)S(1)}, u32[]{:S(2)}, u32[]{:S(2)}) collective-permute-start(f32[2,136,128]{2,1,0:T(8,128)S(1)} %get-tuple-element.35), channel_id=1, source_target_pairs={{0,8},{4,12},{8,0},{12,4},{16,24},{20,28},{24,16},{28,20},{1,9},{5... | collective-permute-start | bytes 417800 | tf_op jit(solution)/shard_map/ppermute | solution.py:423
  40.1 6.0 %collective-permute-start.10 = (f32[2,136,128]{2,1,0:T(8,128)S(1)}, f32[2,136,128]{2,1,0:T(8,128)S(1)}, u32[]{:S(2)}, u32[]{:S(2)}) collective-permute-start(f32[2,136,128]{2,1,0:T(8,128)S(1)} %get-tuple-element.36), channel_id=1, source_target_pairs={{0,12},{4,8},{8,4},{12,0},{16,28},{20,24},{24,20},{28,16},{1,13},{... | collective-permute-start | bytes 417800 | tf_op jit(solution)/shard_map/ppermute | solution.py:423
  46.1 5.8 %copy-start.8 = (f32[2048]{0:T(1024)S(1)}, f32[2048]{0:T(1024)}, u32[]{:S(2)}) copy-start(f32[2048]{0:T(1024)} %param.19) | copy-start | bytes 24580
  47.2 1.8 %collective-permute-start.16 = (f32[1,640]{1,0:T(1,128)S(1)}, f32[1,640]{1,0:T(1,128)S(1)}, u32[]{:S(2)}, u32[]{:S(2)}) collective-permute-start(f32[1,640]{1,0:T(1,128)S(1)} %get-tuple-element.41.refs_0_), channel_id=1, source_target_pairs={{0,3},{1,0},{2,1},{3,2},{4,7},{5,4},{6,5},{7,6},{8,11},{9,8},{10,9... | collective-permute-start | bytes 7688 | tf_op jit(solution)/shard_map/ppermute | solution.py:471
  47.3 3.7 %collective-permute-start.15 = (f32[1,640]{1,0:T(1,128)S(1)}, f32[1,640]{1,0:T(1,128)S(1)}, u32[]{:S(2)}, u32[]{:S(2)}) collective-permute-start(f32[1,640]{1,0:T(1,128)S(1)} %get-tuple-element.41.refs_0_), channel_id=1, source_target_pairs={{0,2},{1,3},{2,0},{3,1},{4,6},{5,7},{6,4},{7,5},{8,10},{9,11},{10,... | collective-permute-start | bytes 7688 | tf_op jit(solution)/shard_map/ppermute | solution.py:471
  48.8 3.0 %collective-permute-start.14 = (f32[1,640]{1,0:T(1,128)S(1)}, f32[1,640]{1,0:T(1,128)S(1)}, u32[]{:S(2)}, u32[]{:S(2)}) collective-permute-start(f32[1,640]{1,0:T(1,128)S(1)} %get-tuple-element.41.refs_0_), channel_id=1, source_target_pairs={{0,1},{1,2},{2,3},{3,0},{4,5},{5,6},{6,7},{7,4},{8,9},{9,10},{10,1... | collective-permute-start | bytes 7688 | tf_op jit(solution)/shard_map/ppermute | solution.py:471

commit v3 on v2

--- a/solution.py
+++ b/solution.py
@@ -38,9 +38,14 @@
     return jnp.concatenate([ref[i].astype(F32) for i in range(ref.shape[0])], axis=0)
 
 
-def owned_cols(place_ref, m, first, heads):
+def place(group):
+    rank = lax.axis_index("seq")
+    return lax.rem(rank, group), lax.div(rank, group)
+
+
+def owned_cols(group, m, first, heads):
     wide = heads * HEAD_DIM
-    return pl.ds(pl.multiple_of(first + (place_ref[0] ^ m) * wide, wide), wide)
+    return pl.ds(pl.multiple_of(first + (place(group)[0] ^ m) * wide, wide), wide)
 
 
 def split(x):
@@ -48,60 +53,78 @@
     return high, (x - high.astype(F32)).astype(BF16)
 
 
-def state_kernel(group, first, place_ref, q_ref, k_hbm, v_hbm, *refs):
-    out_refs, (k_buf, v_buf, sems) = refs[:group], refs[group:]
-    heads = out_refs[0].shape[0]
-    order = [*range(1, group), 0]
-    copies = {}
-    for m in order:
-        cols = owned_cols(place_ref, m, first, heads)
-        copies[m] = [
-            pltpu.make_async_copy(k_hbm.at[:, cols], k_buf.at[m], sems.at[m, 0]),
-            pltpu.make_async_copy(v_hbm.at[:, cols], v_buf.at[m], sems.at[m, 1]),
-        ]
-        for copy in copies[m]:
-            copy.start()
-    for m in order:
-        rows = jnp.concatenate(
-            [
-                q_ref[i, :, owned_cols(place_ref, m, first, heads)].astype(F32)
-                for i in range(q_ref.shape[0])
-            ],
-            axis=0,
-        )
-        for copy in copies[m]:
-            copy.wait()
-        for h in range(heads):
-            cols = head_cols(h)
-            out_refs[m][h, :HEAD_DIM, :] = dot(k_buf[m, :, cols], v_buf[m, :, cols], ((0,), (0,)))
-            out_refs[m][h, HEAD_DIM:, :] = rows[:, cols]
-
-
-def block_states(chunk, group, heads, place, keys, values, step_queries):
+def message(out_ref, rows, keys, values):
+    for h in range(out_ref.shape[0]):
+        cols = head_cols(h)
+        out_ref[h, :HEAD_DIM, :] = dot(keys[:, cols], values[:, cols], ((0,), (0,)))
+        out_ref[h, HEAD_DIM:, :] = rows[:, cols]
+
+
+def step_rows(q_ref, cols):
+    return jnp.concatenate([q_ref[i, :, cols].astype(F32) for i in range(q_ref.shape[0])], axis=0)
+
+
+def fetched_state_kernel(group, m, first, q_hbm, k_hbm, v_hbm, out_ref, q_buf, k_buf, v_buf, sems):
+    cols = owned_cols(group, m, first, out_ref.shape[0])
+    copies = [
+        pltpu.make_async_copy(k_hbm.at[:, cols], k_buf, sems.at[0]),
+        pltpu.make_async_copy(v_hbm.at[:, cols], v_buf, sems.at[1]),
+        pltpu.make_async_copy(q_hbm.at[:, :, cols], q_buf, sems.at[2]),
+    ]
+    for copy in copies:
+        copy.start()
+    for copy in copies:
+        copy.wait()
+    message(out_ref, step_rows(q_buf, slice(None)), k_buf[...], v_buf[...])
+
+
+def fetched_states(m, chunk, group, heads, keys, values, step_queries):
     rows = keys.shape[0]
     steps, samples, _ = step_queries.shape
     wide = heads * HEAD_DIM
-    message = (heads, HEAD_DIM + steps * samples, HEAD_DIM)
     hbm = pl.BlockSpec(memory_space=pltpu.HBM)
     return pl.pallas_call(
-        functools.partial(state_kernel, group, chunk * group * wide),
-        in_specs=[SMEM, VMEM, hbm, hbm],
-        out_specs=[VMEM] * group,
-        out_shape=[jax.ShapeDtypeStruct(message, F32)] * group,
+        functools.partial(fetched_state_kernel, group, m, chunk * group * wide),
+        in_specs=[hbm, hbm, hbm],
+        out_specs=VMEM,
+        out_shape=jax.ShapeDtypeStruct((heads, HEAD_DIM + steps * samples, HEAD_DIM), F32),
         scratch_shapes=[
-            pltpu.VMEM((group, rows, wide), keys.dtype),
-            pltpu.VMEM((group, rows, wide), values.dtype),
-            pltpu.SemaphoreType.DMA((group, 2)),
+            pltpu.VMEM((steps, samples, wide), step_queries.dtype),
+            pltpu.VMEM((rows, wide), keys.dtype),
+            pltpu.VMEM((rows, wide), values.dtype),
+            pltpu.SemaphoreType.DMA((3,)),
         ],
         compiler_params=params(),
-        cost_estimate=cost(2 * rows * wide * HEAD_DIM * group, 4 * rows * wide * group),
-        name="block_states",
+        cost_estimate=cost(2 * rows * wide * HEAD_DIM, 4 * rows * wide),
+        name="fetched_states",
     )(
-        place,
-        step_queries,
+        pltpu.with_memory_space_constraint(step_queries, pltpu.HBM),
         pltpu.with_memory_space_constraint(keys, pltpu.HBM),
         pltpu.with_memory_space_constraint(values, pltpu.HBM),
     )
+
+
+def state_kernel(group, owners, first, q_ref, k_ref, v_ref, *refs):
+    out_refs = refs[-len(owners) :]
+    for m, out_ref in zip(owners, out_refs):
+        cols = owned_cols(group, m, first, out_ref.shape[0])
+        message(out_ref, step_rows(q_ref, cols), k_ref[:, cols], v_ref[:, cols])
+
+
+def block_states(owners, chunk, group, heads, keys, values, step_queries, after):
+    rows = keys.shape[0]
+    steps, samples, _ = step_queries.shape
+    wide = heads * HEAD_DIM
+    shape = jax.ShapeDtypeStruct((heads, HEAD_DIM + steps * samples, HEAD_DIM), F32)
+    return pl.pallas_call(
+        functools.partial(state_kernel, group, owners, chunk * group * wide),
+        in_specs=[VMEM, VMEM, VMEM] + [ANY] * len(after),
+        out_specs=[VMEM] * len(owners),
+        out_shape=[shape] * len(owners),
+        compiler_params=params(),
+        cost_estimate=cost(2 * rows * wide * HEAD_DIM * len(owners), 4 * rows * wide * len(owners)),
+        name="block_states",
+    )(step_queries, keys, values, *after)
 
 
 def total_kernel(group, *refs):
@@ -125,10 +148,10 @@
     )(*parts, *after)
 
 
-def prior_kernel(group, others, place_ref, *refs):
+def prior_kernel(group, others, *refs):
     parts, total_ref = refs[:group], refs[group]
     other_refs, out_refs = refs[group + 1 : group + 1 + others], refs[-group:]
-    place, block = place_ref[0], place_ref[1]
+    here, block = place(group)
     heads = parts[0].shape[0]
     for h in range(heads):
         entering = jnp.zeros((HEAD_DIM, HEAD_DIM), F32)
@@ -146,23 +169,23 @@
             for k in range(group):
                 if k != m:
                     prior = prior + jnp.where(
-                        (place ^ k) < (place ^ m), parts[k][h, :HEAD_DIM, :], 0.0
+                        (here ^ k) < (here ^ m), parts[k][h, :HEAD_DIM, :], 0.0
                     )
             out_refs[m][h, :HEAD_DIM, :] = prior
             out_refs[m][h, HEAD_DIM:, :] = raw[m * dec : (m + 1) * dec]
 
 
-def priors(place, parts, total, others, after):
+def priors(parts, total, others, after):
     group = len(parts)
     return pl.pallas_call(
         functools.partial(prior_kernel, group, len(others)),
-        in_specs=[SMEM] + [VMEM] * (group + 1 + len(others)) + [ANY] * len(after),
+        in_specs=[VMEM] * (group + 1 + len(others)) + [ANY] * len(after),
         out_specs=[VMEM] * group,
         out_shape=[jax.ShapeDtypeStruct(parts[0].shape, F32)] * group,
         compiler_params=params(),
         cost_estimate=cost(0, 4 * parts[0].size * (2 * group + 1 + len(others))),
         name="priors",
-    )(place, *parts, total, *others, *after)
+    )(*parts, total, *others, *after)
 
 
 def intra_kernel(tile, first, q_ref, k_ref, v_ref, *refs):
@@ -173,17 +196,16 @@
     )
     for h in range(wide // HEAD_DIM):
         cols = slice(first + h * HEAD_DIM, first + (h + 1) * HEAD_DIM)
-        for i in range(rows // tile):
-            here = slice(i * tile, (i + 1) * tile)
-            query = q_ref[here, cols]
-            scores = dot(query, k_ref[here, cols], ((1,), (1,)))
-            scores = jnp.where(keep, scores, 0.0).astype(BF16)
-            total = dot(scores, v_ref[here, cols])
-            if i:
-                before = slice(0, i * tile)
-                scores = dot(query, k_ref[before, cols], ((1,), (1,))).astype(BF16)
-                total = total + dot(scores, v_ref[before, cols])
-            out_ref[here, head_cols(h)] = total
+        total = None
+        for i in range(0, rows, tile):
+            scores = dot(q_ref[i:, cols], k_ref[i : i + tile, cols], ((1,), (1,)))
+            near = jnp.where(keep, scores[:tile], 0.0).astype(BF16)
+            if i + tile < rows:
+                near = jnp.concatenate([near, scores[tile:].astype(BF16)], axis=0)
+            part = dot(near, v_ref[i : i + tile, cols])
+            total = part if total is None else total + part
+            out_ref[i : i + tile, head_cols(h)] = total[:tile]
+            total = total[tile:]
 
 
 def intra_block(first, wide, queries, keys, values, after):
@@ -221,32 +243,39 @@
     col = lax.broadcasted_iota(jnp.int32, (heads * rows, rows), 1)
     near = (row % samples == col % samples) & (row // samples >= col // samples)
 
+    pair = 2 if heads % 2 == 0 else 1
+    wide = pair * HEAD_DIM
     for top in range(0, width // HEAD_DIM, heads):
         scores = jnp.zeros((tokens, heads * rows), F32)
         step_scores = jnp.zeros((rows, heads * rows), F32)
-        for h in range(heads):
-            cols = head_cols(top + h)
-            query = queries[:, cols]
-            pieces = [jnp.zeros((h * rows, HEAD_DIM), F32)] if h else []
-            pieces.append(query)
-            if h < heads - 1:
-                pieces.append(jnp.zeros(((heads - 1 - h) * rows, HEAD_DIM), F32))
+        for h in range(0, heads, pair):
+            cols = slice((top + h) * HEAD_DIM, (top + h) * HEAD_DIM + wide)
+            pieces = []
+            for p in range(pair):
+                own = [jnp.zeros((rows, HEAD_DIM), F32)] * pair
+                own[p] = queries[:, head_cols(top + h + p)]
+                pieces.append(jnp.concatenate(own, axis=1))
+            if h:
+                pieces.insert(0, jnp.zeros((h * rows, wide), F32))
+            if h + pair < heads:
+                pieces.append(jnp.zeros(((heads - pair - h) * rows, wide), F32))
             placed = jnp.concatenate(pieces, axis=0).astype(BF16)
-            keys = k_ref[:, :, cols].reshape(tokens, HEAD_DIM)
+            keys = k_ref[:, :, cols].reshape(tokens, wide)
             scores = scores + dot(keys, placed, ((1,), (1,)))
             step_scores = step_scores + dot(step_keys[:, cols], placed, ((1,), (1,)))
-        high, low = split(jnp.where(live, scores.T, 0.0))
-        step_high, step_low = split(jnp.where(near, step_scores.T, 0.0))
-        for h in range(heads):
-            cols = head_cols(top + h)
-            own = slice(h * rows, (h + 1) * rows)
-            values = v_ref[:, :, cols].reshape(tokens, HEAD_DIM)
-            out_ref[:, cols] = (
-                dot(high[own], values)
-                + dot(low[own], values)
-                + dot(step_high[own], step_values[:, cols])
-                + dot(step_low[own], step_values[:, cols])
+        halves = split(jnp.where(live, scores.T, 0.0))
+        step_halves = split(jnp.where(near, step_scores.T, 0.0))
+        for h in range(0, heads, pair):
+            cols = slice((top + h) * HEAD_DIM, (top + h) * HEAD_DIM + wide)
+            own = slice(h * rows, (h + pair) * rows)
+            values = v_ref[:, :, cols].reshape(tokens, wide)
+            both = dot(jnp.concatenate([x[own] for x in halves], axis=0), values) + dot(
+                jnp.concatenate([x[own] for x in step_halves], axis=0), step_values[:, cols]
             )
+            for p in range(pair):
+                high = slice(p * rows, (p + 1) * rows)
+                low = slice((pair + p) * rows, (pair + p + 1) * rows)
+                out_ref[:, head_cols(top + h + p)] = both[high, head_cols(p)] + both[low, head_cols(p)]
 
 
 def suffix_part(lengths, step_queries, suffix_keys, suffix_values, step_keys, step_values, after):
@@ -263,7 +292,20 @@
     )(lengths, step_queries, suffix_keys, suffix_values, step_keys, step_values, *after)
 
 
-def attended_kernel(group, top, first, last, place_ref, q_ref, intra_ref, extra_ref, *refs):
+def pick(refs, owner, group, heads):
+    wide = heads * HEAD_DIM
+    if len(refs) == 1:
+        return refs[0][:, pl.ds(pl.multiple_of(owner * wide, wide), wide)]
+    each = group // len(refs)
+    at = pl.ds(pl.multiple_of(owner % each * wide, wide), wide)
+    found = refs[0][:, at]
+    for i in range(1, len(refs)):
+        found = jnp.where(owner // each == i, refs[i][:, at], found)
+    return found
+
+
+def attended_kernel(group, pieces, top, first, last, q_ref, extra_ref, *refs):
+    intra_refs, refs = refs[:pieces], refs[pieces:]
     parts = refs[:group]
     att_ref, raw_ref, sum_ref, acc_ref = refs[-4:]
     rows = q_ref.shape[0]
@@ -274,10 +316,10 @@
     else:
         acc_ref[...] = refs[group][...]
     for m in range(group):
-        all_cols = owned_cols(place_ref, m, top, heads)
-        own_cols = owned_cols(place_ref, m, 0, heads)
+        all_cols = owned_cols(group, m, top, heads)
+        own_cols = owned_cols(group, m, 0, heads)
         query = q_ref[:, all_cols]
-        intra = intra_ref[:, own_cols]
+        intra = pick(intra_refs, place(group)[0] ^ m, group, heads)
         extra = extra_ref[:, all_cols]
         squares = acc_ref[:rows, :]
         raw_squares = acc_ref[rows : rows + dec, :]
@@ -300,16 +342,17 @@
         sum_ref[...] = acc_ref[...]
 
 
-def attend(chunk, last, place, queries, intra, extra, parts, before, after):
+def attend(chunk, last, queries, intra, extra, parts, before, after):
     group = len(parts)
     heads = parts[0].shape[0]
     wide = group * heads * HEAD_DIM
     rows, dec = queries.shape[0], extra.shape[0]
+    pieces = len(intra)
     padded = -(-(rows + dec) // LANES) * LANES
     sums = (1, padded) if last else (padded, LANES)
     return pl.pallas_call(
-        functools.partial(attended_kernel, group, chunk * wide, not before, last),
-        in_specs=[SMEM] + [VMEM] * (3 + group + len(before)) + [ANY] * len(after),
+        functools.partial(attended_kernel, group, pieces, chunk * wide, not before, last),
+        in_specs=[VMEM] * (2 + pieces + group + len(before)) + [ANY] * len(after),
         out_specs=[VMEM] * 3,
         out_shape=[
             jax.ShapeDtypeStruct((rows, wide), F32),
@@ -320,7 +363,7 @@
         compiler_params=params(),
         cost_estimate=cost(2 * rows * wide * HEAD_DIM, 10 * rows * wide),
         name="attend",
-    )(place, queries, intra, extra, *parts, *before, *after)
+    )(queries, extra, *intra, *parts, *before, *after)
 
 
 def norm_kernel(chunks, sums, width, tile, gain_ref, *refs):
@@ -412,16 +455,14 @@
     group = group_size(devices, heads_here)
     blocks = devices // group
     heads = heads_here // (group * CHUNKS)
-    rank = lax.axis_index("seq")
-    place = jnp.stack([rank % group, rank // group]).astype(jnp.int32)
-
     def swap(m):
         return [(i, i // group * group + (i % group ^ m)) for i in range(devices)]
 
-    def exchange(messages):
-        return [messages[0]] + [
-            lax.ppermute(messages[m], "seq", swap(m)) for m in range(1, group)
-        ]
+    def to_group(messages):
+        arrived = list(messages)
+        for m in range(group - 1, 0, -1):
+            arrived[m] = lax.ppermute(messages[m], "seq", swap(m))
+        return arrived
 
     def across(total):
         return [
@@ -429,38 +470,42 @@
             for k in range(1, blocks)
         ]
 
-    wide = width // CHUNKS
-    parts, totals, others, entering, intra = [], [], [], [], []
-    for c in range(CHUNKS):
-        parts.append(exchange(block_states(c, group, heads, place, keys, values, step_queries)))
-    last = [parts[-1][0]]
-    for c in range(CHUNKS):
-        if c == 0 or CHUNKS == 1:
-            last = [intra_block(c * wide, wide, queries, keys, values, last)]
-            intra += last
-        totals.append(group_total(parts[c], last))
-        others.append(across(totals[c]))
-        if c == 0 and CHUNKS > 1:
-            last = [intra_block(wide, width - wide, queries, keys, values, [totals[c]])]
-            intra += last
-        else:
-            extra = suffix_part(
-                suffix_lengths,
-                step_queries,
-                suffix_keys,
-                suffix_values,
-                step_keys,
-                step_values,
-                [totals[c]],
-            )
-            last = [extra]
-        sent = priors(place, parts[c], totals[c], others[c], last)
-        entering.append(exchange(sent))
-        last = [sent[0]]
+    def states(owners, c, after):
+        return block_states(owners, c, group, heads, keys, values, step_queries, after)
+
+    def intra(first, wide, after):
+        return intra_block(first * HEAD_DIM, wide * HEAD_DIM, queries, keys, values, after)
+
+    half = heads_here // CHUNKS
+    first = fetched_states(group - 1, 0, group, heads, keys, values, step_queries)
+    rest = states(list(range(group - 1)), 0, [first])
+    parts = [to_group([*rest, first])]
+    later = states(list(range(group)), 1, [rest[0]])
+    parts.append(to_group(later))
+    totals = [group_total(parts[0], [later[0]])]
+    others = [across(totals[0])]
+    intras = [intra(0, half // 2, [totals[0]])]
+    totals.append(group_total(parts[1], [intras[0]]))
+    others.append(across(totals[1]))
+    intras.append(intra(half // 2, half - half // 2, [totals[1]]))
+    sent = [priors(parts[0], totals[0], others[0], [intras[1]])]
+    entering = [to_group(sent[0])]
+    sent.append(priors(parts[1], totals[1], others[1], [sent[0][0]]))
+    entering.append(to_group(sent[1]))
+    extra = suffix_part(
+        suffix_lengths,
+        step_queries,
+        suffix_keys,
+        suffix_values,
+        step_keys,
+        step_values,
+        [sent[1][0]],
+    )
+    intras = [intras, [intra(half, half, [extra])]]
     atts, raws, sums = [], [], []
     for c in range(CHUNKS):
         att, raw, total = attend(
-            c, c == CHUNKS - 1, place, queries, intra[c], extra, entering[c], sums, last
+            c, c == CHUNKS - 1, queries, intras[c], extra, entering[c], sums, []
         )
         sums = [total]
         atts.append(att)

time: 54.3 us -> 49.8 us (0.917)
  Pallas kernels: 21.4 us -> 13.2 us
  waiting for transfers between devices: 9.3 us -> 12.6 us
  starting transfers between devices: 21.7 us -> 23 us
  local copies, waits for them, and re-layouts: 0.8 us -> 0.05 us
    pallas_call x4 -> x5, Pallas kernels: 8.02 us -> 3.94 us  [the longest x1 1.5 us: fetched_states(): pl.pallas_call(functools.partial(fetched_state_kernel, group, m, chunk *...]
    pallas_call x2 -> x3, Pallas kernels: 6.56 us -> 4.1 us  [intra_block(): pl.pallas_call(functools.partial(intra_kernel, tile, first), in_specs=[VM...]
    ppermute x2, waiting for transfers between devices: 2.4 us -> 4.55 us  [across(): lax.ppermute(total, 'seq', [(i, (i + k * group) % devices) for i in range...]
    ppermute x12, starting transfers between devices: 16 us -> 17.9 us  [to_group(): arrived[m] = lax.ppermute(messages[m], 'seq', swap(m))]
    ppermute x12, waiting for transfers between devices: 4.05 us -> 5.22 us  [to_group(): arrived[m] = lax.ppermute(messages[m], 'seq', swap(m))]
    pallas_call x2, Pallas kernels: 1.59 us -> 0.53 us  [priors(): pl.pallas_call(functools.partial(prior_kernel, group, len(others)), in_sp...]
    unnamed x20, local copies, waits for them, and re-layouts: 0.8 us -> 0.05 us
    pallas_call x1, Pallas kernels: 2.93 us -> 2.29 us  [suffix_part(): pl.pallas_call(suffix_kernel, in_specs=[SMEM] + [VMEM] * 5 + [ANY] * len(...]
  transfers between devices with their start and end apart: 17 -> 17, of which waited for: 7 -> 7; matrix products, arithmetic and copies ran while one was open for 0% -> 0% of each run, Pallas kernels for 28% -> 17%
where the time goes in v3:
time: 49.8 us; the launch traced here: 49.7 us
  starting transfers between devices  23 us (46%)
  Pallas kernels  13.2 us (27%)
  waiting for transfers between devices  12.6 us (25%)
  between operations  0.83 us (2%)
    ppermute x12, starting transfers between devices, to_group(): arrived[m] = lax.ppermute(messages[m], 'seq', swap(m))  17.9 us
    ppermute x12, waiting for transfers between devices, to_group(): arrived[m] = lax.ppermute(messages[m], 'seq', swap(m))  5.22 us
    ppermute x2, waiting for transfers between devices, across(): lax.ppermute(total, 'seq', [(i, (i + k * group) % devices) for i in range...  4.55 us
    pallas_call x3, Pallas kernels, intra_block(): pl.pallas_call(functools.partial(intra_kernel, tile, first), in_specs=[VM...  4.1 us
    ppermute x2, starting transfers between devices, across(): lax.ppermute(total, 'seq', [(i, (i + k * group) % devices) for i in range...  3.29 us
    ppermute x3, waiting for transfers between devices, on_device(): lax.ppermute(sums, 'head', [(i, (i + k) % others_of_row) for i in range(o...  2.85 us
    pallas_call x1, Pallas kernels, suffix_part(): pl.pallas_call(suffix_kernel, in_specs=[SMEM] + [VMEM] * 5 + [ANY] * len(...  2.29 us
    pallas_call x1, Pallas kernels, normalize(): pl.pallas_call(functools.partial(norm_kernel, len(atts), len(sums), width...  2.24 us
  transfers between devices with their start and end apart: 17, of which 7 were waited for; matrix products, arithmetic and copies ran while one was open for 0% of the time, Pallas kernels for 17%

profile of v3, /device:TPU:0, one launch (start us, length us, event | category | flops | bytes accessed | tf_op | source)
XLA Modules:
  0.0 49.7 jit_solution(8255917361700524024)
XLA Ops:
  0.7 1.5 %fetched_states.1.refs_0_ = f32[2,136,128]{2,1,0:T(8,128)S(1)} custom-call(bf16[2,4,2048]{2,1,0:T(4,128)(2,1)} %q_ref.12, bf16[512,2048]{1,0:T(8,128)(2,1)} %k_ref.11, bf16[512,2048]{1,0:T(8,128)(2,1)} %v_ref.11), custom_call_target="tpu_custom_call" | custom-call | flops 33554432 | bytes 524288 | tf_op jit(solution)/shard_map/fetched_states/pallas_call | solution.py:86
  2.2 4.0 %collective-permute-start.5 = (f32[2,136,128]{2,1,0:T(8,128)S(1)}, f32[2,136,128]{2,1,0:T(8,128)S(1)}, u32[]{:S(2)}, u32[]{:S(2)}) collective-permute-start(f32[2,136,128]{2,1,0:T(8,128)S(1)} %fetched_states.1.refs_0_), channel_id=1, source_target_pairs={{0,12},{4,8},{8,4},{12,0},{16,28},{20,24},{24,20},{28,16},{1,13},{... | collective-permute-start | bytes 417800 | tf_op jit(solution)/shard_map/ppermute | solution.py:464
  6.2 0.5 %block_states.2 = (f32[2,136,128]{2,1,0:T(8,128)S(1)}, f32[2,136,128]{2,1,0:T(8,128)S(1)}, f32[2,136,128]{2,1,0:T(8,128)S(1)}) custom-call(bf16[2,4,2048]{2,1,0:T(4,128)(2,1)S(1)} %copy-done.5, bf16[512,2048]{1,0:T(8,128)(2,1)S(1)} %copy-done, bf16[512,2048]{1,0:T(8,128)(2,1)S(1)} %copy-done.1, f32[2,136,128]{2,1,0:T(8,128)S(1)} %fetched_states.1.refs_0_), custom_call_target="tpu_custom_call" | custom-call | flops 100663296 | bytes 1572864 | tf_op jit(solution)/shard_map/block_states/pallas_call | solution.py:119
  6.8 0.6 %collective-permute-start.3 = (f32[2,136,128]{2,1,0:T(8,128)S(1)}, f32[2,136,128]{2,1,0:T(8,128)S(1)}, u32[]{:S(2)}, u32[]{:S(2)}) collective-permute-start(f32[2,136,128]{2,1,0:T(8,128)S(1)} %get-tuple-element.28), channel_id=1, source_target_pairs={{0,4},{4,0},{8,12},{12,8},{16,20},{20,16},{24,28},{28,24},{1,5},{5... | collective-permute-start | bytes 417800 | tf_op jit(solution)/shard_map/ppermute | solution.py:464
  7.3 0.8 %collective-permute-start.4 = (f32[2,136,128]{2,1,0:T(8,128)S(1)}, f32[2,136,128]{2,1,0:T(8,128)S(1)}, u32[]{:S(2)}, u32[]{:S(2)}) collective-permute-start(f32[2,136,128]{2,1,0:T(8,128)S(1)} %get-tuple-element.29), channel_id=1, source_target_pairs={{0,8},{4,12},{8,0},{12,4},{16,24},{20,28},{24,16},{28,20},{1,9},{5... | collective-permute-start | bytes 417800 | tf_op jit(solution)/shard_map/ppermute | solution.py:464
  8.2 0.6 %block_states.3 = (f32[2,136,128]{2,1,0:T(8,128)S(1)}, f32[2,136,128]{2,1,0:T(8,128)S(1)}, f32[2,136,128]{2,1,0:T(8,128)S(1)}, f32[2,136,128]{2,1,0:T(8,128)S(1)}) custom-call(bf16[2,4,2048]{2,1,0:T(4,128)(2,1)S(1)} %copy-done.5, bf16[512,2048]{1,0:T(8,128)(2,1)S(1)} %copy-done, bf16[512,2048]{1,0:T(8,128)(2,1)S(1)} %copy-done.1, ...), custom_call_target="tpu_custom_call" | custom-call | flops 134217728 | bytes 2097152 | tf_op jit(solution)/shard_map/block_states/pallas_call | solution.py:119
  8.8 1.2 %collective-permute-start = (f32[2,136,128]{2,1,0:T(8,128)S(1)}, f32[2,136,128]{2,1,0:T(8,128)S(1)}, u32[]{:S(2)}, u32[]{:S(2)}) collective-permute-start(f32[2,136,128]{2,1,0:T(8,128)S(1)} %get-tuple-element.25), channel_id=1, source_target_pairs={{0,4},{4,0},{8,12},{12,8},{16,20},{20,16},{24,28},{28,24},{1,5},{5... | collective-permute-start | bytes 417800 | tf_op jit(solution)/shard_map/ppermute | solution.py:464
  10.0 1.6 %collective-permute-start.1 = (f32[2,136,128]{2,1,0:T(8,128)S(1)}, f32[2,136,128]{2,1,0:T(8,128)S(1)}, u32[]{:S(2)}, u32[]{:S(2)}) collective-permute-start(f32[2,136,128]{2,1,0:T(8,128)S(1)} %get-tuple-element.26), channel_id=1, source_target_pairs={{0,8},{4,12},{8,0},{12,4},{16,24},{20,28},{24,16},{28,20},{1,9},{5... | collective-permute-start | bytes 417800 | tf_op jit(solution)/shard_map/ppermute | solution.py:464
  11.6 2.1 %collective-permute-start.2 = (f32[2,136,128]{2,1,0:T(8,128)S(1)}, f32[2,136,128]{2,1,0:T(8,128)S(1)}, u32[]{:S(2)}, u32[]{:S(2)}) collective-permute-start(f32[2,136,128]{2,1,0:T(8,128)S(1)} %get-tuple-element.27), channel_id=1, source_target_pairs={{0,12},{4,8},{8,4},{12,0},{16,28},{20,24},{24,20},{28,16},{1,13},{... | collective-permute-start | bytes 417800 | tf_op jit(solution)/shard_map/ppermute | solution.py:464
  13.7 0.2 collective-permute-done.4.refs_2_
  13.9 2.7 %collective-permute-start.7 = (f32[2,128,128]{2,1,0:T(8,128)S(1)}, f32[2,128,128]{2,1,0:T(8,128)S(1)}, u32[]{:S(2)}, u32[]{:S(2)}) collective-permute-start(f32[2,128,128]{2,1,0:T(8,128)S(1)} %group_total.2.refs_0_.refs_4_), channel_id=1, source_target_pairs={{0,16},{4,20},{8,24},{12,28},{16,0},{20,4},{24,8},{28,12},{1,17},{... | collective-permute-start | bytes 393224 | tf_op jit(solution)/shard_map/ppermute | solution.py:469
  16.6 1.1 %intra_block.3.refs_4_.refs_0_ = f32[512,512]{1,0:T(8,128)S(1)} custom-call(bf16[512,2048]{1,0:T(8,128)(2,1)S(1)} %copy-done.2, bf16[512,2048]{1,0:T(8,128)(2,1)S(1)} %copy-done, bf16[512,2048]{1,0:T(8,128)(2,1)S(1)} %copy-done.1, f32[2,128,128]{2,1,0:T(8,128)S(1)} %group_total.2.refs_0_.refs_4_), custom_call_target="tpu_custom_call" | custom-call | flops 536870912 | bytes 2621440 | tf_op jit(solution)/shard_map/intra_block/pallas_call | solution.py:214
  17.7 0.6 %collective-permute-done.1.refs_2_ = f32[2,136,128]{2,1,0:T(8,128)S(1)} collective-permute-done((f32[2,136,128]{2,1,0:T(8,128)S(1)}, f32[2,136,128]{2,1,0:T(8,128)S(1)}, u32[]{:S(2)}, u32[]{:S(2)}) %collective-permute-start.1) | collective-permute-done | bytes 139296 | tf_op jit(solution)/shard_map/ppermute | solution.py:464
  18.3 3.8 %collective-permute-done.2.refs_3_ = f32[2,136,128]{2,1,0:T(8,128)S(1)} collective-permute-done((f32[2,136,128]{2,1,0:T(8,128)S(1)}, f32[2,136,128]{2,1,0:T(8,128)S(1)}, u32[]{:S(2)}, u32[]{:S(2)}) %collective-permute-start.2) | collective-permute-done | bytes 139296 | tf_op jit(solution)/shard_map/ppermute | solution.py:464
  22.2 1.1 %intra_block.4.refs_6_.refs_1_ = f32[512,512]{1,0:T(8,128)S(1)} custom-call(bf16[512,2048]{1,0:T(8,128)(2,1)S(1)} %copy-done.2, bf16[512,2048]{1,0:T(8,128)(2,1)S(1)} %copy-done, bf16[512,2048]{1,0:T(8,128)(2,1)S(1)} %copy-done.1, f32[2,128,128]{2,1,0:T(8,128)S(1)} %group_total.3.refs_0_.refs_4_), custom_call_target="tpu_custom_call" | custom-call | flops 536870912 | bytes 2621440 | tf_op jit(solution)/shard_map/intra_block/pallas_call | solution.py:214
  23.3 0.3 priors.2
  23.6 1.2 %collective-permute-start.11 = (f32[2,136,128]{2,1,0:T(8,128)S(1)}, f32[2,136,128]{2,1,0:T(8,128)S(1)}, u32[]{:S(2)}, u32[]{:S(2)}) collective-permute-start(f32[2,136,128]{2,1,0:T(8,128)S(1)} %get-tuple-element.35), channel_id=1, source_target_pairs={{0,4},{4,0},{8,12},{12,8},{16,20},{20,16},{24,28},{28,24},{1,5},{5... | collective-permute-start | bytes 417800 | tf_op jit(solution)/shard_map/ppermute | solution.py:464
  24.8 0.6 %collective-permute-start.6 = (f32[2,128,128]{2,1,0:T(8,128)S(1)}, f32[2,128,128]{2,1,0:T(8,128)S(1)}, u32[]{:S(2)}, u32[]{:S(2)}) collective-permute-start(f32[2,128,128]{2,1,0:T(8,128)S(1)} %group_total.3.refs_0_.refs_4_), channel_id=1, source_target_pairs={{0,16},{4,20},{8,24},{12,28},{16,0},{20,4},{24,8},{28,12},{1,17},{... | collective-permute-start | bytes 393224 | tf_op jit(solution)/shard_map/ppermute | solution.py:469
  25.4 2.8 %collective-permute-start.12 = (f32[2,136,128]{2,1,0:T(8,128)S(1)}, f32[2,136,128]{2,1,0:T(8,128)S(1)}, u32[]{:S(2)}, u32[]{:S(2)}) collective-permute-start(f32[2,136,128]{2,1,0:T(8,128)S(1)} %get-tuple-element.36), channel_id=1, source_target_pairs={{0,8},{4,12},{8,0},{12,4},{16,24},{20,28},{24,16},{28,20},{1,9},{5... | collective-permute-start | bytes 417800 | tf_op jit(solution)/shard_map/ppermute | solution.py:464
  28.3 4.5 %collective-permute-done.6.refs_5_ = f32[2,128,128]{2,1,0:T(8,128)S(1)} collective-permute-done((f32[2,128,128]{2,1,0:T(8,128)S(1)}, f32[2,128,128]{2,1,0:T(8,128)S(1)}, u32[]{:S(2)}, u32[]{:S(2)}) %collective-permute-start.6) | collective-permute-done | bytes 131104 | tf_op jit(solution)/shard_map/ppermute | solution.py:469
  32.8 0.3 priors.3
  33.1 1.2 %collective-permute-start.9 = (f32[2,136,128]{2,1,0:T(8,128)S(1)}, f32[2,136,128]{2,1,0:T(8,128)S(1)}, u32[]{:S(2)}, u32[]{:S(2)}) collective-permute-start(f32[2,136,128]{2,1,0:T(8,128)S(1)} %get-tuple-element.33), channel_id=1, source_target_pairs={{0,8},{4,12},{8,0},{12,4},{16,24},{20,28},{24,16},{28,20},{1,9},{5... | collective-permute-start | bytes 417800 | tf_op jit(solution)/shard_map/ppermute | solution.py:464
  34.3 2.3 %collective-permute-start.10 = (f32[2,136,128]{2,1,0:T(8,128)S(1)}, f32[2,136,128]{2,1,0:T(8,128)S(1)}, u32[]{:S(2)}, u32[]{:S(2)}) collective-permute-start(f32[2,136,128]{2,1,0:T(8,128)S(1)} %get-tuple-element.34), channel_id=1, source_target_pairs={{0,12},{4,8},{8,4},{12,0},{16,28},{20,24},{24,20},{28,16},{1,13},{... | collective-permute-start | bytes 417800 | tf_op jit(solution)/shard_map/ppermute | solution.py:464
  36.6 2.3 %suffix_part.1.refs_0_.extra_ref = f32[8,2048]{1,0:T(8,128)S(1)} custom-call(s32[4]{0:T(128)S(1)} %copy-done.9, bf16[2,4,2048]{2,1,0:T(4,128)(2,1)S(1)} %copy-done.5, bf16[4,128,2048]{2,1,0:T(8,128)(2,1)S(1)} %copy-done.3, bf16[4,128,2048]{2,1,0:T(8,128)(2,1)S(1)} %copy-done.4, bf16[2,4,2048]{2,1,0:T(4,128)(2,1)S(1)} %copy-done.6, ...), custom_call_target="tpu_custom_call" | custom-call | flops 67108864 | bytes 4194304 | tf_op jit(solution)/shard_map/suffix_part/pallas_call | solution.py:284
  38.9 1.9 %intra_block.5.refs_0_ = f32[512,1024]{1,0:T(8,128)S(1)} custom-call(bf16[512,2048]{1,0:T(8,128)(2,1)S(1)} %copy-done.2, bf16[512,2048]{1,0:T(8,128)(2,1)S(1)} %copy-done, bf16[512,2048]{1,0:T(8,128)(2,1)S(1)} %copy-done.1, f32[8,2048]{1,0:T(8,128)S(1)} %suffix_part.1.refs_0_.extra_ref), custom_call_target="tpu_custom_call" | custom-call | flops 1073741824 | bytes 5242880 | tf_op jit(solution)/shard_map/intra_block/pallas_call | solution.py:214
  40.9 0.7 %attend.2 = (f32[512,1024]{1,0:T(8,128)S(1)}, f32[8,1024]{1,0:T(8,128)S(1)}, f32[640,128]{1,0:T(8,128)S(1)}) custom-call(bf16[512,2048]{1,0:T(8,128)(2,1)S(1)} %copy-done.2, f32[8,2048]{1,0:T(8,128)S(1)} %suffix_part.1.refs_0_.extra_ref, f32[512,512]{1,0:T(8,128)S(1)} %intra_block.3.refs_4_.refs_0_, f32[512,512]{1,0:T(8,128)S(1)} %intra_block.4.refs_6_.refs_1_, ...), custom_call_target="tpu_custom_call" | custom-call | flops 134217728 | bytes 5242880 | tf_op jit(solution)/shard_map/attend/pallas_call | solution.py:353
  41.6 0.6 %collective-permute-done.10.refs_4_ = f32[2,136,128]{2,1,0:T(8,128)S(1)} collective-permute-done((f32[2,136,128]{2,1,0:T(8,128)S(1)}, f32[2,136,128]{2,1,0:T(8,128)S(1)}, u32[]{:S(2)}, u32[]{:S(2)}) %collective-permute-start.10) | collective-permute-done | bytes 139296 | tf_op jit(solution)/shard_map/ppermute | solution.py:464
  42.2 0.6 %attend.3 = (f32[512,1024]{1,0:T(8,128)S(1)}, f32[8,1024]{1,0:T(8,128)S(1)}, f32[1,640]{1,0:T(1,128)S(1)}) custom-call(bf16[512,2048]{1,0:T(8,128)(2,1)S(1)} %copy-done.2, f32[8,2048]{1,0:T(8,128)S(1)} %suffix_part.1.refs_0_.extra_ref, f32[512,1024]{1,0:T(8,128)S(1)} %intra_block.5.refs_0_, f32[2,136,128]{2,1,0:T(8,128)S(1)} %get-tuple-element.31.refs_0_.refs_1_, ...), custom_call_target="tpu_custom_call" | custom-call | flops 134217728 | bytes 5242880 | tf_op jit(solution)/shard_map/attend/pallas_call | solution.py:353
  42.8 1.6 %collective-permute-start.15 = (f32[1,640]{1,0:T(1,128)S(1)}, f32[1,640]{1,0:T(1,128)S(1)}, u32[]{:S(2)}, u32[]{:S(2)}) collective-permute-start(f32[1,640]{1,0:T(1,128)S(1)} %get-tuple-element.39.refs_0_), channel_id=1, source_target_pairs={{0,2},{1,3},{2,0},{3,1},{4,6},{5,7},{6,4},{7,5},{8,10},{9,11},{10,... | collective-permute-start | bytes 7688 | tf_op jit(solution)/shard_map/ppermute | solution.py:516
  44.6 1.9 %collective-permute-done.15.refs_2_ = f32[1,640]{1,0:T(1,128)S(1)} collective-permute-done((f32[1,640]{1,0:T(1,128)S(1)}, f32[1,640]{1,0:T(1,128)S(1)}, u32[]{:S(2)}, u32[]{:S(2)}) %collective-permute-start.15) | collective-permute-done | bytes 2592 | tf_op jit(solution)/shard_map/ppermute | solution.py:516
  46.5 0.9 %collective-permute-done.14.refs_1_ = f32[1,640]{1,0:T(1,128)S(1)} collective-permute-done((f32[1,640]{1,0:T(1,128)S(1)}, f32[1,640]{1,0:T(1,128)S(1)}, u32[]{:S(2)}, u32[]{:S(2)}) %collective-permute-start.14) | collective-permute-done | bytes 2592 | tf_op jit(solution)/shard_map/ppermute | solution.py:516
  47.4 2.2 %normalize.1 = (bf16[512,2048]{1,0:T(8,128)(2,1)}, bf16[2,4,2048]{2,1,0:T(4,128)(2,1)}) custom-call(f32[1,2048]{1,0:T(1,128)S(1)} %bitcast.1, f32[1,640]{1,0:T(1,128)S(1)} %get-tuple-element.39.refs_0_, f32[1,640]{1,0:T(1,128)S(1)} %collective-permute-done.14.refs_1_, f32[1,640]{1,0:T(1,128)S(1)} %collective-permute-done.15.refs_2_, ...), custom_call_target="tpu_custom_call" | custom-call | bytes 6291456 | tf_op jit(solution)/shard_map/normalize/pallas_call | solution.py:410
  (36 shorter events, 0.5 us)
Async XLA Ops:
  0.6 5.6 %copy-start.1 = (bf16[512,2048]{1,0:T(8,128)(2,1)S(1)}, bf16[512,2048]{1,0:T(8,128)(2,1)}, u32[]{:S(2)}) copy-start(bf16[512,2048]{1,0:T(8,128)(2,1)} %v_ref.11) | copy-start | bytes 6291460
  0.6 5.6 %copy-start = (bf16[512,2048]{1,0:T(8,128)(2,1)S(1)}, bf16[512,2048]{1,0:T(8,128)(2,1)}, u32[]{:S(2)}) copy-start(bf16[512,2048]{1,0:T(8,128)(2,1)} %k_ref.11) | copy-start | bytes 6291460
  0.7 5.6 %copy-start.5 = (bf16[2,4,2048]{2,1,0:T(4,128)(2,1)S(1)}, bf16[2,4,2048]{2,1,0:T(4,128)(2,1)}, u32[]{:S(2)}) copy-start(bf16[2,4,2048]{2,1,0:T(4,128)(2,1)} %q_ref.12) | copy-start | bytes 98308
  2.2 9.4 %collective-permute-start.5 = (f32[2,136,128]{2,1,0:T(8,128)S(1)}, f32[2,136,128]{2,1,0:T(8,128)S(1)}, u32[]{:S(2)}, u32[]{:S(2)}) collective-permute-start(f32[2,136,128]{2,1,0:T(8,128)S(1)} %fetched_states.1.refs_0_), channel_id=1, source_target_pairs={{0,12},{4,8},{8,4},{12,0},{16,28},{20,24},{24,20},{28,16},{1,13},{... | collective-permute-start | bytes 417800 | tf_op jit(solution)/shard_map/ppermute | solution.py:464
  6.8 6.9 %collective-permute-start.3 = (f32[2,136,128]{2,1,0:T(8,128)S(1)}, f32[2,136,128]{2,1,0:T(8,128)S(1)}, u32[]{:S(2)}, u32[]{:S(2)}) collective-permute-start(f32[2,136,128]{2,1,0:T(8,128)S(1)} %get-tuple-element.28), channel_id=1, source_target_pairs={{0,4},{4,0},{8,12},{12,8},{16,20},{20,16},{24,28},{28,24},{1,5},{5... | collective-permute-start | bytes 417800 | tf_op jit(solution)/shard_map/ppermute | solution.py:464
  7.3 6.6 %collective-permute-start.4 = (f32[2,136,128]{2,1,0:T(8,128)S(1)}, f32[2,136,128]{2,1,0:T(8,128)S(1)}, u32[]{:S(2)}, u32[]{:S(2)}) collective-permute-start(f32[2,136,128]{2,1,0:T(8,128)S(1)} %get-tuple-element.29), channel_id=1, source_target_pairs={{0,8},{4,12},{8,0},{12,4},{16,24},{20,28},{24,16},{28,20},{1,9},{5... | collective-permute-start | bytes 417800 | tf_op jit(solution)/shard_map/ppermute | solution.py:464
  8.2 8.4 %copy-start.2 = (bf16[512,2048]{1,0:T(8,128)(2,1)S(1)}, bf16[512,2048]{1,0:T(8,128)(2,1)}, u32[]{:S(2)}) copy-start(bf16[512,2048]{1,0:T(8,128)(2,1)} %q_ref.15) | copy-start | bytes 6291460
  8.8 8.9 %collective-permute-start = (f32[2,136,128]{2,1,0:T(8,128)S(1)}, f32[2,136,128]{2,1,0:T(8,128)S(1)}, u32[]{:S(2)}, u32[]{:S(2)}) collective-permute-start(f32[2,136,128]{2,1,0:T(8,128)S(1)} %get-tuple-element.25), channel_id=1, source_target_pairs={{0,4},{4,0},{8,12},{12,8},{16,20},{20,16},{24,28},{28,24},{1,5},{5... | collective-permute-start | bytes 417800 | tf_op jit(solution)/shard_map/ppermute | solution.py:464
  10.0 8.3 %collective-permute-start.1 = (f32[2,136,128]{2,1,0:T(8,128)S(1)}, f32[2,136,128]{2,1,0:T(8,128)S(1)}, u32[]{:S(2)}, u32[]{:S(2)}) collective-permute-start(f32[2,136,128]{2,1,0:T(8,128)S(1)} %get-tuple-element.26), channel_id=1, source_target_pairs={{0,8},{4,12},{8,0},{12,4},{16,24},{20,28},{24,16},{28,20},{1,9},{5... | collective-permute-start | bytes 417800 | tf_op jit(solution)/shard_map/ppermute | solution.py:464
  11.6 10.5 %collective-permute-start.2 = (f32[2,136,128]{2,1,0:T(8,128)S(1)}, f32[2,136,128]{2,1,0:T(8,128)S(1)}, u32[]{:S(2)}, u32[]{:S(2)}) collective-permute-start(f32[2,136,128]{2,1,0:T(8,128)S(1)} %get-tuple-element.27), channel_id=1, source_target_pairs={{0,12},{4,8},{8,4},{12,0},{16,28},{20,24},{24,20},{28,16},{1,13},{... | collective-permute-start | bytes 417800 | tf_op jit(solution)/shard_map/ppermute | solution.py:464
  13.9 9.4 %collective-permute-start.7 = (f32[2,128,128]{2,1,0:T(8,128)S(1)}, f32[2,128,128]{2,1,0:T(8,128)S(1)}, u32[]{:S(2)}, u32[]{:S(2)}) collective-permute-start(f32[2,128,128]{2,1,0:T(8,128)S(1)} %group_total.2.refs_0_.refs_4_), channel_id=1, source_target_pairs={{0,16},{4,20},{8,24},{12,28},{16,0},{20,4},{24,8},{28,12},{1,17},{... | collective-permute-start | bytes 393224 | tf_op jit(solution)/shard_map/ppermute | solution.py:469
  22.2 14.4 %copy-start.4 = (bf16[4,128,2048]{2,1,0:T(8,128)(2,1)S(1)}, bf16[4,128,2048]{2,1,0:T(8,128)(2,1)}, u32[]{:S(2)}) copy-start(bf16[4,128,2048]{2,1,0:T(8,128)(2,1)} %v_ref.10) | copy-start | bytes 6291460
  23.3 13.3 %copy-start.3 = (bf16[4,128,2048]{2,1,0:T(8,128)(2,1)S(1)}, bf16[4,128,2048]{2,1,0:T(8,128)(2,1)}, u32[]{:S(2)}) copy-start(bf16[4,128,2048]{2,1,0:T(8,128)(2,1)} %k_ref.10) | copy-start | bytes 6291460
  23.3 13.3 %copy-start.6 = (bf16[2,4,2048]{2,1,0:T(4,128)(2,1)S(1)}, bf16[2,4,2048]{2,1,0:T(4,128)(2,1)}, u32[]{:S(2)}) copy-start(bf16[2,4,2048]{2,1,0:T(4,128)(2,1)} %sk_ref.1) | copy-start | bytes 98308
  23.3 13.3 %copy-start.7 = (bf16[2,4,2048]{2,1,0:T(4,128)(2,1)S(1)}, bf16[2,4,2048]{2,1,0:T(4,128)(2,1)}, u32[]{:S(2)}) copy-start(bf16[2,4,2048]{2,1,0:T(4,128)(2,1)} %sv_ref.1) | copy-start | bytes 98308
  23.3 13.3 %copy-start.9 = (s32[4]{0:T(128)S(1)}, s32[4]{0:T(128)}, u32[]{:S(2)}) copy-start(s32[4]{0:T(128)} %lengths_ref.1) | copy-start | bytes 52
  23.6 10.7 %collective-permute-start.11 = (f32[2,136,128]{2,1,0:T(8,128)S(1)}, f32[2,136,128]{2,1,0:T(8,128)S(1)}, u32[]{:S(2)}, u32[]{:S(2)}) collective-permute-start(f32[2,136,128]{2,1,0:T(8,128)S(1)} %get-tuple-element.35), channel_id=1, source_target_pairs={{0,4},{4,0},{8,12},{12,8},{16,20},{20,16},{24,28},{28,24},{1,5},{5... | collective-permute-start | bytes 417800 | tf_op jit(solution)/shard_map/ppermute | solution.py:464
  24.8 8.1 %collective-permute-start.6 = (f32[2,128,128]{2,1,0:T(8,128)S(1)}, f32[2,128,128]{2,1,0:T(8,128)S(1)}, u32[]{:S(2)}, u32[]{:S(2)}) collective-permute-start(f32[2,128,128]{2,1,0:T(8,128)S(1)} %group_total.3.refs_0_.refs_4_), channel_id=1, source_target_pairs={{0,16},{4,20},{8,24},{12,28},{16,0},{20,4},{24,8},{28,12},{1,17},{... | collective-permute-start | bytes 393224 | tf_op jit(solution)/shard_map/ppermute | solution.py:469
  25.4 15.5 %collective-permute-start.12 = (f32[2,136,128]{2,1,0:T(8,128)S(1)}, f32[2,136,128]{2,1,0:T(8,128)S(1)}, u32[]{:S(2)}, u32[]{:S(2)}) collective-permute-start(f32[2,136,128]{2,1,0:T(8,128)S(1)} %get-tuple-element.36), channel_id=1, source_target_pairs={{0,8},{4,12},{8,0},{12,4},{16,24},{20,28},{24,16},{28,20},{1,9},{5... | collective-permute-start | bytes 417800 | tf_op jit(solution)/shard_map/ppermute | solution.py:464
  28.2 12.6 %collective-permute-start.13 = (f32[2,136,128]{2,1,0:T(8,128)S(1)}, f32[2,136,128]{2,1,0:T(8,128)S(1)}, u32[]{:S(2)}, u32[]{:S(2)}) collective-permute-start(f32[2,136,128]{2,1,0:T(8,128)S(1)} %get-tuple-element.37), channel_id=1, source_target_pairs={{0,12},{4,8},{8,4},{12,0},{16,28},{20,24},{24,20},{28,16},{1,13},{... | collective-permute-start | bytes 417800 | tf_op jit(solution)/shard_map/ppermute | solution.py:464
  33.1 8.5 %collective-permute-start.8 = (f32[2,136,128]{2,1,0:T(8,128)S(1)}, f32[2,136,128]{2,1,0:T(8,128)S(1)}, u32[]{:S(2)}, u32[]{:S(2)}) collective-permute-start(f32[2,136,128]{2,1,0:T(8,128)S(1)} %get-tuple-element.32), channel_id=1, source_target_pairs={{0,4},{4,0},{8,12},{12,8},{16,20},{20,16},{24,28},{28,24},{1,5},{5... | collective-permute-start | bytes 417800 | tf_op jit(solution)/shard_map/ppermute | solution.py:464
  33.1 8.5 %collective-permute-start.9 = (f32[2,136,128]{2,1,0:T(8,128)S(1)}, f32[2,136,128]{2,1,0:T(8,128)S(1)}, u32[]{:S(2)}, u32[]{:S(2)}) collective-permute-start(f32[2,136,128]{2,1,0:T(8,128)S(1)} %get-tuple-element.33), channel_id=1, source_target_pairs={{0,8},{4,12},{8,0},{12,4},{16,24},{20,28},{24,16},{28,20},{1,9},{5... | collective-permute-start | bytes 417800 | tf_op jit(solution)/shard_map/ppermute | solution.py:464
  34.3 7.8 %collective-permute-start.10 = (f32[2,136,128]{2,1,0:T(8,128)S(1)}, f32[2,136,128]{2,1,0:T(8,128)S(1)}, u32[]{:S(2)}, u32[]{:S(2)}) collective-permute-start(f32[2,136,128]{2,1,0:T(8,128)S(1)} %get-tuple-element.34), channel_id=1, source_target_pairs={{0,12},{4,8},{8,4},{12,0},{16,28},{20,24},{24,20},{28,16},{1,13},{... | collective-permute-start | bytes 417800 | tf_op jit(solution)/shard_map/ppermute | solution.py:464
  42.2 5.3 %copy-start.8 = (f32[2048]{0:T(1024)S(1)}, f32[2048]{0:T(1024)}, u32[]{:S(2)}) copy-start(f32[2048]{0:T(1024)} %param.19) | copy-start | bytes 24580
  42.7 1.8 %collective-permute-start.16 = (f32[1,640]{1,0:T(1,128)S(1)}, f32[1,640]{1,0:T(1,128)S(1)}, u32[]{:S(2)}, u32[]{:S(2)}) collective-permute-start(f32[1,640]{1,0:T(1,128)S(1)} %get-tuple-element.39.refs_0_), channel_id=1, source_target_pairs={{0,3},{1,0},{2,1},{3,2},{4,7},{5,4},{6,5},{7,6},{8,11},{9,8},{10,9... | collective-permute-start | bytes 7688 | tf_op jit(solution)/shard_map/ppermute | solution.py:516
  42.8 3.7 %collective-permute-start.15 = (f32[1,640]{1,0:T(1,128)S(1)}, f32[1,640]{1,0:T(1,128)S(1)}, u32[]{:S(2)}, u32[]{:S(2)}) collective-permute-start(f32[1,640]{1,0:T(1,128)S(1)} %get-tuple-element.39.refs_0_), channel_id=1, source_target_pairs={{0,2},{1,3},{2,0},{3,1},{4,6},{5,7},{6,4},{7,5},{8,10},{9,11},{10,... | collective-permute-start | bytes 7688 | tf_op jit(solution)/shard_map/ppermute | solution.py:516
  44.4 3.0 %collective-permute-start.14 = (f32[1,640]{1,0:T(1,128)S(1)}, f32[1,640]{1,0:T(1,128)S(1)}, u32[]{:S(2)}, u32[]{:S(2)}) collective-permute-start(f32[1,640]{1,0:T(1,128)S(1)} %get-tuple-element.39.refs_0_), channel_id=1, source_target_pairs={{0,1},{1,2},{2,3},{3,0},{4,5},{5,6},{6,7},{7,4},{8,9},{9,10},{10,1... | collective-permute-start | bytes 7688 | tf_op jit(solution)/shard_map/ppermute | solution.py:516

commit v4 on v3

--- a/solution.py
+++ b/solution.py
@@ -9,7 +9,6 @@
 
 HEAD_DIM = 128
 LANES = 128
-CHUNKS = 2
 F32 = jnp.float32
 BF16 = jnp.bfloat16
 VMEM_LIMIT = 24 * 1024 * 1024
@@ -43,9 +42,10 @@
     return lax.rem(rank, group), lax.div(rank, group)
 
 
-def owned_cols(group, m, first, heads):
-    wide = heads * HEAD_DIM
-    return pl.ds(pl.multiple_of(first + (place(group)[0] ^ m) * wide, wide), wide)
+def owned_cols(group, m, each, heads):
+    lo, hi = heads
+    first = ((place(group)[0] ^ m) * each + lo) * HEAD_DIM
+    return pl.ds(pl.multiple_of(first, HEAD_DIM), (hi - lo) * HEAD_DIM)
 
 
 def split(x):
@@ -64,8 +64,8 @@
     return jnp.concatenate([q_ref[i, :, cols].astype(F32) for i in range(q_ref.shape[0])], axis=0)
 
 
-def fetched_state_kernel(group, m, first, q_hbm, k_hbm, v_hbm, out_ref, q_buf, k_buf, v_buf, sems):
-    cols = owned_cols(group, m, first, out_ref.shape[0])
+def fetched_state_kernel(group, m, each, heads, q_hbm, k_hbm, v_hbm, out_ref, q_buf, k_buf, v_buf, sems):
+    cols = owned_cols(group, m, each, heads)
     copies = [
         pltpu.make_async_copy(k_hbm.at[:, cols], k_buf, sems.at[0]),
         pltpu.make_async_copy(v_hbm.at[:, cols], v_buf, sems.at[1]),
@@ -78,16 +78,17 @@
     message(out_ref, step_rows(q_buf, slice(None)), k_buf[...], v_buf[...])
 
 
-def fetched_states(m, chunk, group, heads, keys, values, step_queries):
+def fetched_states(m, group, each, heads, keys, values, step_queries):
     rows = keys.shape[0]
     steps, samples, _ = step_queries.shape
-    wide = heads * HEAD_DIM
+    count = heads[1] - heads[0]
+    wide = count * HEAD_DIM
     hbm = pl.BlockSpec(memory_space=pltpu.HBM)
     return pl.pallas_call(
-        functools.partial(fetched_state_kernel, group, m, chunk * group * wide),
+        functools.partial(fetched_state_kernel, group, m, each, heads),
         in_specs=[hbm, hbm, hbm],
         out_specs=VMEM,
-        out_shape=jax.ShapeDtypeStruct((heads, HEAD_DIM + steps * samples, HEAD_DIM), F32),
+        out_shape=jax.ShapeDtypeStruct((count, HEAD_DIM + steps * samples, HEAD_DIM), F32),
         scratch_shapes=[
             pltpu.VMEM((steps, samples, wide), step_queries.dtype),
             pltpu.VMEM((rows, wide), keys.dtype),
@@ -104,20 +105,21 @@
     )
 
 
-def state_kernel(group, owners, first, q_ref, k_ref, v_ref, *refs):
+def state_kernel(group, owners, each, heads, q_ref, k_ref, v_ref, *refs):
     out_refs = refs[-len(owners) :]
     for m, out_ref in zip(owners, out_refs):
-        cols = owned_cols(group, m, first, out_ref.shape[0])
+        cols = owned_cols(group, m, each, heads)
         message(out_ref, step_rows(q_ref, cols), k_ref[:, cols], v_ref[:, cols])
 
 
-def block_states(owners, chunk, group, heads, keys, values, step_queries, after):
+def block_states(owners, group, each, heads, keys, values, step_queries, after):
     rows = keys.shape[0]
     steps, samples, _ = step_queries.shape
-    wide = heads * HEAD_DIM
-    shape = jax.ShapeDtypeStruct((heads, HEAD_DIM + steps * samples, HEAD_DIM), F32)
-    return pl.pallas_call(
-        functools.partial(state_kernel, group, owners, chunk * group * wide),
+    count = heads[1] - heads[0]
+    wide = count * HEAD_DIM
+    shape = jax.ShapeDtypeStruct((count, HEAD_DIM + steps * samples, HEAD_DIM), F32)
+    return pl.pallas_call(
+        functools.partial(state_kernel, group, owners, each, heads),
         in_specs=[VMEM, VMEM, VMEM] + [ANY] * len(after),
         out_specs=[VMEM] * len(owners),
         out_shape=[shape] * len(owners),
@@ -127,33 +129,32 @@
     )(step_queries, keys, values, *after)
 
 
-def total_kernel(group, *refs):
-    total = refs[0][:, :HEAD_DIM, :]
+def total_kernel(group, heads, *refs):
+    here = slice(*heads)
+    total = refs[0][here, :HEAD_DIM, :]
     for part in refs[1:group]:
-        total = total + part[:, :HEAD_DIM, :]
+        total = total + part[here, :HEAD_DIM, :]
     refs[-1][...] = total
 
 
-def group_total(parts, after):
-    heads = parts[0].shape[0]
-    shape = (heads, HEAD_DIM, HEAD_DIM)
-    return pl.pallas_call(
-        functools.partial(total_kernel, len(parts)),
+def group_total(parts, heads, after):
+    shape = (heads[1] - heads[0], HEAD_DIM, HEAD_DIM)
+    return pl.pallas_call(
+        functools.partial(total_kernel, len(parts), heads),
         in_specs=[VMEM] * len(parts) + [ANY] * len(after),
         out_specs=VMEM,
         out_shape=jax.ShapeDtypeStruct(shape, F32),
         compiler_params=params(),
-        cost_estimate=cost(0, 4 * heads * HEAD_DIM * HEAD_DIM * (len(parts) + 1)),
+        cost_estimate=cost(0, 4 * shape[0] * HEAD_DIM * HEAD_DIM * (len(parts) + 1)),
         name="group_total",
     )(*parts, *after)
 
 
-def prior_kernel(group, others, *refs):
+def prior_kernel(owners, group, others, top, *refs):
     parts, total_ref = refs[:group], refs[group]
     other_refs, out_refs = refs[group + 1 : group + 1 + others], refs[-group:]
     here, block = place(group)
-    heads = parts[0].shape[0]
-    for h in range(heads):
+    for h in range(total_ref.shape[0]):
         entering = jnp.zeros((HEAD_DIM, HEAD_DIM), F32)
         final = total_ref[h]
         for k in range(others):
@@ -161,41 +162,44 @@
             entering = entering + jnp.where(block > k, other, 0.0)
             final = final + other
         high, low = split(final)
-        query = jnp.concatenate([part[h, HEAD_DIM:, :] for part in parts], axis=0).astype(BF16)
+        query = jnp.concatenate([part[top + h, HEAD_DIM:, :] for part in parts], axis=0)
+        query = query.astype(BF16)
         raw = dot(query, high) + dot(query, low)
         dec = raw.shape[0] // group
         for m in range(group):
+            out_ref = out_refs[owners.index(m)]
             prior = entering
             for k in range(group):
                 if k != m:
                     prior = prior + jnp.where(
-                        (here ^ k) < (here ^ m), parts[k][h, :HEAD_DIM, :], 0.0
+                        (here ^ k) < (here ^ m), parts[k][top + h, :HEAD_DIM, :], 0.0
                     )
-            out_refs[m][h, :HEAD_DIM, :] = prior
-            out_refs[m][h, HEAD_DIM:, :] = raw[m * dec : (m + 1) * dec]
-
-
-def priors(parts, total, others, after):
+            out_ref[h, :HEAD_DIM, :] = prior
+            out_ref[h, HEAD_DIM:, :] = raw[m * dec : (m + 1) * dec]
+
+
+def priors(owners, parts, top, total, others, after):
     group = len(parts)
-    return pl.pallas_call(
-        functools.partial(prior_kernel, group, len(others)),
+    shape = (total.shape[0], *parts[0].shape[1:])
+    return pl.pallas_call(
+        functools.partial(prior_kernel, owners, group, len(others), top),
         in_specs=[VMEM] * (group + 1 + len(others)) + [ANY] * len(after),
         out_specs=[VMEM] * group,
-        out_shape=[jax.ShapeDtypeStruct(parts[0].shape, F32)] * group,
-        compiler_params=params(),
-        cost_estimate=cost(0, 4 * parts[0].size * (2 * group + 1 + len(others))),
+        out_shape=[jax.ShapeDtypeStruct(shape, F32)] * group,
+        compiler_params=params(),
+        cost_estimate=cost(0, 4 * total.size * (2 * group + 1 + len(others))),
         name="priors",
     )(*parts, total, *others, *after)
 
 
-def intra_kernel(tile, first, q_ref, k_ref, v_ref, *refs):
+def intra_kernel(tile, heads, q_ref, k_ref, v_ref, *refs):
     out_ref = refs[-1]
     rows, wide = out_ref.shape
     keep = lax.broadcasted_iota(jnp.int32, (tile, tile), 0) >= lax.broadcasted_iota(
         jnp.int32, (tile, tile), 1
     )
-    for h in range(wide // HEAD_DIM):
-        cols = slice(first + h * HEAD_DIM, first + (h + 1) * HEAD_DIM)
+    for h, head in enumerate(heads):
+        cols = head_cols(head)
         total = None
         for i in range(0, rows, tile):
             scores = dot(q_ref[i:, cols], k_ref[i : i + tile, cols], ((1,), (1,)))
@@ -208,11 +212,12 @@
             total = total[tile:]
 
 
-def intra_block(first, wide, queries, keys, values, after):
+def intra_block(heads, queries, keys, values, after):
     rows = queries.shape[0]
+    wide = len(heads) * HEAD_DIM
     tile = 256 if rows % 256 == 0 else rows
     return pl.pallas_call(
-        functools.partial(intra_kernel, tile, first),
+        functools.partial(intra_kernel, tile, heads),
         in_specs=[VMEM] * 3 + [ANY] * len(after),
         out_specs=VMEM,
         out_shape=jax.ShapeDtypeStruct((rows, wide), F32),
@@ -292,39 +297,37 @@
     )(lengths, step_queries, suffix_keys, suffix_values, step_keys, step_values, *after)
 
 
-def pick(refs, owner, group, heads):
-    wide = heads * HEAD_DIM
-    if len(refs) == 1:
-        return refs[0][:, pl.ds(pl.multiple_of(owner * wide, wide), wide)]
-    each = group // len(refs)
-    at = pl.ds(pl.multiple_of(owner % each * wide, wide), wide)
-    found = refs[0][:, at]
-    for i in range(1, len(refs)):
-        found = jnp.where(owner // each == i, refs[i][:, at], found)
-    return found
-
-
-def attended_kernel(group, pieces, top, first, last, q_ref, extra_ref, *refs):
+def attended_kernel(group, pieces, each, heads, first, last, q_ref, extra_ref, *refs):
     intra_refs, refs = refs[:pieces], refs[pieces:]
     parts = refs[:group]
     att_ref, raw_ref, sum_ref, acc_ref = refs[-4:]
     rows = q_ref.shape[0]
-    heads = parts[0].shape[0]
     dec = extra_ref.shape[0]
+    count = heads[1] - heads[0]
     if first:
         acc_ref[...] = jnp.zeros_like(acc_ref)
     else:
         acc_ref[...] = refs[group][...]
     for m in range(group):
-        all_cols = owned_cols(group, m, top, heads)
-        own_cols = owned_cols(group, m, 0, heads)
+        all_cols = owned_cols(group, m, each, heads)
+        own_cols = owned_cols(group, m, count, (0, count))
         query = q_ref[:, all_cols]
-        intra = pick(intra_refs, place(group)[0] ^ m, group, heads)
         extra = extra_ref[:, all_cols]
+        if pieces == 1:
+            intra = intra_refs[0][:, own_cols]
+        else:
+            owner = place(group)[0] ^ m
+            share = group // pieces
+            at = pl.multiple_of(lax.rem(owner, share) * count * HEAD_DIM, HEAD_DIM)
+            intra = intra_refs[0][:, pl.ds(at, count * HEAD_DIM)]
+            for i in range(1, pieces):
+                intra = jnp.where(
+                    lax.div(owner, share) == i, intra_refs[i][:, pl.ds(at, count * HEAD_DIM)], intra
+                )
         squares = acc_ref[:rows, :]
         raw_squares = acc_ref[rows : rows + dec, :]
         atts, raws = [], []
-        for h in range(heads):
+        for h in range(count):
             cols = head_cols(h)
             att = intra[:, cols] + dot(query[:, cols], parts[m][h, :HEAD_DIM, :].astype(BF16))
             raw = extra[:, cols] + parts[m][h, HEAD_DIM:, :]
@@ -342,16 +345,15 @@
         sum_ref[...] = acc_ref[...]
 
 
-def attend(chunk, last, queries, intra, extra, parts, before, after):
+def attend(each, heads, last, queries, intra, extra, parts, before, after):
     group = len(parts)
-    heads = parts[0].shape[0]
-    wide = group * heads * HEAD_DIM
+    wide = group * (heads[1] - heads[0]) * HEAD_DIM
     rows, dec = queries.shape[0], extra.shape[0]
     pieces = len(intra)
     padded = -(-(rows + dec) // LANES) * LANES
     sums = (1, padded) if last else (padded, LANES)
     return pl.pallas_call(
-        functools.partial(attended_kernel, group, pieces, chunk * wide, not before, last),
+        functools.partial(attended_kernel, group, pieces, each, heads, not before, last),
         in_specs=[VMEM] * (2 + pieces + group + len(before)) + [ANY] * len(after),
         out_specs=[VMEM] * 3,
         out_shape=[
@@ -366,12 +368,13 @@
     )(queries, extra, *intra, *parts, *before, *after)
 
 
-def norm_kernel(chunks, sums, width, tile, gain_ref, *refs):
+def norm_kernel(heads, sums, width, tile, gain_ref, *refs):
+    chunks = len(heads)
     sum_refs = refs[:sums]
     att_refs = refs[sums : sums + chunks]
     raw_refs = refs[sums + chunks : sums + 2 * chunks]
-    out_hbm, dec_ref, scale_ref, buf_ref, sems = refs[sums + 2 * chunks :]
-    rows, wide = att_refs[0].shape
+    out_hbm, dec_hbm, scale_ref, buf_ref, dec_ref, sems = refs[sums + 2 * chunks :]
+    rows = att_refs[0].shape[0]
     dec = raw_refs[0].shape[0]
     samples = dec_ref.shape[1]
     total = sum_refs[0][...]
@@ -384,33 +387,35 @@
         here = slice(i * tile, (i + 1) * tile)
         row_scale = scale_ref[here, :]
         for c in range(chunks):
-            for h in range(wide // HEAD_DIM):
-                at = slice(c * wide + h * HEAD_DIM, c * wide + (h + 1) * HEAD_DIM)
+            for h, head in enumerate(heads[c]):
+                at = head_cols(head)
                 buf_ref[here, at] = (
                     att_refs[c][here, head_cols(h)] * row_scale * gain_ref[:, at]
                 ).astype(BF16)
         copies.append(pltpu.make_async_copy(buf_ref.at[here], out_hbm.at[here], sems.at[i]))
         copies[-1].start()
-    row_scale = scale_ref[rows : rows + dec, :]
-    for c in range(chunks):
-        for h in range(wide // HEAD_DIM):
-            at = slice(c * wide + h * HEAD_DIM, c * wide + (h + 1) * HEAD_DIM)
-            out = raw_refs[c][:, head_cols(h)] * row_scale * gain_ref[:, at]
-            for i in range(dec_ref.shape[0]):
-                dec_ref[i, :, at] = out[i * samples : (i + 1) * samples].astype(BF16)
+        if i == 0:
+            row_scale = scale_ref[rows : rows + dec, :]
+            for c in range(chunks):
+                for h, head in enumerate(heads[c]):
+                    at = head_cols(head)
+                    out = raw_refs[c][:, head_cols(h)] * row_scale * gain_ref[:, at]
+                    for j in range(dec_ref.shape[0]):
+                        dec_ref[j, :, at] = out[j * samples : (j + 1) * samples].astype(BF16)
+            copies.append(pltpu.make_async_copy(dec_ref, dec_hbm, sems.at[rows // tile]))
+            copies[-1].start()
     for copy in copies:
         copy.wait()
 
 
-def normalize(atts, raws, sums, gain, steps, width_all):
-    rows, wide = atts[0].shape
-    width = wide * len(atts)
+def normalize(heads, atts, raws, sums, gain, steps, width_all):
+    rows, width = atts[0].shape[0], gain.shape[0]
     dec = raws[0].shape[0]
     tile = 128 if rows % 128 == 0 else rows
     return pl.pallas_call(
-        functools.partial(norm_kernel, len(atts), len(sums), width_all, tile),
+        functools.partial(norm_kernel, heads, len(sums), width_all, tile),
         in_specs=[VMEM] * (1 + len(sums) + 2 * len(atts)),
-        out_specs=[pl.BlockSpec(memory_space=pltpu.HBM), VMEM],
+        out_specs=[pl.BlockSpec(memory_space=pltpu.HBM)] * 2,
         out_shape=[
             jax.ShapeDtypeStruct((rows, width), BF16),
             jax.ShapeDtypeStruct((steps, dec // steps, width), BF16),
@@ -418,7 +423,8 @@
         scratch_shapes=[
             pltpu.VMEM((sums[0].shape[1], LANES), F32),
             pltpu.VMEM((rows, width), BF16),
-            pltpu.SemaphoreType.DMA((rows // tile,)),
+            pltpu.VMEM((steps, dec // steps, width), BF16),
+            pltpu.SemaphoreType.DMA((rows // tile + 1,)),
         ],
         compiler_params=params(),
         cost_estimate=cost(0, 6 * rows * width),
@@ -426,15 +432,26 @@
     )(gain[None, :], *sums, *atts, *raws)
 
 
+SENT = (1, 1)
+DONE = (1, 1)
+ORDER = "s0 s1 t0 i0.0 i0.1 p0 t1 x p1 i1 a0 a1"
+PIECES = (2, 1)
+FIRST = 1
+RANKING = lambda m: m
+
+
 def group_size(devices, heads):
     size = 1
-    while (
-        devices % (2 * size) == 0
-        and size * size < devices
-        and heads % (2 * size * CHUNKS) == 0
-    ):
+    while devices % (2 * size) == 0 and size * size < devices and heads % (4 * size) == 0:
         size *= 2
     return size
+
+
+def bounds(shares, heads):
+    marks = [0]
+    for i in range(len(shares)):
+        marks.append(heads * sum(shares[: i + 1]) // sum(shares))
+    return list(zip(marks[:-1], marks[1:]))
 
 
 def on_device(
@@ -454,15 +471,31 @@
     devices = lax.axis_size("seq")
     group = group_size(devices, heads_here)
     blocks = devices // group
-    heads = heads_here // (group * CHUNKS)
-    def swap(m):
-        return [(i, i // group * group + (i % group ^ m)) for i in range(devices)]
-
-    def to_group(messages):
-        arrived = list(messages)
-        for m in range(group - 1, 0, -1):
-            arrived[m] = lax.ppermute(messages[m], "seq", swap(m))
-        return arrived
+    each = heads_here // group
+    fine = each % sum(DONE) == 0 and each % sum(SENT) == 0
+    sent_heads, done_heads = (bounds(SENT, each), bounds(DONE, each)) if fine else (
+        bounds((1, 1), each),
+        bounds((1, 1), each),
+    )
+    chunk_heads = [
+        [owner * each + h for owner in range(group) for h in range(lo, hi)] for lo, hi in done_heads
+    ]
+
+    def swap(messages):
+        return [messages[0]] + [
+            lax.ppermute(
+                messages[m],
+                "seq",
+                [(i, i // group * group + (i % group ^ m)) for i in range(devices)],
+            )
+            for m in range(1, group)
+        ]
+
+    owners = sorted(range(group), key=RANKING)
+
+    def ordered(owners, messages):
+        made = dict(zip(owners, messages))
+        return [made[m] for m in range(group)]
 
     def across(total):
         return [
@@ -470,57 +503,95 @@
             for k in range(1, blocks)
         ]
 
-    def states(owners, c, after):
-        return block_states(owners, c, group, heads, keys, values, step_queries, after)
-
-    def intra(first, wide, after):
-        return intra_block(first * HEAD_DIM, wide * HEAD_DIM, queries, keys, values, after)
-
-    half = heads_here // CHUNKS
-    first = fetched_states(group - 1, 0, group, heads, keys, values, step_queries)
-    rest = states(list(range(group - 1)), 0, [first])
-    parts = [to_group([*rest, first])]
-    later = states(list(range(group)), 1, [rest[0]])
-    parts.append(to_group(later))
-    totals = [group_total(parts[0], [later[0]])]
-    others = [across(totals[0])]
-    intras = [intra(0, half // 2, [totals[0]])]
-    totals.append(group_total(parts[1], [intras[0]]))
-    others.append(across(totals[1]))
-    intras.append(intra(half // 2, half - half // 2, [totals[1]]))
-    sent = [priors(parts[0], totals[0], others[0], [intras[1]])]
-    entering = [to_group(sent[0])]
-    sent.append(priors(parts[1], totals[1], others[1], [sent[0][0]]))
-    entering.append(to_group(sent[1]))
-    extra = suffix_part(
-        suffix_lengths,
-        step_queries,
-        suffix_keys,
-        suffix_values,
-        step_keys,
-        step_values,
-        [sent[1][0]],
-    )
-    intras = [intras, [intra(half, half, [extra])]]
-    atts, raws, sums = [], [], []
-    for c in range(CHUNKS):
-        att, raw, total = attend(
-            c, c == CHUNKS - 1, queries, intras[c], extra, entering[c], sums, []
-        )
-        sums = [total]
-        atts.append(att)
-        raws.append(raw)
-    sums = sums[0]
-    others_of_row = lax.axis_size("head")
-    all_sums = [sums] + [
-        lax.ppermute(
-            sums, "head", [(i, (i + k) % others_of_row) for i in range(others_of_row)]
-        )
-        for k in range(1, others_of_row)
+    def holder(c):
+        lo, hi = done_heads[c]
+        for i, (start, end) in enumerate(sent_heads):
+            if start <= lo and hi <= end:
+                return i, lo - start
+
+    parts, totals, others, entering, intras, atts, raws = {}, {}, {}, {}, {}, {}, {}
+    extra, sums, last = None, [], []
+    for step in ORDER.split():
+        kind, c = step[0], int(step[1:].split(".")[0] or 0) if len(step) > 1 else 0
+        if kind == "s" and c < len(sent_heads):
+            if c == 0:
+                m = FIRST % group
+                given = (group, each, sent_heads[0], keys, values, step_queries)
+                first = fetched_states(m, *given)
+                rest = block_states([i for i in owners if i != m], *given, [first])
+                messages = ordered([m] + [i for i in owners if i != m], [first, *rest])
+                last = [rest[0]]
+            else:
+                messages = block_states(
+                    owners,
+                    group,
+                    each,
+                    sent_heads[c],
+                    keys,
+                    values,
+                    step_queries,
+                    last,
+                )
+                last = [messages[0]]
+                messages = ordered(owners, messages)
+            parts[c] = swap(messages)
+        elif kind == "t" and c < len(done_heads):
+            i, top = holder(c)
+            count = done_heads[c][1] - done_heads[c][0]
+            totals[c] = group_total(parts[i], (top, top + count), last)
+            others[c] = across(totals[c])
+            last = [totals[c]]
+        elif kind == "p" and c < len(done_heads):
+            i, top = holder(c)
+            messages = priors(owners, parts[i], top, totals[c], others[c], last)
+            entering[c] = swap(ordered(owners, messages))
+            last = [messages[0]]
+        elif kind == "i" and c < len(done_heads):
+            heads = chunk_heads[c]
+            if "." in step:
+                share = len(heads) // PIECES[c]
+                piece = int(step.split(".")[1])
+                heads = heads[piece * share : (piece + 1) * share]
+            intras.setdefault(c, []).append(intra_block(heads, queries, keys, values, last))
+            last = [intras[c][-1]]
+        elif kind == "x":
+            extra = suffix_part(
+                suffix_lengths,
+                step_queries,
+                suffix_keys,
+                suffix_values,
+                step_keys,
+                step_values,
+                last,
+            )
+            last = [extra]
+        elif kind == "a" and c < len(done_heads):
+            atts[c], raws[c], total = attend(
+                each,
+                done_heads[c],
+                c == len(done_heads) - 1,
+                queries,
+                intras[c],
+                extra,
+                entering[c],
+                sums,
+                [],
+            )
+            sums = [total]
+    row = lax.axis_size("head")
+    step = (lambda i, k: i ^ k) if row & (row - 1) == 0 else (lambda i, k: (i + k) % row)
+    all_sums = sums + [
+        lax.ppermute(sums[0], "head", [(i, step(i, k)) for i in range(row)]) for k in range(1, row)
     ]
     return tuple(
         normalize(
-            atts, raws, all_sums, norm_gain, step_queries.shape[0], width * others_of_row
+            chunk_heads,
+            [atts[c] for c in range(len(done_heads))],
+            [raws[c] for c in range(len(done_heads))],
+            all_sums,
+            norm_gain,
+            step_queries.shape[0],
+            width * row,
         )
     )
 

time: 49.8 us -> 47.5 us (0.954)
  waiting for transfers between devices: 12.6 us -> 9.89 us
  starting transfers between devices: 23 us -> 24 us
  Pallas kernels: 13.2 us -> 12.6 us
    ppermute x2, waiting for transfers between devices: 4.55 us -> 1.85 us  [across(): lax.ppermute(total, 'seq', [(i, (i + k * group) % devices) for i in range...]
    ppermute x2, starting transfers between devices: 3.29 us -> 5.87 us  [across(): lax.ppermute(total, 'seq', [(i, (i + k * group) % devices) for i in range...]
    ppermute x15, starting transfers between devices: 19.7 us -> 18.2 us  [the longest x12 16.2 us: swap(): lax.ppermute(messages[m], 'seq', [(i, i // group * group + (i % group ^ m...]
    pallas_call x13, Pallas kernels: 10.9 us -> 10.3 us  [the longest x3 4.08 us: intra_block(): pl.pallas_call(functools.partial(intra_kernel, tile, heads), in_specs=[VM...]
  transfers between devices with their start and end apart: 17 -> 17, of which waited for: 7 -> 7; matrix products, arithmetic and copies ran while one was open for 0% -> 0% of each run, Pallas kernels for 17% -> 19%
where the time goes in v4:
time: 47.5 us; the launch traced here: 47.4 us
  starting transfers between devices  24 us (51%)
  Pallas kernels  12.6 us (27%)
  waiting for transfers between devices  9.89 us (21%)
  between operations  0.82 us (2%)
    ppermute x12, starting transfers between devices, swap(): lax.ppermute(messages[m], 'seq', [(i, i // group * group + (i % group ^ m...  16.2 us
    ppermute x12, waiting for transfers between devices, swap(): lax.ppermute(messages[m], 'seq', [(i, i // group * group + (i % group ^ m...  6.23 us
    ppermute x2, starting transfers between devices, across(): lax.ppermute(total, 'seq', [(i, (i + k * group) % devices) for i in range...  5.87 us
    pallas_call x3, Pallas kernels, intra_block(): pl.pallas_call(functools.partial(intra_kernel, tile, heads), in_specs=[VM...  4.08 us
    pallas_call x1, Pallas kernels, suffix_part(): pl.pallas_call(suffix_kernel, in_specs=[SMEM] + [VMEM] * 5 + [ANY] * len(...  2.29 us
    ppermute x3, starting transfers between devices, on_device(): lax.ppermute(sums[0], 'head', [(i, step(i, k)) for i in range(row)])  1.92 us
    ppermute x2, waiting for transfers between devices, across(): lax.ppermute(total, 'seq', [(i, (i + k * group) % devices) for i in range...  1.85 us
    ppermute x3, waiting for transfers between devices, on_device(): lax.ppermute(sums[0], 'head', [(i, step(i, k)) for i in range(row)])  1.81 us
  transfers between devices with their start and end apart: 17, of which 7 were waited for; matrix products, arithmetic and copies ran while one was open for 0% of the time, Pallas kernels for 19%

profile of v4, /device:TPU:0, one launch (start us, length us, event | category | flops | bytes accessed | tf_op | source)
XLA Modules:
  0.0 47.4 jit_solution(8328390613033386894)
XLA Ops:
  0.7 1.5 %fetched_states.1.refs_0_ = f32[2,136,128]{2,1,0:T(8,128)S(1)} custom-call(bf16[2,4,2048]{2,1,0:T(4,128)(2,1)} %q_ref.12, bf16[512,2048]{1,0:T(8,128)(2,1)} %k_ref.11, bf16[512,2048]{1,0:T(8,128)(2,1)} %v_ref.11), custom_call_target="tpu_custom_call" | custom-call | flops 33554432 | bytes 524288 | tf_op jit(solution)/shard_map/fetched_states/pallas_call | solution.py:87
  2.2 3.0 %collective-permute-start.3 = (f32[2,136,128]{2,1,0:T(8,128)S(1)}, f32[2,136,128]{2,1,0:T(8,128)S(1)}, u32[]{:S(2)}, u32[]{:S(2)}) collective-permute-start(f32[2,136,128]{2,1,0:T(8,128)S(1)} %fetched_states.1.refs_0_), channel_id=1, source_target_pairs={{0,4},{4,0},{8,12},{12,8},{16,20},{20,16},{24,28},{28,24},{1,5},{5... | collective-permute-start | bytes 417800 | tf_op jit(solution)/shard_map/ppermute | solution.py:486
  5.2 0.5 %block_states.2 = (f32[2,136,128]{2,1,0:T(8,128)S(1)}, f32[2,136,128]{2,1,0:T(8,128)S(1)}, f32[2,136,128]{2,1,0:T(8,128)S(1)}) custom-call(bf16[2,4,2048]{2,1,0:T(4,128)(2,1)S(1)} %copy-done.5, bf16[512,2048]{1,0:T(8,128)(2,1)S(1)} %copy-done, bf16[512,2048]{1,0:T(8,128)(2,1)S(1)} %copy-done.1, f32[2,136,128]{2,1,0:T(8,128)S(1)} %fetched_states.1.refs_0_), custom_call_target="tpu_custom_call" | custom-call | flops 100663296 | bytes 1572864 | tf_op jit(solution)/shard_map/block_states/pallas_call | solution.py:121
  5.7 1.6 %collective-permute-start.4 = (f32[2,136,128]{2,1,0:T(8,128)S(1)}, f32[2,136,128]{2,1,0:T(8,128)S(1)}, u32[]{:S(2)}, u32[]{:S(2)}) collective-permute-start(f32[2,136,128]{2,1,0:T(8,128)S(1)} %get-tuple-element.28), channel_id=1, source_target_pairs={{0,8},{4,12},{8,0},{12,4},{16,24},{20,28},{24,16},{28,20},{1,9},{5... | collective-permute-start | bytes 417800 | tf_op jit(solution)/shard_map/ppermute | solution.py:486
  7.4 0.7 %collective-permute-start.5 = (f32[2,136,128]{2,1,0:T(8,128)S(1)}, f32[2,136,128]{2,1,0:T(8,128)S(1)}, u32[]{:S(2)}, u32[]{:S(2)}) collective-permute-start(f32[2,136,128]{2,1,0:T(8,128)S(1)} %get-tuple-element.29), channel_id=1, source_target_pairs={{0,12},{4,8},{8,4},{12,0},{16,28},{20,24},{24,20},{28,16},{1,13},{... | collective-permute-start | bytes 417800 | tf_op jit(solution)/shard_map/ppermute | solution.py:486
  8.1 0.6 %block_states.3 = (f32[2,136,128]{2,1,0:T(8,128)S(1)}, f32[2,136,128]{2,1,0:T(8,128)S(1)}, f32[2,136,128]{2,1,0:T(8,128)S(1)}, f32[2,136,128]{2,1,0:T(8,128)S(1)}) custom-call(bf16[2,4,2048]{2,1,0:T(4,128)(2,1)S(1)} %copy-done.5, bf16[512,2048]{1,0:T(8,128)(2,1)S(1)} %copy-done, bf16[512,2048]{1,0:T(8,128)(2,1)S(1)} %copy-done.1, ...), custom_call_target="tpu_custom_call" | custom-call | flops 134217728 | bytes 2097152 | tf_op jit(solution)/shard_map/block_states/pallas_call | solution.py:121
  8.7 1.3 %collective-permute-start = (f32[2,136,128]{2,1,0:T(8,128)S(1)}, f32[2,136,128]{2,1,0:T(8,128)S(1)}, u32[]{:S(2)}, u32[]{:S(2)}) collective-permute-start(f32[2,136,128]{2,1,0:T(8,128)S(1)} %get-tuple-element.25), channel_id=1, source_target_pairs={{0,4},{4,0},{8,12},{12,8},{16,20},{20,16},{24,28},{28,24},{1,5},{5... | collective-permute-start | bytes 417800 | tf_op jit(solution)/shard_map/ppermute | solution.py:486
  10.0 1.6 %collective-permute-start.1 = (f32[2,136,128]{2,1,0:T(8,128)S(1)}, f32[2,136,128]{2,1,0:T(8,128)S(1)}, u32[]{:S(2)}, u32[]{:S(2)}) collective-permute-start(f32[2,136,128]{2,1,0:T(8,128)S(1)} %get-tuple-element.26), channel_id=1, source_target_pairs={{0,8},{4,12},{8,0},{12,4},{16,24},{20,28},{24,16},{28,20},{1,9},{5... | collective-permute-start | bytes 417800 | tf_op jit(solution)/shard_map/ppermute | solution.py:486
  11.6 0.7 %collective-permute-start.2 = (f32[2,136,128]{2,1,0:T(8,128)S(1)}, f32[2,136,128]{2,1,0:T(8,128)S(1)}, u32[]{:S(2)}, u32[]{:S(2)}) collective-permute-start(f32[2,136,128]{2,1,0:T(8,128)S(1)} %get-tuple-element.27), channel_id=1, source_target_pairs={{0,12},{4,8},{8,4},{12,0},{16,28},{20,24},{24,20},{28,16},{1,13},{... | collective-permute-start | bytes 417800 | tf_op jit(solution)/shard_map/ppermute | solution.py:486
  12.3 3.3 %collective-permute-done.5.refs_3_ = f32[2,136,128]{2,1,0:T(8,128)S(1)} collective-permute-done((f32[2,136,128]{2,1,0:T(8,128)S(1)}, f32[2,136,128]{2,1,0:T(8,128)S(1)}, u32[]{:S(2)}, u32[]{:S(2)}) %collective-permute-start.5) | collective-permute-done | bytes 139296 | tf_op jit(solution)/shard_map/ppermute | solution.py:486
  15.6 2.7 %collective-permute-start.6 = (f32[2,128,128]{2,1,0:T(8,128)S(1)}, f32[2,128,128]{2,1,0:T(8,128)S(1)}, u32[]{:S(2)}, u32[]{:S(2)}) collective-permute-start(f32[2,128,128]{2,1,0:T(8,128)S(1)} %group_total.2.refs_0_.refs_4_), channel_id=1, source_target_pairs={{0,16},{4,20},{8,24},{12,28},{16,0},{20,4},{24,8},{28,12},{1,17},{... | collective-permute-start | bytes 393224 | tf_op jit(solution)/shard_map/ppermute | solution.py:502
  18.3 1.1 %intra_block.3.refs_0_ = f32[512,512]{1,0:T(8,128)S(1)} custom-call(bf16[512,2048]{1,0:T(8,128)(2,1)S(1)} %copy-done.2, bf16[512,2048]{1,0:T(8,128)(2,1)S(1)} %copy-done, bf16[512,2048]{1,0:T(8,128)(2,1)S(1)} %copy-done.1, f32[2,128,128]{2,1,0:T(8,128)S(1)} %group_total.2.refs_0_.refs_4_), custom_call_target="tpu_custom_call" | custom-call | flops 536870912 | bytes 2621440 | tf_op jit(solution)/shard_map/intra_block/pallas_call | solution.py:219
  19.4 1.1 %intra_block.4.refs_6_.refs_1_ = f32[512,512]{1,0:T(8,128)S(1)} custom-call(bf16[512,2048]{1,0:T(8,128)(2,1)S(1)} %copy-done.2, bf16[512,2048]{1,0:T(8,128)(2,1)S(1)} %copy-done, bf16[512,2048]{1,0:T(8,128)(2,1)S(1)} %copy-done.1, f32[512,512]{1,0:T(8,128)S(1)} %intra_block.3.refs_0_), custom_call_target="tpu_custom_call" | custom-call | flops 536870912 | bytes 2621440 | tf_op jit(solution)/shard_map/intra_block/pallas_call | solution.py:219
  20.5 1.8 %collective-permute-done.6.refs_5_ = f32[2,128,128]{2,1,0:T(8,128)S(1)} collective-permute-done((f32[2,128,128]{2,1,0:T(8,128)S(1)}, f32[2,128,128]{2,1,0:T(8,128)S(1)}, u32[]{:S(2)}, u32[]{:S(2)}) %collective-permute-start.6) | collective-permute-done | bytes 131104 | tf_op jit(solution)/shard_map/ppermute | solution.py:502
  22.6 0.8 %collective-permute-start.11 = (f32[2,136,128]{2,1,0:T(8,128)S(1)}, f32[2,136,128]{2,1,0:T(8,128)S(1)}, u32[]{:S(2)}, u32[]{:S(2)}) collective-permute-start(f32[2,136,128]{2,1,0:T(8,128)S(1)} %get-tuple-element.35), channel_id=1, source_target_pairs={{0,4},{4,0},{8,12},{12,8},{16,20},{20,16},{24,28},{28,24},{1,5},{5... | collective-permute-start | bytes 417800 | tf_op jit(solution)/shard_map/ppermute | solution.py:486
  23.5 3.2 %collective-permute-start.7 = (f32[2,128,128]{2,1,0:T(8,128)S(1)}, f32[2,128,128]{2,1,0:T(8,128)S(1)}, u32[]{:S(2)}, u32[]{:S(2)}) collective-permute-start(f32[2,128,128]{2,1,0:T(8,128)S(1)} %group_total.3.refs_0_.refs_4_), channel_id=1, source_target_pairs={{0,16},{4,20},{8,24},{12,28},{16,0},{20,4},{24,8},{28,12},{1,17},{... | collective-permute-start | bytes 393224 | tf_op jit(solution)/shard_map/ppermute | solution.py:502
  26.7 2.5 %collective-permute-start.12 = (f32[2,136,128]{2,1,0:T(8,128)S(1)}, f32[2,136,128]{2,1,0:T(8,128)S(1)}, u32[]{:S(2)}, u32[]{:S(2)}) collective-permute-start(f32[2,136,128]{2,1,0:T(8,128)S(1)} %get-tuple-element.36), channel_id=1, source_target_pairs={{0,8},{4,12},{8,0},{12,4},{16,24},{20,28},{24,16},{28,20},{1,9},{5... | collective-permute-start | bytes 417800 | tf_op jit(solution)/shard_map/ppermute | solution.py:486
  29.4 2.3 %suffix_part.1.refs_6_.extra_ref = f32[8,2048]{1,0:T(8,128)S(1)} custom-call(s32[4]{0:T(128)S(1)} %copy-done.9, bf16[2,4,2048]{2,1,0:T(4,128)(2,1)S(1)} %copy-done.5, bf16[4,128,2048]{2,1,0:T(8,128)(2,1)S(1)} %copy-done.3, bf16[4,128,2048]{2,1,0:T(8,128)(2,1)S(1)} %copy-done.4, bf16[2,4,2048]{2,1,0:T(4,128)(2,1)S(1)} %copy-done.6, ...), custom_call_target="tpu_custom_call" | custom-call | flops 67108864 | bytes 4194304 | tf_op jit(solution)/shard_map/suffix_part/pallas_call | solution.py:289
  31.7 0.3 priors.3
  32.0 1.3 %collective-permute-start.8 = (f32[2,136,128]{2,1,0:T(8,128)S(1)}, f32[2,136,128]{2,1,0:T(8,128)S(1)}, u32[]{:S(2)}, u32[]{:S(2)}) collective-permute-start(f32[2,136,128]{2,1,0:T(8,128)S(1)} %get-tuple-element.32), channel_id=1, source_target_pairs={{0,4},{4,0},{8,12},{12,8},{16,20},{20,16},{24,28},{28,24},{1,5},{5... | collective-permute-start | bytes 417800 | tf_op jit(solution)/shard_map/ppermute | solution.py:486
  33.3 2.0 %collective-permute-start.9 = (f32[2,136,128]{2,1,0:T(8,128)S(1)}, f32[2,136,128]{2,1,0:T(8,128)S(1)}, u32[]{:S(2)}, u32[]{:S(2)}) collective-permute-start(f32[2,136,128]{2,1,0:T(8,128)S(1)} %get-tuple-element.33), channel_id=1, source_target_pairs={{0,8},{4,12},{8,0},{12,4},{16,24},{20,28},{24,16},{28,20},{1,9},{5... | collective-permute-start | bytes 417800 | tf_op jit(solution)/shard_map/ppermute | solution.py:486
  35.4 0.5 collective-permute-start.10
  35.8 1.9 %intra_block.5.refs_0_ = f32[512,1024]{1,0:T(8,128)S(1)} custom-call(bf16[512,2048]{1,0:T(8,128)(2,1)S(1)} %copy-done.2, bf16[512,2048]{1,0:T(8,128)(2,1)S(1)} %copy-done, bf16[512,2048]{1,0:T(8,128)(2,1)S(1)} %copy-done.1, f32[2,136,128]{2,1,0:T(8,128)S(1)} %get-tuple-element.31.refs_0_.refs_1_), custom_call_target="tpu_custom_call" | custom-call | flops 1073741824 | bytes 5242880 | tf_op jit(solution)/shard_map/intra_block/pallas_call | solution.py:219
  37.7 0.7 %attend.2 = (f32[512,1024]{1,0:T(8,128)S(1)}, f32[8,1024]{1,0:T(8,128)S(1)}, f32[640,128]{1,0:T(8,128)S(1)}) custom-call(bf16[512,2048]{1,0:T(8,128)(2,1)S(1)} %copy-done.2, f32[8,2048]{1,0:T(8,128)S(1)} %suffix_part.1.refs_6_.extra_ref, f32[512,512]{1,0:T(8,128)S(1)} %intra_block.3.refs_0_, f32[512,512]{1,0:T(8,128)S(1)} %intra_block.4.refs_6_.refs_1_, ...), custom_call_target="tpu_custom_call" | custom-call | flops 134217728 | bytes 5242880 | tf_op jit(solution)/shard_map/attend/pallas_call | solution.py:355
  38.4 0.9 %collective-permute-done.8.refs_2_ = f32[2,136,128]{2,1,0:T(8,128)S(1)} collective-permute-done((f32[2,136,128]{2,1,0:T(8,128)S(1)}, f32[2,136,128]{2,1,0:T(8,128)S(1)}, u32[]{:S(2)}, u32[]{:S(2)}) %collective-permute-start.8) | collective-permute-done | bytes 139296 | tf_op jit(solution)/shard_map/ppermute | solution.py:486
  39.5 1.8 %collective-permute-done.10.refs_4_ = f32[2,136,128]{2,1,0:T(8,128)S(1)} collective-permute-done((f32[2,136,128]{2,1,0:T(8,128)S(1)}, f32[2,136,128]{2,1,0:T(8,128)S(1)}, u32[]{:S(2)}, u32[]{:S(2)}) %collective-permute-start.10) | collective-permute-done | bytes 139296 | tf_op jit(solution)/shard_map/ppermute | solution.py:486
  41.3 0.6 %attend.3 = (f32[512,1024]{1,0:T(8,128)S(1)}, f32[8,1024]{1,0:T(8,128)S(1)}, f32[1,640]{1,0:T(1,128)S(1)}) custom-call(bf16[512,2048]{1,0:T(8,128)(2,1)S(1)} %copy-done.2, f32[8,2048]{1,0:T(8,128)S(1)} %suffix_part.1.refs_6_.extra_ref, f32[512,1024]{1,0:T(8,128)S(1)} %intra_block.5.refs_0_, f32[2,136,128]{2,1,0:T(8,128)S(1)} %get-tuple-element.31.refs_0_.refs_1_, ...), custom_call_target="tpu_custom_call" | custom-call | flops 134217728 | bytes 5242880 | tf_op jit(solution)/shard_map/attend/pallas_call | solution.py:355
  42.0 1.6 %collective-permute-start.15 = (f32[1,640]{1,0:T(1,128)S(1)}, f32[1,640]{1,0:T(1,128)S(1)}, u32[]{:S(2)}, u32[]{:S(2)}) collective-permute-start(f32[1,640]{1,0:T(1,128)S(1)} %get-tuple-element.39.refs_0_), channel_id=1, source_target_pairs={{0,2},{1,3},{2,0},{3,1},{4,6},{5,7},{6,4},{7,5},{8,10},{9,11},{10,... | collective-permute-start | bytes 7688 | tf_op jit(solution)/shard_map/ppermute | solution.py:584
  43.5 0.3 collective-permute-start.14
  43.8 1.2 %collective-permute-done.16.refs_3_ = f32[1,640]{1,0:T(1,128)S(1)} collective-permute-done((f32[1,640]{1,0:T(1,128)S(1)}, f32[1,640]{1,0:T(1,128)S(1)}, u32[]{:S(2)}, u32[]{:S(2)}) %collective-permute-start.16) | collective-permute-done | bytes 2592 | tf_op jit(solution)/shard_map/ppermute | solution.py:584
  45.0 0.7 %collective-permute-done.15.refs_2_ = f32[1,640]{1,0:T(1,128)S(1)} collective-permute-done((f32[1,640]{1,0:T(1,128)S(1)}, f32[1,640]{1,0:T(1,128)S(1)}, u32[]{:S(2)}, u32[]{:S(2)}) %collective-permute-start.15) | collective-permute-done | bytes 2592 | tf_op jit(solution)/shard_map/ppermute | solution.py:584
  45.6 1.7 %normalize.1 = (bf16[512,2048]{1,0:T(8,128)(2,1)}, bf16[2,4,2048]{2,1,0:T(4,128)(2,1)}) custom-call(f32[1,2048]{1,0:T(1,128)S(1)} %bitcast.1, f32[1,640]{1,0:T(1,128)S(1)} %get-tuple-element.39.refs_0_, f32[1,640]{1,0:T(1,128)S(1)} %collective-permute-done.14.refs_1_, f32[1,640]{1,0:T(1,128)S(1)} %collective-permute-done.15.refs_2_, ...), custom_call_target="tpu_custom_call" | custom-call | bytes 6291456 | tf_op jit(solution)/shard_map/normalize/pallas_call | solution.py:415
  (36 shorter events, 0.8 us)
Async XLA Ops:
  0.6 4.6 %copy-start.1 = (bf16[512,2048]{1,0:T(8,128)(2,1)S(1)}, bf16[512,2048]{1,0:T(8,128)(2,1)}, u32[]{:S(2)}) copy-start(bf16[512,2048]{1,0:T(8,128)(2,1)} %v_ref.11) | copy-start | bytes 6291460
  0.6 4.6 %copy-start = (bf16[512,2048]{1,0:T(8,128)(2,1)S(1)}, bf16[512,2048]{1,0:T(8,128)(2,1)}, u32[]{:S(2)}) copy-start(bf16[512,2048]{1,0:T(8,128)(2,1)} %k_ref.11) | copy-start | bytes 6291460
  0.7 4.6 %copy-start.5 = (bf16[2,4,2048]{2,1,0:T(4,128)(2,1)S(1)}, bf16[2,4,2048]{2,1,0:T(4,128)(2,1)}, u32[]{:S(2)}) copy-start(bf16[2,4,2048]{2,1,0:T(4,128)(2,1)} %q_ref.12) | copy-start | bytes 98308
  2.2 9.4 %collective-permute-start.3 = (f32[2,136,128]{2,1,0:T(8,128)S(1)}, f32[2,136,128]{2,1,0:T(8,128)S(1)}, u32[]{:S(2)}, u32[]{:S(2)}) collective-permute-start(f32[2,136,128]{2,1,0:T(8,128)S(1)} %fetched_states.1.refs_0_), channel_id=1, source_target_pairs={{0,4},{4,0},{8,12},{12,8},{16,20},{20,16},{24,28},{28,24},{1,5},{5... | collective-permute-start | bytes 417800 | tf_op jit(solution)/shard_map/ppermute | solution.py:486
  5.7 6.5 %collective-permute-start.4 = (f32[2,136,128]{2,1,0:T(8,128)S(1)}, f32[2,136,128]{2,1,0:T(8,128)S(1)}, u32[]{:S(2)}, u32[]{:S(2)}) collective-permute-start(f32[2,136,128]{2,1,0:T(8,128)S(1)} %get-tuple-element.28), channel_id=1, source_target_pairs={{0,8},{4,12},{8,0},{12,4},{16,24},{20,28},{24,16},{28,20},{1,9},{5... | collective-permute-start | bytes 417800 | tf_op jit(solution)/shard_map/ppermute | solution.py:486
  7.4 8.2 %collective-permute-start.5 = (f32[2,136,128]{2,1,0:T(8,128)S(1)}, f32[2,136,128]{2,1,0:T(8,128)S(1)}, u32[]{:S(2)}, u32[]{:S(2)}) collective-permute-start(f32[2,136,128]{2,1,0:T(8,128)S(1)} %get-tuple-element.29), channel_id=1, source_target_pairs={{0,12},{4,8},{8,4},{12,0},{16,28},{20,24},{24,20},{28,16},{1,13},{... | collective-permute-start | bytes 417800 | tf_op jit(solution)/shard_map/ppermute | solution.py:486
  8.1 10.2 %copy-start.2 = (bf16[512,2048]{1,0:T(8,128)(2,1)S(1)}, bf16[512,2048]{1,0:T(8,128)(2,1)}, u32[]{:S(2)}) copy-start(bf16[512,2048]{1,0:T(8,128)(2,1)} %q_ref.15) | copy-start | bytes 6291460
  8.7 14.8 %collective-permute-start = (f32[2,136,128]{2,1,0:T(8,128)S(1)}, f32[2,136,128]{2,1,0:T(8,128)S(1)}, u32[]{:S(2)}, u32[]{:S(2)}) collective-permute-start(f32[2,136,128]{2,1,0:T(8,128)S(1)} %get-tuple-element.25), channel_id=1, source_target_pairs={{0,4},{4,0},{8,12},{12,8},{16,20},{20,16},{24,28},{28,24},{1,5},{5... | collective-permute-start | bytes 417800 | tf_op jit(solution)/shard_map/ppermute | solution.py:486
  10.0 13.5 %collective-permute-start.1 = (f32[2,136,128]{2,1,0:T(8,128)S(1)}, f32[2,136,128]{2,1,0:T(8,128)S(1)}, u32[]{:S(2)}, u32[]{:S(2)}) collective-permute-start(f32[2,136,128]{2,1,0:T(8,128)S(1)} %get-tuple-element.26), channel_id=1, source_target_pairs={{0,8},{4,12},{8,0},{12,4},{16,24},{20,28},{24,16},{28,20},{1,9},{5... | collective-permute-start | bytes 417800 | tf_op jit(solution)/shard_map/ppermute | solution.py:486
  11.6 11.9 %collective-permute-start.2 = (f32[2,136,128]{2,1,0:T(8,128)S(1)}, f32[2,136,128]{2,1,0:T(8,128)S(1)}, u32[]{:S(2)}, u32[]{:S(2)}) collective-permute-start(f32[2,136,128]{2,1,0:T(8,128)S(1)} %get-tuple-element.27), channel_id=1, source_target_pairs={{0,12},{4,8},{8,4},{12,0},{16,28},{20,24},{24,20},{28,16},{1,13},{... | collective-permute-start | bytes 417800 | tf_op jit(solution)/shard_map/ppermute | solution.py:486
  15.6 6.8 %collective-permute-start.6 = (f32[2,128,128]{2,1,0:T(8,128)S(1)}, f32[2,128,128]{2,1,0:T(8,128)S(1)}, u32[]{:S(2)}, u32[]{:S(2)}) collective-permute-start(f32[2,128,128]{2,1,0:T(8,128)S(1)} %group_total.2.refs_0_.refs_4_), channel_id=1, source_target_pairs={{0,16},{4,20},{8,24},{12,28},{16,0},{20,4},{24,8},{28,12},{1,17},{... | collective-permute-start | bytes 393224 | tf_op jit(solution)/shard_map/ppermute | solution.py:502
  19.4 10.0 %copy-start.4 = (bf16[4,128,2048]{2,1,0:T(8,128)(2,1)S(1)}, bf16[4,128,2048]{2,1,0:T(8,128)(2,1)}, u32[]{:S(2)}) copy-start(bf16[4,128,2048]{2,1,0:T(8,128)(2,1)} %v_ref.10) | copy-start | bytes 6291460
  20.5 8.9 %copy-start.3 = (bf16[4,128,2048]{2,1,0:T(8,128)(2,1)S(1)}, bf16[4,128,2048]{2,1,0:T(8,128)(2,1)}, u32[]{:S(2)}) copy-start(bf16[4,128,2048]{2,1,0:T(8,128)(2,1)} %k_ref.10) | copy-start | bytes 6291460
  20.5 8.9 %copy-start.6 = (bf16[2,4,2048]{2,1,0:T(4,128)(2,1)S(1)}, bf16[2,4,2048]{2,1,0:T(4,128)(2,1)}, u32[]{:S(2)}) copy-start(bf16[2,4,2048]{2,1,0:T(4,128)(2,1)} %sk_ref.1) | copy-start | bytes 98308
  20.5 8.9 %copy-start.7 = (bf16[2,4,2048]{2,1,0:T(4,128)(2,1)S(1)}, bf16[2,4,2048]{2,1,0:T(4,128)(2,1)}, u32[]{:S(2)}) copy-start(bf16[2,4,2048]{2,1,0:T(4,128)(2,1)} %sv_ref.1) | copy-start | bytes 98308
  20.5 8.9 %copy-start.9 = (s32[4]{0:T(128)S(1)}, s32[4]{0:T(128)}, u32[]{:S(2)}) copy-start(s32[4]{0:T(128)} %lengths_ref.1) | copy-start | bytes 52
  22.6 12.7 %collective-permute-start.11 = (f32[2,136,128]{2,1,0:T(8,128)S(1)}, f32[2,136,128]{2,1,0:T(8,128)S(1)}, u32[]{:S(2)}, u32[]{:S(2)}) collective-permute-start(f32[2,136,128]{2,1,0:T(8,128)S(1)} %get-tuple-element.35), channel_id=1, source_target_pairs={{0,4},{4,0},{8,12},{12,8},{16,20},{20,16},{24,28},{28,24},{1,5},{5... | collective-permute-start | bytes 417800 | tf_op jit(solution)/shard_map/ppermute | solution.py:486
  23.5 8.2 %collective-permute-start.7 = (f32[2,128,128]{2,1,0:T(8,128)S(1)}, f32[2,128,128]{2,1,0:T(8,128)S(1)}, u32[]{:S(2)}, u32[]{:S(2)}) collective-permute-start(f32[2,128,128]{2,1,0:T(8,128)S(1)} %group_total.3.refs_0_.refs_4_), channel_id=1, source_target_pairs={{0,16},{4,20},{8,24},{12,28},{16,0},{20,4},{24,8},{28,12},{1,17},{... | collective-permute-start | bytes 393224 | tf_op jit(solution)/shard_map/ppermute | solution.py:502
  26.7 11.0 %collective-permute-start.12 = (f32[2,136,128]{2,1,0:T(8,128)S(1)}, f32[2,136,128]{2,1,0:T(8,128)S(1)}, u32[]{:S(2)}, u32[]{:S(2)}) collective-permute-start(f32[2,136,128]{2,1,0:T(8,128)S(1)} %get-tuple-element.36), channel_id=1, source_target_pairs={{0,8},{4,12},{8,0},{12,4},{16,24},{20,28},{24,16},{28,20},{1,9},{5... | collective-permute-start | bytes 417800 | tf_op jit(solution)/shard_map/ppermute | solution.py:486
  29.2 8.5 %collective-permute-start.13 = (f32[2,136,128]{2,1,0:T(8,128)S(1)}, f32[2,136,128]{2,1,0:T(8,128)S(1)}, u32[]{:S(2)}, u32[]{:S(2)}) collective-permute-start(f32[2,136,128]{2,1,0:T(8,128)S(1)} %get-tuple-element.37), channel_id=1, source_target_pairs={{0,12},{4,8},{8,4},{12,0},{16,28},{20,24},{24,20},{28,16},{1,13},{... | collective-permute-start | bytes 417800 | tf_op jit(solution)/shard_map/ppermute | solution.py:486
  32.0 7.3 %collective-permute-start.8 = (f32[2,136,128]{2,1,0:T(8,128)S(1)}, f32[2,136,128]{2,1,0:T(8,128)S(1)}, u32[]{:S(2)}, u32[]{:S(2)}) collective-permute-start(f32[2,136,128]{2,1,0:T(8,128)S(1)} %get-tuple-element.32), channel_id=1, source_target_pairs={{0,4},{4,0},{8,12},{12,8},{16,20},{20,16},{24,28},{28,24},{1,5},{5... | collective-permute-start | bytes 417800 | tf_op jit(solution)/shard_map/ppermute | solution.py:486
  33.3 6.2 %collective-permute-start.9 = (f32[2,136,128]{2,1,0:T(8,128)S(1)}, f32[2,136,128]{2,1,0:T(8,128)S(1)}, u32[]{:S(2)}, u32[]{:S(2)}) collective-permute-start(f32[2,136,128]{2,1,0:T(8,128)S(1)} %get-tuple-element.33), channel_id=1, source_target_pairs={{0,8},{4,12},{8,0},{12,4},{16,24},{20,28},{24,16},{28,20},{1,9},{5... | collective-permute-start | bytes 417800 | tf_op jit(solution)/shard_map/ppermute | solution.py:486
  35.4 6.0 %collective-permute-start.10 = (f32[2,136,128]{2,1,0:T(8,128)S(1)}, f32[2,136,128]{2,1,0:T(8,128)S(1)}, u32[]{:S(2)}, u32[]{:S(2)}) collective-permute-start(f32[2,136,128]{2,1,0:T(8,128)S(1)} %get-tuple-element.34), channel_id=1, source_target_pairs={{0,12},{4,8},{8,4},{12,0},{16,28},{20,24},{24,20},{28,16},{1,13},{... | collective-permute-start | bytes 417800 | tf_op jit(solution)/shard_map/ppermute | solution.py:486
  41.3 4.3 %copy-start.8 = (f32[2048]{0:T(1024)S(1)}, f32[2048]{0:T(1024)}, u32[]{:S(2)}) copy-start(f32[2048]{0:T(1024)} %param.19) | copy-start | bytes 24580
  41.9 3.1 %collective-permute-start.16 = (f32[1,640]{1,0:T(1,128)S(1)}, f32[1,640]{1,0:T(1,128)S(1)}, u32[]{:S(2)}, u32[]{:S(2)}) collective-permute-start(f32[1,640]{1,0:T(1,128)S(1)} %get-tuple-element.39.refs_0_), channel_id=1, source_target_pairs={{0,3},{1,2},{2,1},{3,0},{4,7},{5,6},{6,5},{7,4},{8,11},{9,10},{10,... | collective-permute-start | bytes 7688 | tf_op jit(solution)/shard_map/ppermute | solution.py:584
  42.0 3.7 %collective-permute-start.15 = (f32[1,640]{1,0:T(1,128)S(1)}, f32[1,640]{1,0:T(1,128)S(1)}, u32[]{:S(2)}, u32[]{:S(2)}) collective-permute-start(f32[1,640]{1,0:T(1,128)S(1)} %get-tuple-element.39.refs_0_), channel_id=1, source_target_pairs={{0,2},{1,3},{2,0},{3,1},{4,6},{5,7},{6,4},{7,5},{8,10},{9,11},{10,... | collective-permute-start | bytes 7688 | tf_op jit(solution)/shard_map/ppermute | solution.py:584
  43.5 2.1 %collective-permute-start.14 = (f32[1,640]{1,0:T(1,128)S(1)}, f32[1,640]{1,0:T(1,128)S(1)}, u32[]{:S(2)}, u32[]{:S(2)}) collective-permute-start(f32[1,640]{1,0:T(1,128)S(1)} %get-tuple-element.39.refs_0_), channel_id=1, source_target_pairs={{0,1},{1,0},{2,3},{3,2},{4,5},{5,4},{6,7},{7,6},{8,9},{9,8},{10,11... | collective-permute-start | bytes 7688 | tf_op jit(solution)/shard_map/ppermute | solution.py:584

commit v5 on v4

--- a/solution.py
+++ b/solution.py
@@ -434,10 +434,8 @@
 
 SENT = (1, 1)
 DONE = (1, 1)
-ORDER = "s0 s1 t0 i0.0 i0.1 p0 t1 x p1 i1 a0 a1"
+ORDER = ("s0", "s1", "t0", "i0.0", "i0.1", "p0", "t1", "x", "p1", "i1", "a0", "a1")
 PIECES = (2, 1)
-FIRST = 1
-RANKING = lambda m: m
 
 
 def group_size(devices, heads):
@@ -491,7 +489,7 @@
             for m in range(1, group)
         ]
 
-    owners = sorted(range(group), key=RANKING)
+    owners = list(range(group))[::-1]
 
     def ordered(owners, messages):
         made = dict(zip(owners, messages))
@@ -511,11 +509,11 @@
 
     parts, totals, others, entering, intras, atts, raws = {}, {}, {}, {}, {}, {}, {}
     extra, sums, last = None, [], []
-    for step in ORDER.split():
+    for step in ORDER:
         kind, c = step[0], int(step[1:].split(".")[0] or 0) if len(step) > 1 else 0
         if kind == "s" and c < len(sent_heads):
             if c == 0:
-                m = FIRST % group
+                m = owners[0]
                 given = (group, each, sent_heads[0], keys, values, step_queries)
                 first = fetched_states(m, *given)
                 rest = block_states([i for i in owners if i != m], *given, [first])

time: 47.5 us -> 47.3 us (level)
  waiting for transfers between devices: 9.89 us -> 7.96 us
  starting transfers between devices: 24 us -> 25.7 us
    ppermute x12, waiting for transfers between devices: 6.23 us -> 4.03 us  [swap(): lax.ppermute(messages[m], 'seq', [(i, i // group * group + (i % group ^ m...]
    ppermute x12, starting transfers between devices: 16.2 us -> 18.3 us  [swap(): lax.ppermute(messages[m], 'seq', [(i, i // group * group + (i % group ^ m...]
where the time goes in v5:
time: 47.3 us; the launch traced here: 47.2 us
  starting transfers between devices  25.7 us (54%)
  Pallas kernels  12.6 us (27%)
  waiting for transfers between devices  7.96 us (17%)
  between operations  0.81 us (2%)
    ppermute x12, starting transfers between devices, swap(): lax.ppermute(messages[m], 'seq', [(i, i // group * group + (i % group ^ m...  18.3 us
    ppermute x2, starting transfers between devices, across(): lax.ppermute(total, 'seq', [(i, (i + k * group) % devices) for i in range...  5.53 us
    pallas_call x3, Pallas kernels, intra_block(): pl.pallas_call(functools.partial(intra_kernel, tile, heads), in_specs=[VM...  4.08 us
    ppermute x12, waiting for transfers between devices, swap(): lax.ppermute(messages[m], 'seq', [(i, i // group * group + (i % group ^ m...  4.03 us
    pallas_call x1, Pallas kernels, suffix_part(): pl.pallas_call(suffix_kernel, in_specs=[SMEM] + [VMEM] * 5 + [ANY] * len(...  2.29 us
    ppermute x2, waiting for transfers between devices, across(): lax.ppermute(total, 'seq', [(i, (i + k * group) % devices) for i in range...  2.12 us
    ppermute x3, starting transfers between devices, on_device(): lax.ppermute(sums[0], 'head', [(i, step(i, k)) for i in range(row)])  1.92 us
    ppermute x3, waiting for transfers between devices, on_device(): lax.ppermute(sums[0], 'head', [(i, step(i, k)) for i in range(row)])  1.81 us
  transfers between devices with their start and end apart: 17, of which 7 were waited for; matrix products, arithmetic and copies ran while one was open for 0% of the time, Pallas kernels for 19%

profile of v5, /device:TPU:0, one launch (start us, length us, event | category | flops | bytes accessed | tf_op | source)
XLA Modules:
  0.0 47.2 jit_solution(15404969266966538064)
XLA Ops:
  0.7 1.5 %fetched_states.1.refs_0_ = f32[2,136,128]{2,1,0:T(8,128)S(1)} custom-call(bf16[2,4,2048]{2,1,0:T(4,128)(2,1)} %q_ref.12, bf16[512,2048]{1,0:T(8,128)(2,1)} %k_ref.11, bf16[512,2048]{1,0:T(8,128)(2,1)} %v_ref.11), custom_call_target="tpu_custom_call" | custom-call | flops 33554432 | bytes 524288 | tf_op jit(solution)/shard_map/fetched_states/pallas_call | solution.py:87
  2.2 4.0 %collective-permute-start.5 = (f32[2,136,128]{2,1,0:T(8,128)S(1)}, f32[2,136,128]{2,1,0:T(8,128)S(1)}, u32[]{:S(2)}, u32[]{:S(2)}) collective-permute-start(f32[2,136,128]{2,1,0:T(8,128)S(1)} %fetched_states.1.refs_0_), channel_id=1, source_target_pairs={{0,12},{4,8},{8,4},{12,0},{16,28},{20,24},{24,20},{28,16},{1,13},{... | collective-permute-start | bytes 417800 | tf_op jit(solution)/shard_map/ppermute | solution.py:484
  6.2 0.5 %block_states.2 = (f32[2,136,128]{2,1,0:T(8,128)S(1)}, f32[2,136,128]{2,1,0:T(8,128)S(1)}, f32[2,136,128]{2,1,0:T(8,128)S(1)}) custom-call(bf16[2,4,2048]{2,1,0:T(4,128)(2,1)S(1)} %copy-done.5, bf16[512,2048]{1,0:T(8,128)(2,1)S(1)} %copy-done, bf16[512,2048]{1,0:T(8,128)(2,1)S(1)} %copy-done.1, f32[2,136,128]{2,1,0:T(8,128)S(1)} %fetched_states.1.refs_0_), custom_call_target="tpu_custom_call" | custom-call | flops 100663296 | bytes 1572864 | tf_op jit(solution)/shard_map/block_states/pallas_call | solution.py:121
  6.8 0.6 %collective-permute-start.3 = (f32[2,136,128]{2,1,0:T(8,128)S(1)}, f32[2,136,128]{2,1,0:T(8,128)S(1)}, u32[]{:S(2)}, u32[]{:S(2)}) collective-permute-start(f32[2,136,128]{2,1,0:T(8,128)S(1)} %get-tuple-element.29), channel_id=1, source_target_pairs={{0,4},{4,0},{8,12},{12,8},{16,20},{20,16},{24,28},{28,24},{1,5},{5... | collective-permute-start | bytes 417800 | tf_op jit(solution)/shard_map/ppermute | solution.py:484
  7.3 0.8 %collective-permute-start.4 = (f32[2,136,128]{2,1,0:T(8,128)S(1)}, f32[2,136,128]{2,1,0:T(8,128)S(1)}, u32[]{:S(2)}, u32[]{:S(2)}) collective-permute-start(f32[2,136,128]{2,1,0:T(8,128)S(1)} %get-tuple-element.23.refs_0_), channel_id=1, source_target_pairs={{0,8},{4,12},{8,0},{12,4},{16,24},{20,28},{24,16},{28,20},{1,9},{5... | collective-permute-start | bytes 417800 | tf_op jit(solution)/shard_map/ppermute | solution.py:484
  8.2 0.6 %block_states.3 = (f32[2,136,128]{2,1,0:T(8,128)S(1)}, f32[2,136,128]{2,1,0:T(8,128)S(1)}, f32[2,136,128]{2,1,0:T(8,128)S(1)}, f32[2,136,128]{2,1,0:T(8,128)S(1)}) custom-call(bf16[2,4,2048]{2,1,0:T(4,128)(2,1)S(1)} %copy-done.5, bf16[512,2048]{1,0:T(8,128)(2,1)S(1)} %copy-done, bf16[512,2048]{1,0:T(8,128)(2,1)S(1)} %copy-done.1, ...), custom_call_target="tpu_custom_call" | custom-call | flops 134217728 | bytes 2097152 | tf_op jit(solution)/shard_map/block_states/pallas_call | solution.py:121
  8.8 1.2 %collective-permute-start = (f32[2,136,128]{2,1,0:T(8,128)S(1)}, f32[2,136,128]{2,1,0:T(8,128)S(1)}, u32[]{:S(2)}, u32[]{:S(2)}) collective-permute-start(f32[2,136,128]{2,1,0:T(8,128)S(1)} %get-tuple-element.25), channel_id=1, source_target_pairs={{0,4},{4,0},{8,12},{12,8},{16,20},{20,16},{24,28},{28,24},{1,5},{5... | collective-permute-start | bytes 417800 | tf_op jit(solution)/shard_map/ppermute | solution.py:484
  10.0 1.6 %collective-permute-start.1 = (f32[2,136,128]{2,1,0:T(8,128)S(1)}, f32[2,136,128]{2,1,0:T(8,128)S(1)}, u32[]{:S(2)}, u32[]{:S(2)}) collective-permute-start(f32[2,136,128]{2,1,0:T(8,128)S(1)} %get-tuple-element.26), channel_id=1, source_target_pairs={{0,8},{4,12},{8,0},{12,4},{16,24},{20,28},{24,16},{28,20},{1,9},{5... | collective-permute-start | bytes 417800 | tf_op jit(solution)/shard_map/ppermute | solution.py:484
  11.6 2.1 %collective-permute-start.2 = (f32[2,136,128]{2,1,0:T(8,128)S(1)}, f32[2,136,128]{2,1,0:T(8,128)S(1)}, u32[]{:S(2)}, u32[]{:S(2)}) collective-permute-start(f32[2,136,128]{2,1,0:T(8,128)S(1)} %get-tuple-element.27.refs_4_), channel_id=1, source_target_pairs={{0,12},{4,8},{8,4},{12,0},{16,28},{20,24},{24,20},{28,16},{1,13},{... | collective-permute-start | bytes 417800 | tf_op jit(solution)/shard_map/ppermute | solution.py:484
  13.9 2.6 %collective-permute-start.6 = (f32[2,128,128]{2,1,0:T(8,128)S(1)}, f32[2,128,128]{2,1,0:T(8,128)S(1)}, u32[]{:S(2)}, u32[]{:S(2)}) collective-permute-start(f32[2,128,128]{2,1,0:T(8,128)S(1)} %group_total.2.refs_0_.refs_4_), channel_id=1, source_target_pairs={{0,16},{4,20},{8,24},{12,28},{16,0},{20,4},{24,8},{28,12},{1,17},{... | collective-permute-start | bytes 393224 | tf_op jit(solution)/shard_map/ppermute | solution.py:500
  16.6 1.1 %intra_block.3.refs_0_ = f32[512,512]{1,0:T(8,128)S(1)} custom-call(bf16[512,2048]{1,0:T(8,128)(2,1)S(1)} %copy-done.2, bf16[512,2048]{1,0:T(8,128)(2,1)S(1)} %copy-done, bf16[512,2048]{1,0:T(8,128)(2,1)S(1)} %copy-done.1, f32[2,128,128]{2,1,0:T(8,128)S(1)} %group_total.2.refs_0_.refs_4_), custom_call_target="tpu_custom_call" | custom-call | flops 536870912 | bytes 2621440 | tf_op jit(solution)/shard_map/intra_block/pallas_call | solution.py:219
  17.7 1.1 %intra_block.4.refs_6_.refs_1_ = f32[512,512]{1,0:T(8,128)S(1)} custom-call(bf16[512,2048]{1,0:T(8,128)(2,1)S(1)} %copy-done.2, bf16[512,2048]{1,0:T(8,128)(2,1)S(1)} %copy-done, bf16[512,2048]{1,0:T(8,128)(2,1)S(1)} %copy-done.1, f32[512,512]{1,0:T(8,128)S(1)} %intra_block.3.refs_0_), custom_call_target="tpu_custom_call" | custom-call | flops 536870912 | bytes 2621440 | tf_op jit(solution)/shard_map/intra_block/pallas_call | solution.py:219
  18.8 2.1 %collective-permute-done.6.refs_5_ = f32[2,128,128]{2,1,0:T(8,128)S(1)} collective-permute-done((f32[2,128,128]{2,1,0:T(8,128)S(1)}, f32[2,128,128]{2,1,0:T(8,128)S(1)}, u32[]{:S(2)}, u32[]{:S(2)}) %collective-permute-start.6) | collective-permute-done | bytes 131104 | tf_op jit(solution)/shard_map/ppermute | solution.py:500
  21.2 1.1 %collective-permute-start.11 = (f32[2,136,128]{2,1,0:T(8,128)S(1)}, f32[2,136,128]{2,1,0:T(8,128)S(1)}, u32[]{:S(2)}, u32[]{:S(2)}) collective-permute-start(f32[2,136,128]{2,1,0:T(8,128)S(1)} %get-tuple-element.36), channel_id=1, source_target_pairs={{0,4},{4,0},{8,12},{12,8},{16,20},{20,16},{24,28},{28,24},{1,5},{5... | collective-permute-start | bytes 417800 | tf_op jit(solution)/shard_map/ppermute | solution.py:484
  22.4 2.9 %collective-permute-start.7 = (f32[2,128,128]{2,1,0:T(8,128)S(1)}, f32[2,128,128]{2,1,0:T(8,128)S(1)}, u32[]{:S(2)}, u32[]{:S(2)}) collective-permute-start(f32[2,128,128]{2,1,0:T(8,128)S(1)} %group_total.3.refs_0_.refs_4_), channel_id=1, source_target_pairs={{0,16},{4,20},{8,24},{12,28},{16,0},{20,4},{24,8},{28,12},{1,17},{... | collective-permute-start | bytes 393224 | tf_op jit(solution)/shard_map/ppermute | solution.py:500
  25.3 3.0 %collective-permute-start.12 = (f32[2,136,128]{2,1,0:T(8,128)S(1)}, f32[2,136,128]{2,1,0:T(8,128)S(1)}, u32[]{:S(2)}, u32[]{:S(2)}) collective-permute-start(f32[2,136,128]{2,1,0:T(8,128)S(1)} %get-tuple-element.37), channel_id=1, source_target_pairs={{0,8},{4,12},{8,0},{12,4},{16,24},{20,28},{24,16},{28,20},{1,9},{5... | collective-permute-start | bytes 417800 | tf_op jit(solution)/shard_map/ppermute | solution.py:484
  28.4 2.3 %suffix_part.1.refs_6_.extra_ref = f32[8,2048]{1,0:T(8,128)S(1)} custom-call(s32[4]{0:T(128)S(1)} %copy-done.9, bf16[2,4,2048]{2,1,0:T(4,128)(2,1)S(1)} %copy-done.5, bf16[4,128,2048]{2,1,0:T(8,128)(2,1)S(1)} %copy-done.3, bf16[4,128,2048]{2,1,0:T(8,128)(2,1)S(1)} %copy-done.4, bf16[2,4,2048]{2,1,0:T(4,128)(2,1)S(1)} %copy-done.6, ...), custom_call_target="tpu_custom_call" | custom-call | flops 67108864 | bytes 4194304 | tf_op jit(solution)/shard_map/suffix_part/pallas_call | solution.py:289
  30.7 0.3 priors.3
  31.0 1.3 %collective-permute-start.8 = (f32[2,136,128]{2,1,0:T(8,128)S(1)}, f32[2,136,128]{2,1,0:T(8,128)S(1)}, u32[]{:S(2)}, u32[]{:S(2)}) collective-permute-start(f32[2,136,128]{2,1,0:T(8,128)S(1)} %get-tuple-element.33), channel_id=1, source_target_pairs={{0,4},{4,0},{8,12},{12,8},{16,20},{20,16},{24,28},{28,24},{1,5},{5... | collective-permute-start | bytes 417800 | tf_op jit(solution)/shard_map/ppermute | solution.py:484
  32.4 2.1 %collective-permute-start.9 = (f32[2,136,128]{2,1,0:T(8,128)S(1)}, f32[2,136,128]{2,1,0:T(8,128)S(1)}, u32[]{:S(2)}, u32[]{:S(2)}) collective-permute-start(f32[2,136,128]{2,1,0:T(8,128)S(1)} %get-tuple-element.34), channel_id=1, source_target_pairs={{0,8},{4,12},{8,0},{12,4},{16,24},{20,28},{24,16},{28,20},{1,9},{5... | collective-permute-start | bytes 417800 | tf_op jit(solution)/shard_map/ppermute | solution.py:484
  34.4 0.3 collective-permute-start.10
  34.7 1.9 %intra_block.5.refs_0_ = f32[512,1024]{1,0:T(8,128)S(1)} custom-call(bf16[512,2048]{1,0:T(8,128)(2,1)S(1)} %copy-done.2, bf16[512,2048]{1,0:T(8,128)(2,1)S(1)} %copy-done, bf16[512,2048]{1,0:T(8,128)(2,1)S(1)} %copy-done.1, f32[2,136,128]{2,1,0:T(8,128)S(1)} %get-tuple-element.31.refs_0_), custom_call_target="tpu_custom_call" | custom-call | flops 1073741824 | bytes 5242880 | tf_op jit(solution)/shard_map/intra_block/pallas_call | solution.py:219
  36.7 0.7 %attend.2 = (f32[512,1024]{1,0:T(8,128)S(1)}, f32[8,1024]{1,0:T(8,128)S(1)}, f32[640,128]{1,0:T(8,128)S(1)}) custom-call(bf16[512,2048]{1,0:T(8,128)(2,1)S(1)} %copy-done.2, f32[8,2048]{1,0:T(8,128)S(1)} %suffix_part.1.refs_6_.extra_ref, f32[512,512]{1,0:T(8,128)S(1)} %intra_block.3.refs_0_, f32[512,512]{1,0:T(8,128)S(1)} %intra_block.4.refs_6_.refs_1_, ...), custom_call_target="tpu_custom_call" | custom-call | flops 134217728 | bytes 5242880 | tf_op jit(solution)/shard_map/attend/pallas_call | solution.py:355
  37.3 0.7 %collective-permute-done.8.refs_2_ = f32[2,136,128]{2,1,0:T(8,128)S(1)} collective-permute-done((f32[2,136,128]{2,1,0:T(8,128)S(1)}, f32[2,136,128]{2,1,0:T(8,128)S(1)}, u32[]{:S(2)}, u32[]{:S(2)}) %collective-permute-start.8) | collective-permute-done | bytes 139296 | tf_op jit(solution)/shard_map/ppermute | solution.py:484
  38.1 0.9 %collective-permute-done.9.refs_3_ = f32[2,136,128]{2,1,0:T(8,128)S(1)} collective-permute-done((f32[2,136,128]{2,1,0:T(8,128)S(1)}, f32[2,136,128]{2,1,0:T(8,128)S(1)}, u32[]{:S(2)}, u32[]{:S(2)}) %collective-permute-start.9) | collective-permute-done | bytes 139296 | tf_op jit(solution)/shard_map/ppermute | solution.py:484
  39.0 2.2 %collective-permute-done.10.refs_4_ = f32[2,136,128]{2,1,0:T(8,128)S(1)} collective-permute-done((f32[2,136,128]{2,1,0:T(8,128)S(1)}, f32[2,136,128]{2,1,0:T(8,128)S(1)}, u32[]{:S(2)}, u32[]{:S(2)}) %collective-permute-start.10) | collective-permute-done | bytes 139296 | tf_op jit(solution)/shard_map/ppermute | solution.py:484
  41.1 0.6 %attend.3 = (f32[512,1024]{1,0:T(8,128)S(1)}, f32[8,1024]{1,0:T(8,128)S(1)}, f32[1,640]{1,0:T(1,128)S(1)}) custom-call(bf16[512,2048]{1,0:T(8,128)(2,1)S(1)} %copy-done.2, f32[8,2048]{1,0:T(8,128)S(1)} %suffix_part.1.refs_6_.extra_ref, f32[512,1024]{1,0:T(8,128)S(1)} %intra_block.5.refs_0_, f32[2,136,128]{2,1,0:T(8,128)S(1)} %get-tuple-element.32.refs_1_, ...), custom_call_target="tpu_custom_call" | custom-call | flops 134217728 | bytes 5242880 | tf_op jit(solution)/shard_map/attend/pallas_call | solution.py:355
  41.8 1.6 %collective-permute-start.15 = (f32[1,640]{1,0:T(1,128)S(1)}, f32[1,640]{1,0:T(1,128)S(1)}, u32[]{:S(2)}, u32[]{:S(2)}) collective-permute-start(f32[1,640]{1,0:T(1,128)S(1)} %get-tuple-element.39.refs_0_), channel_id=1, source_target_pairs={{0,2},{1,3},{2,0},{3,1},{4,6},{5,7},{6,4},{7,5},{8,10},{9,11},{10,... | collective-permute-start | bytes 7688 | tf_op jit(solution)/shard_map/ppermute | solution.py:582
  43.4 0.3 collective-permute-start.14
  43.6 1.2 %collective-permute-done.16.refs_3_ = f32[1,640]{1,0:T(1,128)S(1)} collective-permute-done((f32[1,640]{1,0:T(1,128)S(1)}, f32[1,640]{1,0:T(1,128)S(1)}, u32[]{:S(2)}, u32[]{:S(2)}) %collective-permute-start.16) | collective-permute-done | bytes 2592 | tf_op jit(solution)/shard_map/ppermute | solution.py:582
  44.8 0.7 %collective-permute-done.15.refs_2_ = f32[1,640]{1,0:T(1,128)S(1)} collective-permute-done((f32[1,640]{1,0:T(1,128)S(1)}, f32[1,640]{1,0:T(1,128)S(1)}, u32[]{:S(2)}, u32[]{:S(2)}) %collective-permute-start.15) | collective-permute-done | bytes 2592 | tf_op jit(solution)/shard_map/ppermute | solution.py:582
  45.5 1.7 %normalize.1 = (bf16[512,2048]{1,0:T(8,128)(2,1)}, bf16[2,4,2048]{2,1,0:T(4,128)(2,1)}) custom-call(f32[1,2048]{1,0:T(1,128)S(1)} %bitcast.1, f32[1,640]{1,0:T(1,128)S(1)} %get-tuple-element.39.refs_0_, f32[1,640]{1,0:T(1,128)S(1)} %collective-permute-done.14.refs_1_, f32[1,640]{1,0:T(1,128)S(1)} %collective-permute-done.15.refs_2_, ...), custom_call_target="tpu_custom_call" | custom-call | bytes 6291456 | tf_op jit(solution)/shard_map/normalize/pallas_call | solution.py:415
  (36 shorter events, 0.8 us)
Async XLA Ops:
  0.6 5.6 %copy-start.1 = (bf16[512,2048]{1,0:T(8,128)(2,1)S(1)}, bf16[512,2048]{1,0:T(8,128)(2,1)}, u32[]{:S(2)}) copy-start(bf16[512,2048]{1,0:T(8,128)(2,1)} %v_ref.11) | copy-start | bytes 6291460
  0.6 5.6 %copy-start = (bf16[512,2048]{1,0:T(8,128)(2,1)S(1)}, bf16[512,2048]{1,0:T(8,128)(2,1)}, u32[]{:S(2)}) copy-start(bf16[512,2048]{1,0:T(8,128)(2,1)} %k_ref.11) | copy-start | bytes 6291460
  0.7 5.6 %copy-start.5 = (bf16[2,4,2048]{2,1,0:T(4,128)(2,1)S(1)}, bf16[2,4,2048]{2,1,0:T(4,128)(2,1)}, u32[]{:S(2)}) copy-start(bf16[2,4,2048]{2,1,0:T(4,128)(2,1)} %q_ref.12) | copy-start | bytes 98308
  2.2 9.4 %collective-permute-start.5 = (f32[2,136,128]{2,1,0:T(8,128)S(1)}, f32[2,136,128]{2,1,0:T(8,128)S(1)}, u32[]{:S(2)}, u32[]{:S(2)}) collective-permute-start(f32[2,136,128]{2,1,0:T(8,128)S(1)} %fetched_states.1.refs_0_), channel_id=1, source_target_pairs={{0,12},{4,8},{8,4},{12,0},{16,28},{20,24},{24,20},{28,16},{1,13},{... | collective-permute-start | bytes 417800 | tf_op jit(solution)/shard_map/ppermute | solution.py:484
  6.8 6.9 %collective-permute-start.3 = (f32[2,136,128]{2,1,0:T(8,128)S(1)}, f32[2,136,128]{2,1,0:T(8,128)S(1)}, u32[]{:S(2)}, u32[]{:S(2)}) collective-permute-start(f32[2,136,128]{2,1,0:T(8,128)S(1)} %get-tuple-element.29), channel_id=1, source_target_pairs={{0,4},{4,0},{8,12},{12,8},{16,20},{20,16},{24,28},{28,24},{1,5},{5... | collective-permute-start | bytes 417800 | tf_op jit(solution)/shard_map/ppermute | solution.py:484
  7.3 9.3 %copy-start.2 = (bf16[512,2048]{1,0:T(8,128)(2,1)S(1)}, bf16[512,2048]{1,0:T(8,128)(2,1)}, u32[]{:S(2)}) copy-start(bf16[512,2048]{1,0:T(8,128)(2,1)} %q_ref.15) | copy-start | bytes 6291460
  7.3 6.6 %collective-permute-start.4 = (f32[2,136,128]{2,1,0:T(8,128)S(1)}, f32[2,136,128]{2,1,0:T(8,128)S(1)}, u32[]{:S(2)}, u32[]{:S(2)}) collective-permute-start(f32[2,136,128]{2,1,0:T(8,128)S(1)} %get-tuple-element.23.refs_0_), channel_id=1, source_target_pairs={{0,8},{4,12},{8,0},{12,4},{16,24},{20,28},{24,16},{28,20},{1,9},{5... | collective-permute-start | bytes 417800 | tf_op jit(solution)/shard_map/ppermute | solution.py:484
  8.8 13.5 %collective-permute-start = (f32[2,136,128]{2,1,0:T(8,128)S(1)}, f32[2,136,128]{2,1,0:T(8,128)S(1)}, u32[]{:S(2)}, u32[]{:S(2)}) collective-permute-start(f32[2,136,128]{2,1,0:T(8,128)S(1)} %get-tuple-element.25), channel_id=1, source_target_pairs={{0,4},{4,0},{8,12},{12,8},{16,20},{20,16},{24,28},{28,24},{1,5},{5... | collective-permute-start | bytes 417800 | tf_op jit(solution)/shard_map/ppermute | solution.py:484
  10.0 12.3 %collective-permute-start.1 = (f32[2,136,128]{2,1,0:T(8,128)S(1)}, f32[2,136,128]{2,1,0:T(8,128)S(1)}, u32[]{:S(2)}, u32[]{:S(2)}) collective-permute-start(f32[2,136,128]{2,1,0:T(8,128)S(1)} %get-tuple-element.26), channel_id=1, source_target_pairs={{0,8},{4,12},{8,0},{12,4},{16,24},{20,28},{24,16},{28,20},{1,9},{5... | collective-permute-start | bytes 417800 | tf_op jit(solution)/shard_map/ppermute | solution.py:484
  11.6 10.8 %collective-permute-start.2 = (f32[2,136,128]{2,1,0:T(8,128)S(1)}, f32[2,136,128]{2,1,0:T(8,128)S(1)}, u32[]{:S(2)}, u32[]{:S(2)}) collective-permute-start(f32[2,136,128]{2,1,0:T(8,128)S(1)} %get-tuple-element.27.refs_4_), channel_id=1, source_target_pairs={{0,12},{4,8},{8,4},{12,0},{16,28},{20,24},{24,20},{28,16},{1,13},{... | collective-permute-start | bytes 417800 | tf_op jit(solution)/shard_map/ppermute | solution.py:484
  13.9 7.0 %collective-permute-start.6 = (f32[2,128,128]{2,1,0:T(8,128)S(1)}, f32[2,128,128]{2,1,0:T(8,128)S(1)}, u32[]{:S(2)}, u32[]{:S(2)}) collective-permute-start(f32[2,128,128]{2,1,0:T(8,128)S(1)} %group_total.2.refs_0_.refs_4_), channel_id=1, source_target_pairs={{0,16},{4,20},{8,24},{12,28},{16,0},{20,4},{24,8},{28,12},{1,17},{... | collective-permute-start | bytes 393224 | tf_op jit(solution)/shard_map/ppermute | solution.py:500
  17.7 10.7 %copy-start.4 = (bf16[4,128,2048]{2,1,0:T(8,128)(2,1)S(1)}, bf16[4,128,2048]{2,1,0:T(8,128)(2,1)}, u32[]{:S(2)}) copy-start(bf16[4,128,2048]{2,1,0:T(8,128)(2,1)} %v_ref.10) | copy-start | bytes 6291460
  18.8 9.6 %copy-start.3 = (bf16[4,128,2048]{2,1,0:T(8,128)(2,1)S(1)}, bf16[4,128,2048]{2,1,0:T(8,128)(2,1)}, u32[]{:S(2)}) copy-start(bf16[4,128,2048]{2,1,0:T(8,128)(2,1)} %k_ref.10) | copy-start | bytes 6291460
  18.8 9.6 %copy-start.6 = (bf16[2,4,2048]{2,1,0:T(4,128)(2,1)S(1)}, bf16[2,4,2048]{2,1,0:T(4,128)(2,1)}, u32[]{:S(2)}) copy-start(bf16[2,4,2048]{2,1,0:T(4,128)(2,1)} %sk_ref.1) | copy-start | bytes 98308
  18.8 9.6 %copy-start.7 = (bf16[2,4,2048]{2,1,0:T(4,128)(2,1)S(1)}, bf16[2,4,2048]{2,1,0:T(4,128)(2,1)}, u32[]{:S(2)}) copy-start(bf16[2,4,2048]{2,1,0:T(4,128)(2,1)} %sv_ref.1) | copy-start | bytes 98308
  18.8 9.6 %copy-start.9 = (s32[4]{0:T(128)S(1)}, s32[4]{0:T(128)}, u32[]{:S(2)}) copy-start(s32[4]{0:T(128)} %lengths_ref.1) | copy-start | bytes 52
  21.2 13.2 %collective-permute-start.11 = (f32[2,136,128]{2,1,0:T(8,128)S(1)}, f32[2,136,128]{2,1,0:T(8,128)S(1)}, u32[]{:S(2)}, u32[]{:S(2)}) collective-permute-start(f32[2,136,128]{2,1,0:T(8,128)S(1)} %get-tuple-element.36), channel_id=1, source_target_pairs={{0,4},{4,0},{8,12},{12,8},{16,20},{20,16},{24,28},{28,24},{1,5},{5... | collective-permute-start | bytes 417800 | tf_op jit(solution)/shard_map/ppermute | solution.py:484
  22.4 8.3 %collective-permute-start.7 = (f32[2,128,128]{2,1,0:T(8,128)S(1)}, f32[2,128,128]{2,1,0:T(8,128)S(1)}, u32[]{:S(2)}, u32[]{:S(2)}) collective-permute-start(f32[2,128,128]{2,1,0:T(8,128)S(1)} %group_total.3.refs_0_.refs_4_), channel_id=1, source_target_pairs={{0,16},{4,20},{8,24},{12,28},{16,0},{20,4},{24,8},{28,12},{1,17},{... | collective-permute-start | bytes 393224 | tf_op jit(solution)/shard_map/ppermute | solution.py:500
  25.3 11.4 %collective-permute-start.12 = (f32[2,136,128]{2,1,0:T(8,128)S(1)}, f32[2,136,128]{2,1,0:T(8,128)S(1)}, u32[]{:S(2)}, u32[]{:S(2)}) collective-permute-start(f32[2,136,128]{2,1,0:T(8,128)S(1)} %get-tuple-element.37), channel_id=1, source_target_pairs={{0,8},{4,12},{8,0},{12,4},{16,24},{20,28},{24,16},{28,20},{1,9},{5... | collective-permute-start | bytes 417800 | tf_op jit(solution)/shard_map/ppermute | solution.py:484
  28.3 8.4 %collective-permute-start.13 = (f32[2,136,128]{2,1,0:T(8,128)S(1)}, f32[2,136,128]{2,1,0:T(8,128)S(1)}, u32[]{:S(2)}, u32[]{:S(2)}) collective-permute-start(f32[2,136,128]{2,1,0:T(8,128)S(1)} %get-tuple-element.30.refs_4_), channel_id=1, source_target_pairs={{0,12},{4,8},{8,4},{12,0},{16,28},{20,24},{24,20},{28,16},{1,13},{... | collective-permute-start | bytes 417800 | tf_op jit(solution)/shard_map/ppermute | solution.py:484
  31.0 7.0 %collective-permute-start.8 = (f32[2,136,128]{2,1,0:T(8,128)S(1)}, f32[2,136,128]{2,1,0:T(8,128)S(1)}, u32[]{:S(2)}, u32[]{:S(2)}) collective-permute-start(f32[2,136,128]{2,1,0:T(8,128)S(1)} %get-tuple-element.33), channel_id=1, source_target_pairs={{0,4},{4,0},{8,12},{12,8},{16,20},{20,16},{24,28},{28,24},{1,5},{5... | collective-permute-start | bytes 417800 | tf_op jit(solution)/shard_map/ppermute | solution.py:484
  32.4 6.6 %collective-permute-start.9 = (f32[2,136,128]{2,1,0:T(8,128)S(1)}, f32[2,136,128]{2,1,0:T(8,128)S(1)}, u32[]{:S(2)}, u32[]{:S(2)}) collective-permute-start(f32[2,136,128]{2,1,0:T(8,128)S(1)} %get-tuple-element.34), channel_id=1, source_target_pairs={{0,8},{4,12},{8,0},{12,4},{16,24},{20,28},{24,16},{28,20},{1,9},{5... | collective-permute-start | bytes 417800 | tf_op jit(solution)/shard_map/ppermute | solution.py:484
  34.4 6.7 %collective-permute-start.10 = (f32[2,136,128]{2,1,0:T(8,128)S(1)}, f32[2,136,128]{2,1,0:T(8,128)S(1)}, u32[]{:S(2)}, u32[]{:S(2)}) collective-permute-start(f32[2,136,128]{2,1,0:T(8,128)S(1)} %get-tuple-element.31.refs_0_), channel_id=1, source_target_pairs={{0,12},{4,8},{8,4},{12,0},{16,28},{20,24},{24,20},{28,16},{1,13},{... | collective-permute-start | bytes 417800 | tf_op jit(solution)/shard_map/ppermute | solution.py:484
  41.1 4.3 %copy-start.8 = (f32[2048]{0:T(1024)S(1)}, f32[2048]{0:T(1024)}, u32[]{:S(2)}) copy-start(f32[2048]{0:T(1024)} %param.19) | copy-start | bytes 24580
  41.7 3.1 %collective-permute-start.16 = (f32[1,640]{1,0:T(1,128)S(1)}, f32[1,640]{1,0:T(1,128)S(1)}, u32[]{:S(2)}, u32[]{:S(2)}) collective-permute-start(f32[1,640]{1,0:T(1,128)S(1)} %get-tuple-element.39.refs_0_), channel_id=1, source_target_pairs={{0,3},{1,2},{2,1},{3,0},{4,7},{5,6},{6,5},{7,4},{8,11},{9,10},{10,... | collective-permute-start | bytes 7688 | tf_op jit(solution)/shard_map/ppermute | solution.py:582
  41.8 3.7 %collective-permute-start.15 = (f32[1,640]{1,0:T(1,128)S(1)}, f32[1,640]{1,0:T(1,128)S(1)}, u32[]{:S(2)}, u32[]{:S(2)}) collective-permute-start(f32[1,640]{1,0:T(1,128)S(1)} %get-tuple-element.39.refs_0_), channel_id=1, source_target_pairs={{0,2},{1,3},{2,0},{3,1},{4,6},{5,7},{6,4},{7,5},{8,10},{9,11},{10,... | collective-permute-start | bytes 7688 | tf_op jit(solution)/shard_map/ppermute | solution.py:582
  43.4 2.1 %collective-permute-start.14 = (f32[1,640]{1,0:T(1,128)S(1)}, f32[1,640]{1,0:T(1,128)S(1)}, u32[]{:S(2)}, u32[]{:S(2)}) collective-permute-start(f32[1,640]{1,0:T(1,128)S(1)} %get-tuple-element.39.refs_0_), channel_id=1, source_target_pairs={{0,1},{1,0},{2,3},{3,2},{4,5},{5,4},{6,7},{7,6},{8,9},{9,8},{10,11... | collective-permute-start | bytes 7688 | tf_op jit(solution)/shard_map/ppermute | solution.py:582

commit v6 on v5

--- a/solution.py
+++ b/solution.py
@@ -297,9 +297,9 @@
     )(lengths, step_queries, suffix_keys, suffix_values, step_keys, step_values, *after)
 
 
-def attended_kernel(group, pieces, each, heads, first, last, q_ref, extra_ref, *refs):
+def attended_kernel(group, owners, pieces, each, heads, first, last, q_ref, extra_ref, *refs):
     intra_refs, refs = refs[:pieces], refs[pieces:]
-    parts = refs[:group]
+    parts = dict(zip(owners, refs))
     att_ref, raw_ref, sum_ref, acc_ref = refs[-4:]
     rows = q_ref.shape[0]
     dec = extra_ref.shape[0]
@@ -307,8 +307,8 @@
     if first:
         acc_ref[...] = jnp.zeros_like(acc_ref)
     else:
-        acc_ref[...] = refs[group][...]
-    for m in range(group):
+        acc_ref[...] = refs[len(owners)][...]
+    for m in owners:
         all_cols = owned_cols(group, m, each, heads)
         own_cols = owned_cols(group, m, count, (0, count))
         query = q_ref[:, all_cols]
@@ -345,16 +345,17 @@
         sum_ref[...] = acc_ref[...]
 
 
-def attend(each, heads, last, queries, intra, extra, parts, before, after):
+def attend(owners, each, heads, last, queries, intra, extra, parts, before, begun):
     group = len(parts)
+    parts = [parts[m] for m in owners]
     wide = group * (heads[1] - heads[0]) * HEAD_DIM
     rows, dec = queries.shape[0], extra.shape[0]
     pieces = len(intra)
     padded = -(-(rows + dec) // LANES) * LANES
     sums = (1, padded) if last else (padded, LANES)
     return pl.pallas_call(
-        functools.partial(attended_kernel, group, pieces, each, heads, not before, last),
-        in_specs=[VMEM] * (2 + pieces + group + len(before)) + [ANY] * len(after),
+        functools.partial(attended_kernel, group, owners, pieces, each, heads, not before, last),
+        in_specs=[VMEM] * (2 + pieces + len(owners) + len(before) + len(begun)),
         out_specs=[VMEM] * 3,
         out_shape=[
             jax.ShapeDtypeStruct((rows, wide), F32),
@@ -364,8 +365,29 @@
         scratch_shapes=[pltpu.VMEM((padded, LANES), F32)],
         compiler_params=params(),
         cost_estimate=cost(2 * rows * wide * HEAD_DIM, 10 * rows * wide),
+        input_output_aliases={2 + pieces + len(owners) + len(before) + i: i for i in range(len(begun))},
         name="attend",
-    )(queries, extra, *intra, *parts, *before, *after)
+    )(queries, extra, *intra, *parts, *before, *begun)
+
+
+def gain_kernel(heads, gain_ref, *refs):
+    chunks = len(heads)
+    for c in range(chunks):
+        for h, head in enumerate(heads[c]):
+            cols = head_cols(h)
+            refs[chunks + c][:, cols] = refs[c][:, cols] * gain_ref[:, head_cols(head)]
+
+
+def gained(heads, atts, gain):
+    return pl.pallas_call(
+        functools.partial(gain_kernel, heads),
+        in_specs=[VMEM] * (1 + len(atts)),
+        out_specs=[VMEM] * len(atts),
+        out_shape=[jax.ShapeDtypeStruct(att.shape, F32) for att in atts],
+        compiler_params=params(),
+        cost_estimate=cost(0, 8 * sum(att.size for att in atts)),
+        name="gained",
+    )(gain[None, :], *atts)
 
 
 def norm_kernel(heads, sums, width, tile, gain_ref, *refs):
@@ -389,9 +411,7 @@
         for c in range(chunks):
             for h, head in enumerate(heads[c]):
                 at = head_cols(head)
-                buf_ref[here, at] = (
-                    att_refs[c][here, head_cols(h)] * row_scale * gain_ref[:, at]
-                ).astype(BF16)
+                buf_ref[here, at] = (att_refs[c][here, head_cols(h)] * row_scale).astype(BF16)
         copies.append(pltpu.make_async_copy(buf_ref.at[here], out_hbm.at[here], sems.at[i]))
         copies[-1].start()
         if i == 0:
@@ -564,18 +584,25 @@
             )
             last = [extra]
         elif kind == "a" and c < len(done_heads):
-            atts[c], raws[c], total = attend(
-                each,
-                done_heads[c],
-                c == len(done_heads) - 1,
-                queries,
-                intras[c],
-                extra,
-                entering[c],
-                sums,
-                [],
-            )
-            sums = [total]
+            last_chunk = c == len(done_heads) - 1
+            begun = []
+            near = group // 2 if last_chunk else group
+            for some in ([*range(near)], [*range(near, group)]):
+                if some:
+                    *begun, total = attend(
+                        some,
+                        each,
+                        done_heads[c],
+                        last_chunk and group - 1 in some,
+                        queries,
+                        intras[c],
+                        extra,
+                        entering[c],
+                        sums,
+                        begun,
+                    )
+                    sums = [total]
+            atts[c], raws[c] = begun
     row = lax.axis_size("head")
     step = (lambda i, k: i ^ k) if row & (row - 1) == 0 else (lambda i, k: (i + k) % row)
     all_sums = sums + [
@@ -584,7 +611,7 @@
     return tuple(
         normalize(
             chunk_heads,
-            [atts[c] for c in range(len(done_heads))],
+            gained(chunk_heads, [atts[c] for c in range(len(done_heads))], norm_gain),
             [raws[c] for c in range(len(done_heads))],
             all_sums,
             norm_gain,

time: 47.3 us -> 46.9 us (level)
  starting transfers between devices: 25.7 us -> 24.6 us
  Pallas kernels: 12.6 us -> 13.2 us
    ppermute x12, starting transfers between devices: 18.3 us -> 17.4 us  [swap(): lax.ppermute(messages[m], 'seq', [(i, i // group * group + (i % group ^ m...]
    pallas_call x2 -> x4, Pallas kernels: 1.23 us -> 1.91 us  [the longest x3 1.36 us: attend(): pl.pallas_call(functools.partial(attended_kernel, group, owners, pieces,...]
    ppermute x12, waiting for transfers between devices: 4.03 us -> 4.68 us  [swap(): lax.ppermute(messages[m], 'seq', [(i, i // group * group + (i % group ^ m...]
    ppermute x3, waiting for transfers between devices: 1.81 us -> 1.25 us  [on_device(): lax.ppermute(sums[0], 'head', [(i, step(i, k)) for i in range(row)])]
  transfers between devices with their start and end apart: 17 -> 17, of which waited for: 7 -> 8; matrix products, arithmetic and copies ran while one was open for 0% -> 0% of each run, Pallas kernels for 19% -> 21%
where the time goes in v6:
time: 46.9 us; the launch traced here: 46.8 us
  starting transfers between devices  24.6 us (52%)
  Pallas kernels  13.2 us (28%)
  waiting for transfers between devices  8.04 us (17%)
  between operations  0.82 us (2%)
    ppermute x12, starting transfers between devices, swap(): lax.ppermute(messages[m], 'seq', [(i, i // group * group + (i % group ^ m...  17.4 us
    ppermute x2, starting transfers between devices, across(): lax.ppermute(total, 'seq', [(i, (i + k * group) % devices) for i in range...  5.27 us
    ppermute x12, waiting for transfers between devices, swap(): lax.ppermute(messages[m], 'seq', [(i, i // group * group + (i % group ^ m...  4.68 us
    pallas_call x3, Pallas kernels, intra_block(): pl.pallas_call(functools.partial(intra_kernel, tile, heads), in_specs=[VM...  4.08 us
    pallas_call x1, Pallas kernels, suffix_part(): pl.pallas_call(suffix_kernel, in_specs=[SMEM] + [VMEM] * 5 + [ANY] * len(...  2.29 us
    ppermute x2, waiting for transfers between devices, across(): lax.ppermute(total, 'seq', [(i, (i + k * group) % devices) for i in range...  2.12 us
    ppermute x3, starting transfers between devices, on_device(): lax.ppermute(sums[0], 'head', [(i, step(i, k)) for i in range(row)])  1.92 us
    pallas_call x1, Pallas kernels, normalize(): pl.pallas_call(functools.partial(norm_kernel, heads, len(sums), width_all...  1.63 us
  transfers between devices with their start and end apart: 17, of which 8 were waited for; matrix products, arithmetic and copies ran while one was open for 0% of the time, Pallas kernels for 21%

profile of v6, /device:TPU:0, one launch (start us, length us, event | category | flops | bytes accessed | tf_op | source)
XLA Modules:
  0.0 46.8 jit_solution(15585068191701487074)
XLA Ops:
  0.7 1.5 %fetched_states.1.refs_0_ = f32[2,136,128]{2,1,0:T(8,128)S(1)} custom-call(bf16[2,4,2048]{2,1,0:T(4,128)(2,1)} %q_ref.13, bf16[512,2048]{1,0:T(8,128)(2,1)} %k_ref.11, bf16[512,2048]{1,0:T(8,128)(2,1)} %v_ref.11), custom_call_target="tpu_custom_call" | custom-call | flops 33554432 | bytes 524288 | tf_op jit(solution)/shard_map/fetched_states/pallas_call | solution.py:87
  2.2 4.0 %collective-permute-start.5 = (f32[2,136,128]{2,1,0:T(8,128)S(1)}, f32[2,136,128]{2,1,0:T(8,128)S(1)}, u32[]{:S(2)}, u32[]{:S(2)}) collective-permute-start(f32[2,136,128]{2,1,0:T(8,128)S(1)} %fetched_states.1.refs_0_), channel_id=1, source_target_pairs={{0,12},{4,8},{8,4},{12,0},{16,28},{20,24},{24,20},{28,16},{1,13},{... | collective-permute-start | bytes 417800 | tf_op jit(solution)/shard_map/ppermute | solution.py:504
  6.2 0.5 %block_states.2 = (f32[2,136,128]{2,1,0:T(8,128)S(1)}, f32[2,136,128]{2,1,0:T(8,128)S(1)}, f32[2,136,128]{2,1,0:T(8,128)S(1)}) custom-call(bf16[2,4,2048]{2,1,0:T(4,128)(2,1)S(1)} %copy-done.5, bf16[512,2048]{1,0:T(8,128)(2,1)S(1)} %copy-done, bf16[512,2048]{1,0:T(8,128)(2,1)S(1)} %copy-done.1, f32[2,136,128]{2,1,0:T(8,128)S(1)} %fetched_states.1.refs_0_), custom_call_target="tpu_custom_call" | custom-call | flops 100663296 | bytes 1572864 | tf_op jit(solution)/shard_map/block_states/pallas_call | solution.py:121
  6.8 0.6 %collective-permute-start.3 = (f32[2,136,128]{2,1,0:T(8,128)S(1)}, f32[2,136,128]{2,1,0:T(8,128)S(1)}, u32[]{:S(2)}, u32[]{:S(2)}) collective-permute-start(f32[2,136,128]{2,1,0:T(8,128)S(1)} %get-tuple-element.34), channel_id=1, source_target_pairs={{0,4},{4,0},{8,12},{12,8},{16,20},{20,16},{24,28},{28,24},{1,5},{5... | collective-permute-start | bytes 417800 | tf_op jit(solution)/shard_map/ppermute | solution.py:504
  7.3 0.8 %collective-permute-start.4 = (f32[2,136,128]{2,1,0:T(8,128)S(1)}, f32[2,136,128]{2,1,0:T(8,128)S(1)}, u32[]{:S(2)}, u32[]{:S(2)}) collective-permute-start(f32[2,136,128]{2,1,0:T(8,128)S(1)} %get-tuple-element.28.refs_0_), channel_id=1, source_target_pairs={{0,8},{4,12},{8,0},{12,4},{16,24},{20,28},{24,16},{28,20},{1,9},{5... | collective-permute-start | bytes 417800 | tf_op jit(solution)/shard_map/ppermute | solution.py:504
  8.2 0.6 %block_states.3 = (f32[2,136,128]{2,1,0:T(8,128)S(1)}, f32[2,136,128]{2,1,0:T(8,128)S(1)}, f32[2,136,128]{2,1,0:T(8,128)S(1)}, f32[2,136,128]{2,1,0:T(8,128)S(1)}) custom-call(bf16[2,4,2048]{2,1,0:T(4,128)(2,1)S(1)} %copy-done.5, bf16[512,2048]{1,0:T(8,128)(2,1)S(1)} %copy-done, bf16[512,2048]{1,0:T(8,128)(2,1)S(1)} %copy-done.1, ...), custom_call_target="tpu_custom_call" | custom-call | flops 134217728 | bytes 2097152 | tf_op jit(solution)/shard_map/block_states/pallas_call | solution.py:121
  8.8 1.2 %collective-permute-start = (f32[2,136,128]{2,1,0:T(8,128)S(1)}, f32[2,136,128]{2,1,0:T(8,128)S(1)}, u32[]{:S(2)}, u32[]{:S(2)}) collective-permute-start(f32[2,136,128]{2,1,0:T(8,128)S(1)} %get-tuple-element.30), channel_id=1, source_target_pairs={{0,4},{4,0},{8,12},{12,8},{16,20},{20,16},{24,28},{28,24},{1,5},{5... | collective-permute-start | bytes 417800 | tf_op jit(solution)/shard_map/ppermute | solution.py:504
  10.0 1.6 %collective-permute-start.1 = (f32[2,136,128]{2,1,0:T(8,128)S(1)}, f32[2,136,128]{2,1,0:T(8,128)S(1)}, u32[]{:S(2)}, u32[]{:S(2)}) collective-permute-start(f32[2,136,128]{2,1,0:T(8,128)S(1)} %get-tuple-element.31), channel_id=1, source_target_pairs={{0,8},{4,12},{8,0},{12,4},{16,24},{20,28},{24,16},{28,20},{1,9},{5... | collective-permute-start | bytes 417800 | tf_op jit(solution)/shard_map/ppermute | solution.py:504
  11.6 2.1 %collective-permute-start.2 = (f32[2,136,128]{2,1,0:T(8,128)S(1)}, f32[2,136,128]{2,1,0:T(8,128)S(1)}, u32[]{:S(2)}, u32[]{:S(2)}) collective-permute-start(f32[2,136,128]{2,1,0:T(8,128)S(1)} %get-tuple-element.32.refs_4_), channel_id=1, source_target_pairs={{0,12},{4,8},{8,4},{12,0},{16,28},{20,24},{24,20},{28,16},{1,13},{... | collective-permute-start | bytes 417800 | tf_op jit(solution)/shard_map/ppermute | solution.py:504
  13.9 2.6 %collective-permute-start.6 = (f32[2,128,128]{2,1,0:T(8,128)S(1)}, f32[2,128,128]{2,1,0:T(8,128)S(1)}, u32[]{:S(2)}, u32[]{:S(2)}) collective-permute-start(f32[2,128,128]{2,1,0:T(8,128)S(1)} %group_total.2.refs_0_.refs_4_), channel_id=1, source_target_pairs={{0,16},{4,20},{8,24},{12,28},{16,0},{20,4},{24,8},{28,12},{1,17},{... | collective-permute-start | bytes 393224 | tf_op jit(solution)/shard_map/ppermute | solution.py:520
  16.6 1.1 %intra_block.3.refs_0_ = f32[512,512]{1,0:T(8,128)S(1)} custom-call(bf16[512,2048]{1,0:T(8,128)(2,1)S(1)} %copy-done.2, bf16[512,2048]{1,0:T(8,128)(2,1)S(1)} %copy-done, bf16[512,2048]{1,0:T(8,128)(2,1)S(1)} %copy-done.1, f32[2,128,128]{2,1,0:T(8,128)S(1)} %group_total.2.refs_0_.refs_4_), custom_call_target="tpu_custom_call" | custom-call | flops 536870912 | bytes 2621440 | tf_op jit(solution)/shard_map/intra_block/pallas_call | solution.py:219
  17.7 1.1 %intra_block.4.refs_6_.refs_1_ = f32[512,512]{1,0:T(8,128)S(1)} custom-call(bf16[512,2048]{1,0:T(8,128)(2,1)S(1)} %copy-done.2, bf16[512,2048]{1,0:T(8,128)(2,1)S(1)} %copy-done, bf16[512,2048]{1,0:T(8,128)(2,1)S(1)} %copy-done.1, f32[512,512]{1,0:T(8,128)S(1)} %intra_block.3.refs_0_), custom_call_target="tpu_custom_call" | custom-call | flops 536870912 | bytes 2621440 | tf_op jit(solution)/shard_map/intra_block/pallas_call | solution.py:219
  18.8 2.1 %collective-permute-done.6.refs_5_ = f32[2,128,128]{2,1,0:T(8,128)S(1)} collective-permute-done((f32[2,128,128]{2,1,0:T(8,128)S(1)}, f32[2,128,128]{2,1,0:T(8,128)S(1)}, u32[]{:S(2)}, u32[]{:S(2)}) %collective-permute-start.6) | collective-permute-done | bytes 131104 | tf_op jit(solution)/shard_map/ppermute | solution.py:520
  21.2 0.9 %collective-permute-done.2.refs_3_ = f32[2,136,128]{2,1,0:T(8,128)S(1)} collective-permute-done((f32[2,136,128]{2,1,0:T(8,128)S(1)}, f32[2,136,128]{2,1,0:T(8,128)S(1)}, u32[]{:S(2)}, u32[]{:S(2)}) %collective-permute-start.2) | collective-permute-done | bytes 139296 | tf_op jit(solution)/shard_map/ppermute | solution.py:504
  22.2 2.6 %collective-permute-start.7 = (f32[2,128,128]{2,1,0:T(8,128)S(1)}, f32[2,128,128]{2,1,0:T(8,128)S(1)}, u32[]{:S(2)}, u32[]{:S(2)}) collective-permute-start(f32[2,128,128]{2,1,0:T(8,128)S(1)} %group_total.3.refs_0_.refs_4_), channel_id=1, source_target_pairs={{0,16},{4,20},{8,24},{12,28},{16,0},{20,4},{24,8},{28,12},{1,17},{... | collective-permute-start | bytes 393224 | tf_op jit(solution)/shard_map/ppermute | solution.py:520
  24.8 0.5 %collective-permute-start.11 = (f32[2,136,128]{2,1,0:T(8,128)S(1)}, f32[2,136,128]{2,1,0:T(8,128)S(1)}, u32[]{:S(2)}, u32[]{:S(2)}) collective-permute-start(f32[2,136,128]{2,1,0:T(8,128)S(1)} %get-tuple-element.41), channel_id=1, source_target_pairs={{0,4},{4,0},{8,12},{12,8},{16,20},{20,16},{24,28},{28,24},{1,5},{5... | collective-permute-start | bytes 417800 | tf_op jit(solution)/shard_map/ppermute | solution.py:504
  25.3 3.0 %collective-permute-start.12 = (f32[2,136,128]{2,1,0:T(8,128)S(1)}, f32[2,136,128]{2,1,0:T(8,128)S(1)}, u32[]{:S(2)}, u32[]{:S(2)}) collective-permute-start(f32[2,136,128]{2,1,0:T(8,128)S(1)} %get-tuple-element.42), channel_id=1, source_target_pairs={{0,8},{4,12},{8,0},{12,4},{16,24},{20,28},{24,16},{28,20},{1,9},{5... | collective-permute-start | bytes 417800 | tf_op jit(solution)/shard_map/ppermute | solution.py:504
  28.4 2.3 %suffix_part.1.refs_6_.extra_ref = f32[8,2048]{1,0:T(8,128)S(1)} custom-call(s32[4]{0:T(128)S(1)} %copy-done.9, bf16[2,4,2048]{2,1,0:T(4,128)(2,1)S(1)} %copy-done.5, bf16[4,128,2048]{2,1,0:T(8,128)(2,1)S(1)} %copy-done.3, bf16[4,128,2048]{2,1,0:T(8,128)(2,1)S(1)} %copy-done.4, bf16[2,4,2048]{2,1,0:T(4,128)(2,1)S(1)} %copy-done.6, ...), custom_call_target="tpu_custom_call" | custom-call | flops 67108864 | bytes 4194304 | tf_op jit(solution)/shard_map/suffix_part/pallas_call | solution.py:289
  31.0 1.3 %collective-permute-start.10 = (f32[2,136,128]{2,1,0:T(8,128)S(1)}, f32[2,136,128]{2,1,0:T(8,128)S(1)}, u32[]{:S(2)}, u32[]{:S(2)}) collective-permute-start(f32[2,136,128]{2,1,0:T(8,128)S(1)} %get-tuple-element.39), channel_id=1, source_target_pairs={{0,4},{4,0},{8,12},{12,8},{16,20},{20,16},{24,28},{28,24},{1,5},{5... | collective-permute-start | bytes 417800 | tf_op jit(solution)/shard_map/ppermute | solution.py:504
  32.4 2.0 %collective-permute-start.8 = (f32[2,136,128]{2,1,0:T(8,128)S(1)}, f32[2,136,128]{2,1,0:T(8,128)S(1)}, u32[]{:S(2)}, u32[]{:S(2)}) collective-permute-start(f32[2,136,128]{2,1,0:T(8,128)S(1)} %get-tuple-element.37), channel_id=1, source_target_pairs={{0,8},{4,12},{8,0},{12,4},{16,24},{20,28},{24,16},{28,20},{1,9},{5... | collective-permute-start | bytes 417800 | tf_op jit(solution)/shard_map/ppermute | solution.py:504
  34.5 1.9 %intra_block.5.refs_0_ = f32[512,1024]{1,0:T(8,128)S(1)} custom-call(bf16[512,2048]{1,0:T(8,128)(2,1)S(1)} %copy-done.2, bf16[512,2048]{1,0:T(8,128)(2,1)S(1)} %copy-done, bf16[512,2048]{1,0:T(8,128)(2,1)S(1)} %copy-done.1, f32[2,136,128]{2,1,0:T(8,128)S(1)} %get-tuple-element.36.refs_0_), custom_call_target="tpu_custom_call" | custom-call | flops 1073741824 | bytes 5242880 | tf_op jit(solution)/shard_map/intra_block/pallas_call | solution.py:219
  36.5 0.6 %attend.3 = (f32[512,1024]{1,0:T(8,128)S(1)}, f32[8,1024]{1,0:T(8,128)S(1)}, f32[640,128]{1,0:T(8,128)S(1)}) custom-call(bf16[512,2048]{1,0:T(8,128)(2,1)S(1)} %copy-done.2, f32[8,2048]{1,0:T(8,128)S(1)} %suffix_part.1.refs_6_.extra_ref, f32[512,512]{1,0:T(8,128)S(1)} %intra_block.3.refs_0_, f32[512,512]{1,0:T(8,128)S(1)} %intra_block.4.refs_6_.refs_1_, ...), custom_call_target="tpu_custom_call" | custom-call | flops 134217728 | bytes 5242880 | tf_op jit(solution)/shard_map/attend/pallas_call | solution.py:356
  37.1 1.0 %collective-permute-done.10.refs_2_ = f32[2,136,128]{2,1,0:T(8,128)S(1)} collective-permute-done((f32[2,136,128]{2,1,0:T(8,128)S(1)}, f32[2,136,128]{2,1,0:T(8,128)S(1)}, u32[]{:S(2)}, u32[]{:S(2)}) %collective-permute-start.10) | collective-permute-done | bytes 139296 | tf_op jit(solution)/shard_map/ppermute | solution.py:504
  38.1 0.3 attend.4
  38.4 0.6 %collective-permute-done.8.refs_1_ = f32[2,136,128]{2,1,0:T(8,128)S(1)} collective-permute-done((f32[2,136,128]{2,1,0:T(8,128)S(1)}, f32[2,136,128]{2,1,0:T(8,128)S(1)}, u32[]{:S(2)}, u32[]{:S(2)}) %collective-permute-start.8) | collective-permute-done | bytes 139296 | tf_op jit(solution)/shard_map/ppermute | solution.py:504
  39.1 1.9 %collective-permute-done.9.refs_2_ = f32[2,136,128]{2,1,0:T(8,128)S(1)} collective-permute-done((f32[2,136,128]{2,1,0:T(8,128)S(1)}, f32[2,136,128]{2,1,0:T(8,128)S(1)}, u32[]{:S(2)}, u32[]{:S(2)}) %collective-permute-start.9) | collective-permute-done | bytes 139296 | tf_op jit(solution)/shard_map/ppermute | solution.py:504
  41.0 0.4 attend.5
  41.5 1.6 %collective-permute-start.15 = (f32[1,640]{1,0:T(1,128)S(1)}, f32[1,640]{1,0:T(1,128)S(1)}, u32[]{:S(2)}, u32[]{:S(2)}) collective-permute-start(f32[1,640]{1,0:T(1,128)S(1)} %get-tuple-element.47.refs_0_), channel_id=1, source_target_pairs={{0,2},{1,3},{2,0},{3,1},{4,6},{5,7},{6,4},{7,5},{8,10},{9,11},{10,... | collective-permute-start | bytes 7688 | tf_op jit(solution)/shard_map/ppermute | solution.py:609
  43.3 0.6 %gained.1 = (f32[512,1024]{1,0:T(8,128)S(1)}, f32[512,1024]{1,0:T(8,128)S(1)}) custom-call(f32[1,2048]{1,0:T(1,128)S(1)} %bitcast.1, f32[512,1024]{1,0:T(8,128)S(1)} %get-tuple-element.48.refs_0_, f32[512,1024]{1,0:T(8,128)S(1)} %get-tuple-element.49.refs_1_), custom_call_target="tpu_custom_call" | custom-call | bytes 8388608 | tf_op jit(solution)/shard_map/gained/pallas_call | solution.py:382
  43.9 0.6 %collective-permute-done.16.refs_3_ = f32[1,640]{1,0:T(1,128)S(1)} collective-permute-done((f32[1,640]{1,0:T(1,128)S(1)}, f32[1,640]{1,0:T(1,128)S(1)}, u32[]{:S(2)}, u32[]{:S(2)}) %collective-permute-start.16) | collective-permute-done | bytes 2592 | tf_op jit(solution)/shard_map/ppermute | solution.py:609
  44.5 0.7 %collective-permute-done.15.refs_2_ = f32[1,640]{1,0:T(1,128)S(1)} collective-permute-done((f32[1,640]{1,0:T(1,128)S(1)}, f32[1,640]{1,0:T(1,128)S(1)}, u32[]{:S(2)}, u32[]{:S(2)}) %collective-permute-start.15) | collective-permute-done | bytes 2592 | tf_op jit(solution)/shard_map/ppermute | solution.py:609
  45.1 1.6 %normalize.1 = (bf16[512,2048]{1,0:T(8,128)(2,1)}, bf16[2,4,2048]{2,1,0:T(4,128)(2,1)}) custom-call(f32[1,2048]{1,0:T(1,128)S(1)} %bitcast.2, f32[1,640]{1,0:T(1,128)S(1)} %get-tuple-element.47.refs_0_, f32[1,640]{1,0:T(1,128)S(1)} %collective-permute-done.14.refs_1_, f32[1,640]{1,0:T(1,128)S(1)} %collective-permute-done.15.refs_2_, ...), custom_call_target="tpu_custom_call" | custom-call | bytes 6291456 | tf_op jit(solution)/shard_map/normalize/pallas_call | solution.py:435
  (38 shorter events, 1.5 us)
Async XLA Ops:
  0.6 5.6 %copy-start.1 = (bf16[512,2048]{1,0:T(8,128)(2,1)S(1)}, bf16[512,2048]{1,0:T(8,128)(2,1)}, u32[]{:S(2)}) copy-start(bf16[512,2048]{1,0:T(8,128)(2,1)} %v_ref.11) | copy-start | bytes 6291460
  0.6 5.6 %copy-start = (bf16[512,2048]{1,0:T(8,128)(2,1)S(1)}, bf16[512,2048]{1,0:T(8,128)(2,1)}, u32[]{:S(2)}) copy-start(bf16[512,2048]{1,0:T(8,128)(2,1)} %k_ref.11) | copy-start | bytes 6291460
  0.7 5.6 %copy-start.5 = (bf16[2,4,2048]{2,1,0:T(4,128)(2,1)S(1)}, bf16[2,4,2048]{2,1,0:T(4,128)(2,1)}, u32[]{:S(2)}) copy-start(bf16[2,4,2048]{2,1,0:T(4,128)(2,1)} %q_ref.13) | copy-start | bytes 98308
  2.2 9.4 %collective-permute-start.5 = (f32[2,136,128]{2,1,0:T(8,128)S(1)}, f32[2,136,128]{2,1,0:T(8,128)S(1)}, u32[]{:S(2)}, u32[]{:S(2)}) collective-permute-start(f32[2,136,128]{2,1,0:T(8,128)S(1)} %fetched_states.1.refs_0_), channel_id=1, source_target_pairs={{0,12},{4,8},{8,4},{12,0},{16,28},{20,24},{24,20},{28,16},{1,13},{... | collective-permute-start | bytes 417800 | tf_op jit(solution)/shard_map/ppermute | solution.py:504
  6.8 6.9 %collective-permute-start.3 = (f32[2,136,128]{2,1,0:T(8,128)S(1)}, f32[2,136,128]{2,1,0:T(8,128)S(1)}, u32[]{:S(2)}, u32[]{:S(2)}) collective-permute-start(f32[2,136,128]{2,1,0:T(8,128)S(1)} %get-tuple-element.34), channel_id=1, source_target_pairs={{0,4},{4,0},{8,12},{12,8},{16,20},{20,16},{24,28},{28,24},{1,5},{5... | collective-permute-start | bytes 417800 | tf_op jit(solution)/shard_map/ppermute | solution.py:504
  7.3 9.3 %copy-start.2 = (bf16[512,2048]{1,0:T(8,128)(2,1)S(1)}, bf16[512,2048]{1,0:T(8,128)(2,1)}, u32[]{:S(2)}) copy-start(bf16[512,2048]{1,0:T(8,128)(2,1)} %q_ref.17) | copy-start | bytes 6291460
  7.3 6.6 %collective-permute-start.4 = (f32[2,136,128]{2,1,0:T(8,128)S(1)}, f32[2,136,128]{2,1,0:T(8,128)S(1)}, u32[]{:S(2)}, u32[]{:S(2)}) collective-permute-start(f32[2,136,128]{2,1,0:T(8,128)S(1)} %get-tuple-element.28.refs_0_), channel_id=1, source_target_pairs={{0,8},{4,12},{8,0},{12,4},{16,24},{20,28},{24,16},{28,20},{1,9},{5... | collective-permute-start | bytes 417800 | tf_op jit(solution)/shard_map/ppermute | solution.py:504
  8.8 12.4 %collective-permute-start = (f32[2,136,128]{2,1,0:T(8,128)S(1)}, f32[2,136,128]{2,1,0:T(8,128)S(1)}, u32[]{:S(2)}, u32[]{:S(2)}) collective-permute-start(f32[2,136,128]{2,1,0:T(8,128)S(1)} %get-tuple-element.30), channel_id=1, source_target_pairs={{0,4},{4,0},{8,12},{12,8},{16,20},{20,16},{24,28},{28,24},{1,5},{5... | collective-permute-start | bytes 417800 | tf_op jit(solution)/shard_map/ppermute | solution.py:504
  10.0 11.2 %collective-permute-start.1 = (f32[2,136,128]{2,1,0:T(8,128)S(1)}, f32[2,136,128]{2,1,0:T(8,128)S(1)}, u32[]{:S(2)}, u32[]{:S(2)}) collective-permute-start(f32[2,136,128]{2,1,0:T(8,128)S(1)} %get-tuple-element.31), channel_id=1, source_target_pairs={{0,8},{4,12},{8,0},{12,4},{16,24},{20,28},{24,16},{28,20},{1,9},{5... | collective-permute-start | bytes 417800 | tf_op jit(solution)/shard_map/ppermute | solution.py:504
  11.6 10.5 %collective-permute-start.2 = (f32[2,136,128]{2,1,0:T(8,128)S(1)}, f32[2,136,128]{2,1,0:T(8,128)S(1)}, u32[]{:S(2)}, u32[]{:S(2)}) collective-permute-start(f32[2,136,128]{2,1,0:T(8,128)S(1)} %get-tuple-element.32.refs_4_), channel_id=1, source_target_pairs={{0,12},{4,8},{8,4},{12,0},{16,28},{20,24},{24,20},{28,16},{1,13},{... | collective-permute-start | bytes 417800 | tf_op jit(solution)/shard_map/ppermute | solution.py:504
  13.9 7.0 %collective-permute-start.6 = (f32[2,128,128]{2,1,0:T(8,128)S(1)}, f32[2,128,128]{2,1,0:T(8,128)S(1)}, u32[]{:S(2)}, u32[]{:S(2)}) collective-permute-start(f32[2,128,128]{2,1,0:T(8,128)S(1)} %group_total.2.refs_0_.refs_4_), channel_id=1, source_target_pairs={{0,16},{4,20},{8,24},{12,28},{16,0},{20,4},{24,8},{28,12},{1,17},{... | collective-permute-start | bytes 393224 | tf_op jit(solution)/shard_map/ppermute | solution.py:520
  17.7 10.8 %copy-start.4 = (bf16[4,128,2048]{2,1,0:T(8,128)(2,1)S(1)}, bf16[4,128,2048]{2,1,0:T(8,128)(2,1)}, u32[]{:S(2)}) copy-start(bf16[4,128,2048]{2,1,0:T(8,128)(2,1)} %v_ref.10) | copy-start | bytes 6291460
  18.8 9.6 %copy-start.3 = (bf16[4,128,2048]{2,1,0:T(8,128)(2,1)S(1)}, bf16[4,128,2048]{2,1,0:T(8,128)(2,1)}, u32[]{:S(2)}) copy-start(bf16[4,128,2048]{2,1,0:T(8,128)(2,1)} %k_ref.10) | copy-start | bytes 6291460
  18.8 9.6 %copy-start.6 = (bf16[2,4,2048]{2,1,0:T(4,128)(2,1)S(1)}, bf16[2,4,2048]{2,1,0:T(4,128)(2,1)}, u32[]{:S(2)}) copy-start(bf16[2,4,2048]{2,1,0:T(4,128)(2,1)} %sk_ref.1) | copy-start | bytes 98308
  18.8 9.6 %copy-start.7 = (bf16[2,4,2048]{2,1,0:T(4,128)(2,1)S(1)}, bf16[2,4,2048]{2,1,0:T(4,128)(2,1)}, u32[]{:S(2)}) copy-start(bf16[2,4,2048]{2,1,0:T(4,128)(2,1)} %sv_ref.1) | copy-start | bytes 98308
  18.8 9.6 %copy-start.9 = (s32[4]{0:T(128)S(1)}, s32[4]{0:T(128)}, u32[]{:S(2)}) copy-start(s32[4]{0:T(128)} %lengths_ref.1) | copy-start | bytes 52
  22.2 8.6 %collective-permute-start.7 = (f32[2,128,128]{2,1,0:T(8,128)S(1)}, f32[2,128,128]{2,1,0:T(8,128)S(1)}, u32[]{:S(2)}, u32[]{:S(2)}) collective-permute-start(f32[2,128,128]{2,1,0:T(8,128)S(1)} %group_total.3.refs_0_.refs_4_), channel_id=1, source_target_pairs={{0,16},{4,20},{8,24},{12,28},{16,0},{20,4},{24,8},{28,12},{1,17},{... | collective-permute-start | bytes 393224 | tf_op jit(solution)/shard_map/ppermute | solution.py:520
  24.8 9.6 %collective-permute-start.11 = (f32[2,136,128]{2,1,0:T(8,128)S(1)}, f32[2,136,128]{2,1,0:T(8,128)S(1)}, u32[]{:S(2)}, u32[]{:S(2)}) collective-permute-start(f32[2,136,128]{2,1,0:T(8,128)S(1)} %get-tuple-element.41), channel_id=1, source_target_pairs={{0,4},{4,0},{8,12},{12,8},{16,20},{20,16},{24,28},{28,24},{1,5},{5... | collective-permute-start | bytes 417800 | tf_op jit(solution)/shard_map/ppermute | solution.py:504
  25.3 11.2 %collective-permute-start.12 = (f32[2,136,128]{2,1,0:T(8,128)S(1)}, f32[2,136,128]{2,1,0:T(8,128)S(1)}, u32[]{:S(2)}, u32[]{:S(2)}) collective-permute-start(f32[2,136,128]{2,1,0:T(8,128)S(1)} %get-tuple-element.42), channel_id=1, source_target_pairs={{0,8},{4,12},{8,0},{12,4},{16,24},{20,28},{24,16},{28,20},{1,9},{5... | collective-permute-start | bytes 417800 | tf_op jit(solution)/shard_map/ppermute | solution.py:504
  28.3 8.2 %collective-permute-start.13 = (f32[2,136,128]{2,1,0:T(8,128)S(1)}, f32[2,136,128]{2,1,0:T(8,128)S(1)}, u32[]{:S(2)}, u32[]{:S(2)}) collective-permute-start(f32[2,136,128]{2,1,0:T(8,128)S(1)} %get-tuple-element.35.refs_4_), channel_id=1, source_target_pairs={{0,12},{4,8},{8,4},{12,0},{16,28},{20,24},{24,20},{28,16},{1,13},{... | collective-permute-start | bytes 417800 | tf_op jit(solution)/shard_map/ppermute | solution.py:504
  31.0 7.1 %collective-permute-start.10 = (f32[2,136,128]{2,1,0:T(8,128)S(1)}, f32[2,136,128]{2,1,0:T(8,128)S(1)}, u32[]{:S(2)}, u32[]{:S(2)}) collective-permute-start(f32[2,136,128]{2,1,0:T(8,128)S(1)} %get-tuple-element.39), channel_id=1, source_target_pairs={{0,4},{4,0},{8,12},{12,8},{16,20},{20,16},{24,28},{28,24},{1,5},{5... | collective-permute-start | bytes 417800 | tf_op jit(solution)/shard_map/ppermute | solution.py:504
  32.4 6.7 %collective-permute-start.8 = (f32[2,136,128]{2,1,0:T(8,128)S(1)}, f32[2,136,128]{2,1,0:T(8,128)S(1)}, u32[]{:S(2)}, u32[]{:S(2)}) collective-permute-start(f32[2,136,128]{2,1,0:T(8,128)S(1)} %get-tuple-element.37), channel_id=1, source_target_pairs={{0,8},{4,12},{8,0},{12,4},{16,24},{20,28},{24,16},{28,20},{1,9},{5... | collective-permute-start | bytes 417800 | tf_op jit(solution)/shard_map/ppermute | solution.py:504
  34.4 6.6 %collective-permute-start.9 = (f32[2,136,128]{2,1,0:T(8,128)S(1)}, f32[2,136,128]{2,1,0:T(8,128)S(1)}, u32[]{:S(2)}, u32[]{:S(2)}) collective-permute-start(f32[2,136,128]{2,1,0:T(8,128)S(1)} %get-tuple-element.36.refs_0_), channel_id=1, source_target_pairs={{0,12},{4,8},{8,4},{12,0},{16,28},{20,24},{24,20},{28,16},{1,13},{... | collective-permute-start | bytes 417800 | tf_op jit(solution)/shard_map/ppermute | solution.py:504
  41.0 2.3 %copy-start.8 = (f32[2048]{0:T(1024)S(1)}, f32[2048]{0:T(1024)}, u32[]{:S(2)}) copy-start(f32[2048]{0:T(1024)} %param.19) | copy-start | bytes 24580
  41.4 3.1 %collective-permute-start.16 = (f32[1,640]{1,0:T(1,128)S(1)}, f32[1,640]{1,0:T(1,128)S(1)}, u32[]{:S(2)}, u32[]{:S(2)}) collective-permute-start(f32[1,640]{1,0:T(1,128)S(1)} %get-tuple-element.47.refs_0_), channel_id=1, source_target_pairs={{0,3},{1,2},{2,1},{3,0},{4,7},{5,6},{6,5},{7,4},{8,11},{9,10},{10,... | collective-permute-start | bytes 7688 | tf_op jit(solution)/shard_map/ppermute | solution.py:609
  41.5 3.7 %collective-permute-start.15 = (f32[1,640]{1,0:T(1,128)S(1)}, f32[1,640]{1,0:T(1,128)S(1)}, u32[]{:S(2)}, u32[]{:S(2)}) collective-permute-start(f32[1,640]{1,0:T(1,128)S(1)} %get-tuple-element.47.refs_0_), channel_id=1, source_target_pairs={{0,2},{1,3},{2,0},{3,1},{4,6},{5,7},{6,4},{7,5},{8,10},{9,11},{10,... | collective-permute-start | bytes 7688 | tf_op jit(solution)/shard_map/ppermute | solution.py:609
  43.0 2.1 %collective-permute-start.14 = (f32[1,640]{1,0:T(1,128)S(1)}, f32[1,640]{1,0:T(1,128)S(1)}, u32[]{:S(2)}, u32[]{:S(2)}) collective-permute-start(f32[1,640]{1,0:T(1,128)S(1)} %get-tuple-element.47.refs_0_), channel_id=1, source_target_pairs={{0,1},{1,0},{2,3},{3,2},{4,5},{5,4},{6,7},{7,6},{8,9},{9,8},{10,11... | collective-permute-start | bytes 7688 | tf_op jit(solution)/shard_map/ppermute | solution.py:609

commit v7 on v6

--- a/solution.py
+++ b/solution.py
@@ -586,7 +586,7 @@
         elif kind == "a" and c < len(done_heads):
             last_chunk = c == len(done_heads) - 1
             begun = []
-            near = group // 2 if last_chunk else group
+            near = group - 1 if last_chunk else group
             for some in ([*range(near)], [*range(near, group)]):
                 if some:
                     *begun, total = attend(

time: 46.9 us -> 46.8 us (level)
  no operation moved by 1% of the time
where the time goes in v7:
time: 46.8 us; the launch traced here: 46.7 us
  starting transfers between devices  24.6 us (53%)
  Pallas kernels  13.2 us (28%)
  waiting for transfers between devices  7.97 us (17%)
  between operations  0.82 us (2%)
    ppermute x12, starting transfers between devices, swap(): lax.ppermute(messages[m], 'seq', [(i, i // group * group + (i % group ^ m...  17.4 us
    ppermute x2, starting transfers between devices, across(): lax.ppermute(total, 'seq', [(i, (i + k * group) % devices) for i in range...  5.27 us
    ppermute x12, waiting for transfers between devices, swap(): lax.ppermute(messages[m], 'seq', [(i, i // group * group + (i % group ^ m...  4.6 us
    pallas_call x3, Pallas kernels, intra_block(): pl.pallas_call(functools.partial(intra_kernel, tile, heads), in_specs=[VM...  4.08 us
    pallas_call x1, Pallas kernels, suffix_part(): pl.pallas_call(suffix_kernel, in_specs=[SMEM] + [VMEM] * 5 + [ANY] * len(...  2.29 us
    ppermute x2, waiting for transfers between devices, across(): lax.ppermute(total, 'seq', [(i, (i + k * group) % devices) for i in range...  2.12 us
    ppermute x3, starting transfers between devices, on_device(): lax.ppermute(sums[0], 'head', [(i, step(i, k)) for i in range(row)])  1.92 us
    pallas_call x1, Pallas kernels, normalize(): pl.pallas_call(functools.partial(norm_kernel, heads, len(sums), width_all...  1.63 us
  transfers between devices with their start and end apart: 17, of which 8 were waited for; matrix products, arithmetic and copies ran while one was open for 0% of the time, Pallas kernels for 21%

profile of v7, /device:TPU:0, one launch (start us, length us, event | category | flops | bytes accessed | tf_op | source)
XLA Modules:
  0.0 46.7 jit_solution(16157391016802380036)
XLA Ops:
  0.7 1.5 %fetched_states.1.refs_0_ = f32[2,136,128]{2,1,0:T(8,128)S(1)} custom-call(bf16[2,4,2048]{2,1,0:T(4,128)(2,1)} %q_ref.13, bf16[512,2048]{1,0:T(8,128)(2,1)} %k_ref.11, bf16[512,2048]{1,0:T(8,128)(2,1)} %v_ref.11), custom_call_target="tpu_custom_call" | custom-call | flops 33554432 | bytes 524288 | tf_op jit(solution)/shard_map/fetched_states/pallas_call | solution.py:87
  2.2 4.0 %collective-permute-start.5 = (f32[2,136,128]{2,1,0:T(8,128)S(1)}, f32[2,136,128]{2,1,0:T(8,128)S(1)}, u32[]{:S(2)}, u32[]{:S(2)}) collective-permute-start(f32[2,136,128]{2,1,0:T(8,128)S(1)} %fetched_states.1.refs_0_), channel_id=1, source_target_pairs={{0,12},{4,8},{8,4},{12,0},{16,28},{20,24},{24,20},{28,16},{1,13},{... | collective-permute-start | bytes 417800 | tf_op jit(solution)/shard_map/ppermute | solution.py:504
  6.2 0.5 %block_states.2 = (f32[2,136,128]{2,1,0:T(8,128)S(1)}, f32[2,136,128]{2,1,0:T(8,128)S(1)}, f32[2,136,128]{2,1,0:T(8,128)S(1)}) custom-call(bf16[2,4,2048]{2,1,0:T(4,128)(2,1)S(1)} %copy-done.5, bf16[512,2048]{1,0:T(8,128)(2,1)S(1)} %copy-done, bf16[512,2048]{1,0:T(8,128)(2,1)S(1)} %copy-done.1, f32[2,136,128]{2,1,0:T(8,128)S(1)} %fetched_states.1.refs_0_), custom_call_target="tpu_custom_call" | custom-call | flops 100663296 | bytes 1572864 | tf_op jit(solution)/shard_map/block_states/pallas_call | solution.py:121
  6.8 0.6 %collective-permute-start.3 = (f32[2,136,128]{2,1,0:T(8,128)S(1)}, f32[2,136,128]{2,1,0:T(8,128)S(1)}, u32[]{:S(2)}, u32[]{:S(2)}) collective-permute-start(f32[2,136,128]{2,1,0:T(8,128)S(1)} %get-tuple-element.34), channel_id=1, source_target_pairs={{0,4},{4,0},{8,12},{12,8},{16,20},{20,16},{24,28},{28,24},{1,5},{5... | collective-permute-start | bytes 417800 | tf_op jit(solution)/shard_map/ppermute | solution.py:504
  7.3 0.8 %collective-permute-start.4 = (f32[2,136,128]{2,1,0:T(8,128)S(1)}, f32[2,136,128]{2,1,0:T(8,128)S(1)}, u32[]{:S(2)}, u32[]{:S(2)}) collective-permute-start(f32[2,136,128]{2,1,0:T(8,128)S(1)} %get-tuple-element.28.refs_0_), channel_id=1, source_target_pairs={{0,8},{4,12},{8,0},{12,4},{16,24},{20,28},{24,16},{28,20},{1,9},{5... | collective-permute-start | bytes 417800 | tf_op jit(solution)/shard_map/ppermute | solution.py:504
  8.2 0.6 %block_states.3 = (f32[2,136,128]{2,1,0:T(8,128)S(1)}, f32[2,136,128]{2,1,0:T(8,128)S(1)}, f32[2,136,128]{2,1,0:T(8,128)S(1)}, f32[2,136,128]{2,1,0:T(8,128)S(1)}) custom-call(bf16[2,4,2048]{2,1,0:T(4,128)(2,1)S(1)} %copy-done.5, bf16[512,2048]{1,0:T(8,128)(2,1)S(1)} %copy-done, bf16[512,2048]{1,0:T(8,128)(2,1)S(1)} %copy-done.1, ...), custom_call_target="tpu_custom_call" | custom-call | flops 134217728 | bytes 2097152 | tf_op jit(solution)/shard_map/block_states/pallas_call | solution.py:121
  8.8 1.2 %collective-permute-start = (f32[2,136,128]{2,1,0:T(8,128)S(1)}, f32[2,136,128]{2,1,0:T(8,128)S(1)}, u32[]{:S(2)}, u32[]{:S(2)}) collective-permute-start(f32[2,136,128]{2,1,0:T(8,128)S(1)} %get-tuple-element.30), channel_id=1, source_target_pairs={{0,4},{4,0},{8,12},{12,8},{16,20},{20,16},{24,28},{28,24},{1,5},{5... | collective-permute-start | bytes 417800 | tf_op jit(solution)/shard_map/ppermute | solution.py:504
  10.0 1.6 %collective-permute-start.1 = (f32[2,136,128]{2,1,0:T(8,128)S(1)}, f32[2,136,128]{2,1,0:T(8,128)S(1)}, u32[]{:S(2)}, u32[]{:S(2)}) collective-permute-start(f32[2,136,128]{2,1,0:T(8,128)S(1)} %get-tuple-element.31), channel_id=1, source_target_pairs={{0,8},{4,12},{8,0},{12,4},{16,24},{20,28},{24,16},{28,20},{1,9},{5... | collective-permute-start | bytes 417800 | tf_op jit(solution)/shard_map/ppermute | solution.py:504
  11.6 2.1 %collective-permute-start.2 = (f32[2,136,128]{2,1,0:T(8,128)S(1)}, f32[2,136,128]{2,1,0:T(8,128)S(1)}, u32[]{:S(2)}, u32[]{:S(2)}) collective-permute-start(f32[2,136,128]{2,1,0:T(8,128)S(1)} %get-tuple-element.32.refs_4_), channel_id=1, source_target_pairs={{0,12},{4,8},{8,4},{12,0},{16,28},{20,24},{24,20},{28,16},{1,13},{... | collective-permute-start | bytes 417800 | tf_op jit(solution)/shard_map/ppermute | solution.py:504
  13.9 2.6 %collective-permute-start.6 = (f32[2,128,128]{2,1,0:T(8,128)S(1)}, f32[2,128,128]{2,1,0:T(8,128)S(1)}, u32[]{:S(2)}, u32[]{:S(2)}) collective-permute-start(f32[2,128,128]{2,1,0:T(8,128)S(1)} %group_total.2.refs_0_.refs_4_), channel_id=1, source_target_pairs={{0,16},{4,20},{8,24},{12,28},{16,0},{20,4},{24,8},{28,12},{1,17},{... | collective-permute-start | bytes 393224 | tf_op jit(solution)/shard_map/ppermute | solution.py:520
  16.6 1.1 %intra_block.3.refs_0_ = f32[512,512]{1,0:T(8,128)S(1)} custom-call(bf16[512,2048]{1,0:T(8,128)(2,1)S(1)} %copy-done.2, bf16[512,2048]{1,0:T(8,128)(2,1)S(1)} %copy-done, bf16[512,2048]{1,0:T(8,128)(2,1)S(1)} %copy-done.1, f32[2,128,128]{2,1,0:T(8,128)S(1)} %group_total.2.refs_0_.refs_4_), custom_call_target="tpu_custom_call" | custom-call | flops 536870912 | bytes 2621440 | tf_op jit(solution)/shard_map/intra_block/pallas_call | solution.py:219
  17.7 1.1 %intra_block.4.refs_6_.refs_1_ = f32[512,512]{1,0:T(8,128)S(1)} custom-call(bf16[512,2048]{1,0:T(8,128)(2,1)S(1)} %copy-done.2, bf16[512,2048]{1,0:T(8,128)(2,1)S(1)} %copy-done, bf16[512,2048]{1,0:T(8,128)(2,1)S(1)} %copy-done.1, f32[512,512]{1,0:T(8,128)S(1)} %intra_block.3.refs_0_), custom_call_target="tpu_custom_call" | custom-call | flops 536870912 | bytes 2621440 | tf_op jit(solution)/shard_map/intra_block/pallas_call | solution.py:219
  18.8 2.1 %collective-permute-done.6.refs_5_ = f32[2,128,128]{2,1,0:T(8,128)S(1)} collective-permute-done((f32[2,128,128]{2,1,0:T(8,128)S(1)}, f32[2,128,128]{2,1,0:T(8,128)S(1)}, u32[]{:S(2)}, u32[]{:S(2)}) %collective-permute-start.6) | collective-permute-done | bytes 131104 | tf_op jit(solution)/shard_map/ppermute | solution.py:520
  21.2 0.9 %collective-permute-done.2.refs_3_ = f32[2,136,128]{2,1,0:T(8,128)S(1)} collective-permute-done((f32[2,136,128]{2,1,0:T(8,128)S(1)}, f32[2,136,128]{2,1,0:T(8,128)S(1)}, u32[]{:S(2)}, u32[]{:S(2)}) %collective-permute-start.2) | collective-permute-done | bytes 139296 | tf_op jit(solution)/shard_map/ppermute | solution.py:504
  22.2 2.6 %collective-permute-start.7 = (f32[2,128,128]{2,1,0:T(8,128)S(1)}, f32[2,128,128]{2,1,0:T(8,128)S(1)}, u32[]{:S(2)}, u32[]{:S(2)}) collective-permute-start(f32[2,128,128]{2,1,0:T(8,128)S(1)} %group_total.3.refs_0_.refs_4_), channel_id=1, source_target_pairs={{0,16},{4,20},{8,24},{12,28},{16,0},{20,4},{24,8},{28,12},{1,17},{... | collective-permute-start | bytes 393224 | tf_op jit(solution)/shard_map/ppermute | solution.py:520
  24.8 0.5 %collective-permute-start.11 = (f32[2,136,128]{2,1,0:T(8,128)S(1)}, f32[2,136,128]{2,1,0:T(8,128)S(1)}, u32[]{:S(2)}, u32[]{:S(2)}) collective-permute-start(f32[2,136,128]{2,1,0:T(8,128)S(1)} %get-tuple-element.41), channel_id=1, source_target_pairs={{0,4},{4,0},{8,12},{12,8},{16,20},{20,16},{24,28},{28,24},{1,5},{5... | collective-permute-start | bytes 417800 | tf_op jit(solution)/shard_map/ppermute | solution.py:504
  25.3 3.0 %collective-permute-start.12 = (f32[2,136,128]{2,1,0:T(8,128)S(1)}, f32[2,136,128]{2,1,0:T(8,128)S(1)}, u32[]{:S(2)}, u32[]{:S(2)}) collective-permute-start(f32[2,136,128]{2,1,0:T(8,128)S(1)} %get-tuple-element.42), channel_id=1, source_target_pairs={{0,8},{4,12},{8,0},{12,4},{16,24},{20,28},{24,16},{28,20},{1,9},{5... | collective-permute-start | bytes 417800 | tf_op jit(solution)/shard_map/ppermute | solution.py:504
  28.4 2.3 %suffix_part.1.refs_6_.extra_ref = f32[8,2048]{1,0:T(8,128)S(1)} custom-call(s32[4]{0:T(128)S(1)} %copy-done.9, bf16[2,4,2048]{2,1,0:T(4,128)(2,1)S(1)} %copy-done.5, bf16[4,128,2048]{2,1,0:T(8,128)(2,1)S(1)} %copy-done.3, bf16[4,128,2048]{2,1,0:T(8,128)(2,1)S(1)} %copy-done.4, bf16[2,4,2048]{2,1,0:T(4,128)(2,1)S(1)} %copy-done.6, ...), custom_call_target="tpu_custom_call" | custom-call | flops 67108864 | bytes 4194304 | tf_op jit(solution)/shard_map/suffix_part/pallas_call | solution.py:289
  31.0 1.3 %collective-permute-start.9 = (f32[2,136,128]{2,1,0:T(8,128)S(1)}, f32[2,136,128]{2,1,0:T(8,128)S(1)}, u32[]{:S(2)}, u32[]{:S(2)}) collective-permute-start(f32[2,136,128]{2,1,0:T(8,128)S(1)} %get-tuple-element.38), channel_id=1, source_target_pairs={{0,4},{4,0},{8,12},{12,8},{16,20},{20,16},{24,28},{28,24},{1,5},{5... | collective-permute-start | bytes 417800 | tf_op jit(solution)/shard_map/ppermute | solution.py:504
  32.4 2.0 %collective-permute-start.10 = (f32[2,136,128]{2,1,0:T(8,128)S(1)}, f32[2,136,128]{2,1,0:T(8,128)S(1)}, u32[]{:S(2)}, u32[]{:S(2)}) collective-permute-start(f32[2,136,128]{2,1,0:T(8,128)S(1)} %get-tuple-element.39), channel_id=1, source_target_pairs={{0,8},{4,12},{8,0},{12,4},{16,24},{20,28},{24,16},{28,20},{1,9},{5... | collective-permute-start | bytes 417800 | tf_op jit(solution)/shard_map/ppermute | solution.py:504
  34.5 1.9 %intra_block.5.refs_0_ = f32[512,1024]{1,0:T(8,128)S(1)} custom-call(bf16[512,2048]{1,0:T(8,128)(2,1)S(1)} %copy-done.2, bf16[512,2048]{1,0:T(8,128)(2,1)S(1)} %copy-done, bf16[512,2048]{1,0:T(8,128)(2,1)S(1)} %copy-done.1, f32[2,136,128]{2,1,0:T(8,128)S(1)} %get-tuple-element.36.refs_0_), custom_call_target="tpu_custom_call" | custom-call | flops 1073741824 | bytes 5242880 | tf_op jit(solution)/shard_map/intra_block/pallas_call | solution.py:219
  36.5 0.6 %attend.3 = (f32[512,1024]{1,0:T(8,128)S(1)}, f32[8,1024]{1,0:T(8,128)S(1)}, f32[640,128]{1,0:T(8,128)S(1)}) custom-call(bf16[512,2048]{1,0:T(8,128)(2,1)S(1)} %copy-done.2, f32[8,2048]{1,0:T(8,128)S(1)} %suffix_part.1.refs_6_.extra_ref, f32[512,512]{1,0:T(8,128)S(1)} %intra_block.3.refs_0_, f32[512,512]{1,0:T(8,128)S(1)} %intra_block.4.refs_6_.refs_1_, ...), custom_call_target="tpu_custom_call" | custom-call | flops 134217728 | bytes 5242880 | tf_op jit(solution)/shard_map/attend/pallas_call | solution.py:356
  37.1 1.0 %collective-permute-done.9.refs_2_ = f32[2,136,128]{2,1,0:T(8,128)S(1)} collective-permute-done((f32[2,136,128]{2,1,0:T(8,128)S(1)}, f32[2,136,128]{2,1,0:T(8,128)S(1)}, u32[]{:S(2)}, u32[]{:S(2)}) %collective-permute-start.9) | collective-permute-done | bytes 139296 | tf_op jit(solution)/shard_map/ppermute | solution.py:504
  38.1 0.9 %collective-permute-done.10.refs_3_ = f32[2,136,128]{2,1,0:T(8,128)S(1)} collective-permute-done((f32[2,136,128]{2,1,0:T(8,128)S(1)}, f32[2,136,128]{2,1,0:T(8,128)S(1)}, u32[]{:S(2)}, u32[]{:S(2)}) %collective-permute-start.10) | collective-permute-done | bytes 139296 | tf_op jit(solution)/shard_map/ppermute | solution.py:504
  39.1 0.4 attend.4
  39.4 1.5 %collective-permute-done.8.refs_1_ = f32[2,136,128]{2,1,0:T(8,128)S(1)} collective-permute-done((f32[2,136,128]{2,1,0:T(8,128)S(1)}, f32[2,136,128]{2,1,0:T(8,128)S(1)}, u32[]{:S(2)}, u32[]{:S(2)}) %collective-permute-start.8) | collective-permute-done | bytes 139296 | tf_op jit(solution)/shard_map/ppermute | solution.py:504
  41.0 0.3 attend.5
  41.4 1.6 %collective-permute-start.15 = (f32[1,640]{1,0:T(1,128)S(1)}, f32[1,640]{1,0:T(1,128)S(1)}, u32[]{:S(2)}, u32[]{:S(2)}) collective-permute-start(f32[1,640]{1,0:T(1,128)S(1)} %get-tuple-element.47.refs_0_), channel_id=1, source_target_pairs={{0,2},{1,3},{2,0},{3,1},{4,6},{5,7},{6,4},{7,5},{8,10},{9,11},{10,... | collective-permute-start | bytes 7688 | tf_op jit(solution)/shard_map/ppermute | solution.py:609
  43.2 0.6 %gained.1 = (f32[512,1024]{1,0:T(8,128)S(1)}, f32[512,1024]{1,0:T(8,128)S(1)}) custom-call(f32[1,2048]{1,0:T(1,128)S(1)} %bitcast.1, f32[512,1024]{1,0:T(8,128)S(1)} %get-tuple-element.48.refs_0_, f32[512,1024]{1,0:T(8,128)S(1)} %get-tuple-element.49.refs_1_), custom_call_target="tpu_custom_call" | custom-call | bytes 8388608 | tf_op jit(solution)/shard_map/gained/pallas_call | solution.py:382
  43.8 0.6 %collective-permute-done.16.refs_3_ = f32[1,640]{1,0:T(1,128)S(1)} collective-permute-done((f32[1,640]{1,0:T(1,128)S(1)}, f32[1,640]{1,0:T(1,128)S(1)}, u32[]{:S(2)}, u32[]{:S(2)}) %collective-permute-start.16) | collective-permute-done | bytes 2592 | tf_op jit(solution)/shard_map/ppermute | solution.py:609
  44.4 0.7 %collective-permute-done.15.refs_2_ = f32[1,640]{1,0:T(1,128)S(1)} collective-permute-done((f32[1,640]{1,0:T(1,128)S(1)}, f32[1,640]{1,0:T(1,128)S(1)}, u32[]{:S(2)}, u32[]{:S(2)}) %collective-permute-start.15) | collective-permute-done | bytes 2592 | tf_op jit(solution)/shard_map/ppermute | solution.py:609
  45.1 1.6 %normalize.1 = (bf16[512,2048]{1,0:T(8,128)(2,1)}, bf16[2,4,2048]{2,1,0:T(4,128)(2,1)}) custom-call(f32[1,2048]{1,0:T(1,128)S(1)} %bitcast.2, f32[1,640]{1,0:T(1,128)S(1)} %get-tuple-element.47.refs_0_, f32[1,640]{1,0:T(1,128)S(1)} %collective-permute-done.14.refs_1_, f32[1,640]{1,0:T(1,128)S(1)} %collective-permute-done.15.refs_2_, ...), custom_call_target="tpu_custom_call" | custom-call | bytes 6291456 | tf_op jit(solution)/shard_map/normalize/pallas_call | solution.py:435
  (38 shorter events, 1.5 us)
Async XLA Ops:
  0.6 5.6 %copy-start.1 = (bf16[512,2048]{1,0:T(8,128)(2,1)S(1)}, bf16[512,2048]{1,0:T(8,128)(2,1)}, u32[]{:S(2)}) copy-start(bf16[512,2048]{1,0:T(8,128)(2,1)} %v_ref.11) | copy-start | bytes 6291460
  0.6 5.6 %copy-start = (bf16[512,2048]{1,0:T(8,128)(2,1)S(1)}, bf16[512,2048]{1,0:T(8,128)(2,1)}, u32[]{:S(2)}) copy-start(bf16[512,2048]{1,0:T(8,128)(2,1)} %k_ref.11) | copy-start | bytes 6291460
  0.7 5.6 %copy-start.5 = (bf16[2,4,2048]{2,1,0:T(4,128)(2,1)S(1)}, bf16[2,4,2048]{2,1,0:T(4,128)(2,1)}, u32[]{:S(2)}) copy-start(bf16[2,4,2048]{2,1,0:T(4,128)(2,1)} %q_ref.13) | copy-start | bytes 98308
  2.2 9.4 %collective-permute-start.5 = (f32[2,136,128]{2,1,0:T(8,128)S(1)}, f32[2,136,128]{2,1,0:T(8,128)S(1)}, u32[]{:S(2)}, u32[]{:S(2)}) collective-permute-start(f32[2,136,128]{2,1,0:T(8,128)S(1)} %fetched_states.1.refs_0_), channel_id=1, source_target_pairs={{0,12},{4,8},{8,4},{12,0},{16,28},{20,24},{24,20},{28,16},{1,13},{... | collective-permute-start | bytes 417800 | tf_op jit(solution)/shard_map/ppermute | solution.py:504
  6.8 6.9 %collective-permute-start.3 = (f32[2,136,128]{2,1,0:T(8,128)S(1)}, f32[2,136,128]{2,1,0:T(8,128)S(1)}, u32[]{:S(2)}, u32[]{:S(2)}) collective-permute-start(f32[2,136,128]{2,1,0:T(8,128)S(1)} %get-tuple-element.34), channel_id=1, source_target_pairs={{0,4},{4,0},{8,12},{12,8},{16,20},{20,16},{24,28},{28,24},{1,5},{5... | collective-permute-start | bytes 417800 | tf_op jit(solution)/shard_map/ppermute | solution.py:504
  7.3 9.3 %copy-start.2 = (bf16[512,2048]{1,0:T(8,128)(2,1)S(1)}, bf16[512,2048]{1,0:T(8,128)(2,1)}, u32[]{:S(2)}) copy-start(bf16[512,2048]{1,0:T(8,128)(2,1)} %q_ref.17) | copy-start | bytes 6291460
  7.3 6.6 %collective-permute-start.4 = (f32[2,136,128]{2,1,0:T(8,128)S(1)}, f32[2,136,128]{2,1,0:T(8,128)S(1)}, u32[]{:S(2)}, u32[]{:S(2)}) collective-permute-start(f32[2,136,128]{2,1,0:T(8,128)S(1)} %get-tuple-element.28.refs_0_), channel_id=1, source_target_pairs={{0,8},{4,12},{8,0},{12,4},{16,24},{20,28},{24,16},{28,20},{1,9},{5... | collective-permute-start | bytes 417800 | tf_op jit(solution)/shard_map/ppermute | solution.py:504
  8.8 12.4 %collective-permute-start = (f32[2,136,128]{2,1,0:T(8,128)S(1)}, f32[2,136,128]{2,1,0:T(8,128)S(1)}, u32[]{:S(2)}, u32[]{:S(2)}) collective-permute-start(f32[2,136,128]{2,1,0:T(8,128)S(1)} %get-tuple-element.30), channel_id=1, source_target_pairs={{0,4},{4,0},{8,12},{12,8},{16,20},{20,16},{24,28},{28,24},{1,5},{5... | collective-permute-start | bytes 417800 | tf_op jit(solution)/shard_map/ppermute | solution.py:504
  10.0 11.2 %collective-permute-start.1 = (f32[2,136,128]{2,1,0:T(8,128)S(1)}, f32[2,136,128]{2,1,0:T(8,128)S(1)}, u32[]{:S(2)}, u32[]{:S(2)}) collective-permute-start(f32[2,136,128]{2,1,0:T(8,128)S(1)} %get-tuple-element.31), channel_id=1, source_target_pairs={{0,8},{4,12},{8,0},{12,4},{16,24},{20,28},{24,16},{28,20},{1,9},{5... | collective-permute-start | bytes 417800 | tf_op jit(solution)/shard_map/ppermute | solution.py:504
  11.6 10.5 %collective-permute-start.2 = (f32[2,136,128]{2,1,0:T(8,128)S(1)}, f32[2,136,128]{2,1,0:T(8,128)S(1)}, u32[]{:S(2)}, u32[]{:S(2)}) collective-permute-start(f32[2,136,128]{2,1,0:T(8,128)S(1)} %get-tuple-element.32.refs_4_), channel_id=1, source_target_pairs={{0,12},{4,8},{8,4},{12,0},{16,28},{20,24},{24,20},{28,16},{1,13},{... | collective-permute-start | bytes 417800 | tf_op jit(solution)/shard_map/ppermute | solution.py:504
  13.9 7.0 %collective-permute-start.6 = (f32[2,128,128]{2,1,0:T(8,128)S(1)}, f32[2,128,128]{2,1,0:T(8,128)S(1)}, u32[]{:S(2)}, u32[]{:S(2)}) collective-permute-start(f32[2,128,128]{2,1,0:T(8,128)S(1)} %group_total.2.refs_0_.refs_4_), channel_id=1, source_target_pairs={{0,16},{4,20},{8,24},{12,28},{16,0},{20,4},{24,8},{28,12},{1,17},{... | collective-permute-start | bytes 393224 | tf_op jit(solution)/shard_map/ppermute | solution.py:520
  17.7 10.8 %copy-start.4 = (bf16[4,128,2048]{2,1,0:T(8,128)(2,1)S(1)}, bf16[4,128,2048]{2,1,0:T(8,128)(2,1)}, u32[]{:S(2)}) copy-start(bf16[4,128,2048]{2,1,0:T(8,128)(2,1)} %v_ref.10) | copy-start | bytes 6291460
  18.8 9.6 %copy-start.3 = (bf16[4,128,2048]{2,1,0:T(8,128)(2,1)S(1)}, bf16[4,128,2048]{2,1,0:T(8,128)(2,1)}, u32[]{:S(2)}) copy-start(bf16[4,128,2048]{2,1,0:T(8,128)(2,1)} %k_ref.10) | copy-start | bytes 6291460
  18.8 9.6 %copy-start.6 = (bf16[2,4,2048]{2,1,0:T(4,128)(2,1)S(1)}, bf16[2,4,2048]{2,1,0:T(4,128)(2,1)}, u32[]{:S(2)}) copy-start(bf16[2,4,2048]{2,1,0:T(4,128)(2,1)} %sk_ref.1) | copy-start | bytes 98308
  18.8 9.6 %copy-start.7 = (bf16[2,4,2048]{2,1,0:T(4,128)(2,1)S(1)}, bf16[2,4,2048]{2,1,0:T(4,128)(2,1)}, u32[]{:S(2)}) copy-start(bf16[2,4,2048]{2,1,0:T(4,128)(2,1)} %sv_ref.1) | copy-start | bytes 98308
  18.8 9.6 %copy-start.9 = (s32[4]{0:T(128)S(1)}, s32[4]{0:T(128)}, u32[]{:S(2)}) copy-start(s32[4]{0:T(128)} %lengths_ref.1) | copy-start | bytes 52
  22.2 8.6 %collective-permute-start.7 = (f32[2,128,128]{2,1,0:T(8,128)S(1)}, f32[2,128,128]{2,1,0:T(8,128)S(1)}, u32[]{:S(2)}, u32[]{:S(2)}) collective-permute-start(f32[2,128,128]{2,1,0:T(8,128)S(1)} %group_total.3.refs_0_.refs_4_), channel_id=1, source_target_pairs={{0,16},{4,20},{8,24},{12,28},{16,0},{20,4},{24,8},{28,12},{1,17},{... | collective-permute-start | bytes 393224 | tf_op jit(solution)/shard_map/ppermute | solution.py:520
  24.8 9.6 %collective-permute-start.11 = (f32[2,136,128]{2,1,0:T(8,128)S(1)}, f32[2,136,128]{2,1,0:T(8,128)S(1)}, u32[]{:S(2)}, u32[]{:S(2)}) collective-permute-start(f32[2,136,128]{2,1,0:T(8,128)S(1)} %get-tuple-element.41), channel_id=1, source_target_pairs={{0,4},{4,0},{8,12},{12,8},{16,20},{20,16},{24,28},{28,24},{1,5},{5... | collective-permute-start | bytes 417800 | tf_op jit(solution)/shard_map/ppermute | solution.py:504
  25.3 11.2 %collective-permute-start.12 = (f32[2,136,128]{2,1,0:T(8,128)S(1)}, f32[2,136,128]{2,1,0:T(8,128)S(1)}, u32[]{:S(2)}, u32[]{:S(2)}) collective-permute-start(f32[2,136,128]{2,1,0:T(8,128)S(1)} %get-tuple-element.42), channel_id=1, source_target_pairs={{0,8},{4,12},{8,0},{12,4},{16,24},{20,28},{24,16},{28,20},{1,9},{5... | collective-permute-start | bytes 417800 | tf_op jit(solution)/shard_map/ppermute | solution.py:504
  28.3 8.2 %collective-permute-start.13 = (f32[2,136,128]{2,1,0:T(8,128)S(1)}, f32[2,136,128]{2,1,0:T(8,128)S(1)}, u32[]{:S(2)}, u32[]{:S(2)}) collective-permute-start(f32[2,136,128]{2,1,0:T(8,128)S(1)} %get-tuple-element.35.refs_4_), channel_id=1, source_target_pairs={{0,12},{4,8},{8,4},{12,0},{16,28},{20,24},{24,20},{28,16},{1,13},{... | collective-permute-start | bytes 417800 | tf_op jit(solution)/shard_map/ppermute | solution.py:504
  31.0 7.1 %collective-permute-start.9 = (f32[2,136,128]{2,1,0:T(8,128)S(1)}, f32[2,136,128]{2,1,0:T(8,128)S(1)}, u32[]{:S(2)}, u32[]{:S(2)}) collective-permute-start(f32[2,136,128]{2,1,0:T(8,128)S(1)} %get-tuple-element.38), channel_id=1, source_target_pairs={{0,4},{4,0},{8,12},{12,8},{16,20},{20,16},{24,28},{28,24},{1,5},{5... | collective-permute-start | bytes 417800 | tf_op jit(solution)/shard_map/ppermute | solution.py:504
  32.4 6.7 %collective-permute-start.10 = (f32[2,136,128]{2,1,0:T(8,128)S(1)}, f32[2,136,128]{2,1,0:T(8,128)S(1)}, u32[]{:S(2)}, u32[]{:S(2)}) collective-permute-start(f32[2,136,128]{2,1,0:T(8,128)S(1)} %get-tuple-element.39), channel_id=1, source_target_pairs={{0,8},{4,12},{8,0},{12,4},{16,24},{20,28},{24,16},{28,20},{1,9},{5... | collective-permute-start | bytes 417800 | tf_op jit(solution)/shard_map/ppermute | solution.py:504
  34.4 6.6 %collective-permute-start.8 = (f32[2,136,128]{2,1,0:T(8,128)S(1)}, f32[2,136,128]{2,1,0:T(8,128)S(1)}, u32[]{:S(2)}, u32[]{:S(2)}) collective-permute-start(f32[2,136,128]{2,1,0:T(8,128)S(1)} %get-tuple-element.36.refs_0_), channel_id=1, source_target_pairs={{0,12},{4,8},{8,4},{12,0},{16,28},{20,24},{24,20},{28,16},{1,13},{... | collective-permute-start | bytes 417800 | tf_op jit(solution)/shard_map/ppermute | solution.py:504
  41.0 2.3 %copy-start.8 = (f32[2048]{0:T(1024)S(1)}, f32[2048]{0:T(1024)}, u32[]{:S(2)}) copy-start(f32[2048]{0:T(1024)} %param.19) | copy-start | bytes 24580
  41.3 3.1 %collective-permute-start.16 = (f32[1,640]{1,0:T(1,128)S(1)}, f32[1,640]{1,0:T(1,128)S(1)}, u32[]{:S(2)}, u32[]{:S(2)}) collective-permute-start(f32[1,640]{1,0:T(1,128)S(1)} %get-tuple-element.47.refs_0_), channel_id=1, source_target_pairs={{0,3},{1,2},{2,1},{3,0},{4,7},{5,6},{6,5},{7,4},{8,11},{9,10},{10,... | collective-permute-start | bytes 7688 | tf_op jit(solution)/shard_map/ppermute | solution.py:609
  41.4 3.7 %collective-permute-start.15 = (f32[1,640]{1,0:T(1,128)S(1)}, f32[1,640]{1,0:T(1,128)S(1)}, u32[]{:S(2)}, u32[]{:S(2)}) collective-permute-start(f32[1,640]{1,0:T(1,128)S(1)} %get-tuple-element.47.refs_0_), channel_id=1, source_target_pairs={{0,2},{1,3},{2,0},{3,1},{4,6},{5,7},{6,4},{7,5},{8,10},{9,11},{10,... | collective-permute-start | bytes 7688 | tf_op jit(solution)/shard_map/ppermute | solution.py:609
  43.0 2.1 %collective-permute-start.14 = (f32[1,640]{1,0:T(1,128)S(1)}, f32[1,640]{1,0:T(1,128)S(1)}, u32[]{:S(2)}, u32[]{:S(2)}) collective-permute-start(f32[1,640]{1,0:T(1,128)S(1)} %get-tuple-element.47.refs_0_), channel_id=1, source_target_pairs={{0,1},{1,0},{2,3},{3,2},{4,5},{5,4},{6,7},{7,6},{8,9},{9,8},{10,11... | collective-permute-start | bytes 7688 | tf_op jit(solution)/shard_map/ppermute | solution.py:609
